TPU v7x, 32 devices: a whole 2x2x4 slice. The times are simulated.
32 devices in a mesh: dp: 2 (over y), row: 4 (over x, core), col: 4 (over z).
Axes of the slice: x: 2, y: 2, z: 4, core: 2. Of those that a mesh axis runs over, the one named last changes fastest.
Arguments:
- tokens_in: bfloat16 [16384, 768], P(('dp', 'row', 'col')), may hold values from -6 to 6
- segment_ids: int32 [32, 512], P('dp'), may hold values from 0 to 3, never falling along the last dimension, each value on 1 to 256 neighbouring positions
- attn_gain: float32 [768], replicated, may hold values from 0.5 to 1.5
- attn_shift: float32 [768], replicated, may hold values from -1.25 to 1.25
- mlp_gain: float32 [768], replicated, may hold values from 0.5 to 1.5
- mlp_shift: float32 [768], replicated, may hold values from -1.25 to 1.25
- qkv_weight: bfloat16 [768, 2304], P('row', 'col'), may hold values from -0.21875 to 0.21875
- qkv_bias: float32 [2304], replicated, may hold values from -1.75 to 1.75
- out_weight: bfloat16 [768, 768], P('col', 'row'), may hold values from -0.875 to 0.875
- out_bias: float32 [768], replicated, may hold values from -1.75 to 1.75
- up_weight: bfloat16 [768, 3072], P('row', 'col'), may hold values from -0.21875 to 0.21875
- up_bias: float32 [3072], replicated, may hold values from -1.75 to 1.75
- down_weight: bfloat16 [3072, 768], P('col', 'row'), may hold values from -0.109375 to 0.109375
- down_bias: float32 [768], replicated, may hold values from -1.75 to 1.75
- out_cotangent: bfloat16 [16384, 768], P(('dp', 'row', 'col')), may hold values from -6 to 6
Outputs:
- block_out: bfloat16 [16384, 768], P(('dp', 'row', 'col'))
- in_grad: bfloat16 [16384, 768], P(('dp', 'row', 'col'))
- grad_attn_gain: float32 [768], replicated
- grad_attn_shift: float32 [768], replicated
- grad_mlp_gain: float32 [768], replicated
- grad_mlp_shift: float32 [768], replicated
- grad_qkv_weight: float32 [768, 2304], P('row', 'col')
- grad_qkv_bias: float32 [2304], replicated
- grad_out_weight: float32 [768, 768], P('col', 'row')
- grad_out_bias: float32 [768], replicated
- grad_up_weight: float32 [768, 3072], P('row', 'col')
- grad_up_bias: float32 [3072], replicated
- grad_down_weight: float32 [3072, 768], P('col', 'row')
- grad_down_bias: float32 [768], replicated
Inputs may be any that keep to these rules, and one draw needn't show every extreme that they name: `segment_ids`: along each sequence the numbers never fall; each document has 1 to 256 tokens, and some document of each sequence has exactly 256.
All inputs are finite; a program needn't handle non-finite values.
Results may differ from a plain program's by a relative error of at most 0.011.
Values may be sent and summed in bfloat16 or wider, within the bound.
No kernel may reach another device: no remote copies, remote signals or barrier semaphores. Data moves between devices by JAX's collectives and lax.ppermute only.
A program may use at most 384 MiB of HBM per device.

v0:
```python
import math

import jax
import jax.numpy as jnp
from jax import lax
from jax.sharding import PartitionSpec as P

HD = 64
ROT = 16


EPSILON = 1e-05
ROPE_BASE = 10000.0
CONTRACT_LAST = (((1,), (1,)), ((), ()))
CONTRACT_FIRST = (((0,), (0,)), ((), ()))


def as_sent(value):

    def short(part):
        return part.astype(jnp.bfloat16) if part.dtype == jnp.float32 else part

    return jax.tree.map(short, value)


def rotary_tables(seg_rows, rot_dims):
    column_ids = lax.broadcasted_iota(jnp.int32, seg_rows.shape, 1)
    previous = jnp.concatenate([seg_rows[:, :1] - 1, seg_rows[:, :-1]], axis=1)
    starts = lax.cummax(jnp.where(seg_rows != previous, column_ids, 0), axis=1)
    places = (column_ids - starts).astype(jnp.float32)
    halves = rot_dims // 2
    frequency = ROPE_BASE ** (-(jnp.arange(halves, dtype=jnp.float32) * (2.0 / rot_dims)))
    angles = places[:, :, None] * frequency
    return (jnp.cos(angles), jnp.sin(angles))


def apply_rotary(vectors, cosine, sine_table, rot_dims):
    halves = rot_dims // 2
    first_half = vectors[..., :halves]
    second_half = vectors[..., halves:rot_dims]
    cos_wide = cosine[:, :, None, :]
    sin_wide = sine_table[:, :, None, :]
    return jnp.concatenate(
        [
            first_half * cos_wide - second_half * sin_wide,
            second_half * cos_wide + first_half * sin_wide,
            vectors[..., rot_dims:],
        ],
        axis=-1,
    )


def rotary_back(grads, cosine, sine_table, rot_dims):
    halves = rot_dims // 2
    first_half = grads[..., :halves]
    second_half = grads[..., halves:rot_dims]
    cos_wide = cosine[:, :, None, :]
    sin_wide = sine_table[:, :, None, :]
    return jnp.concatenate(
        [
            first_half * cos_wide + second_half * sin_wide,
            second_half * cos_wide - first_half * sin_wide,
            grads[..., rot_dims:],
        ],
        axis=-1,
    )


def mask_block(seg_one, block_rows):
    query_ids = lax.broadcasted_iota(jnp.int32, (block_rows, 1), 0)
    key_ids = lax.broadcasted_iota(jnp.int32, (1, seg_one.shape[0]), 1)
    return (key_ids <= query_ids) & (seg_one[None, :] == seg_one[:, None])


def to_items(array):
    seq_count, length, head_count, width = array.shape
    return array.transpose(0, 2, 1, 3).reshape(seq_count * head_count, length, width)


def from_items(array, seq_count):
    item_count, length, width = array.shape
    return array.reshape(seq_count, item_count // seq_count, length, width).transpose(0, 2, 1, 3)


def attend_forward(qkv_proj, seg_rows):
    seq_count, length = seg_rows.shape
    head_count = qkv_proj.shape[1] // (3 * HD)
    cosine, sine_table = rotary_tables(seg_rows, ROT)
    split_heads = qkv_proj.reshape(seq_count, length, head_count, 3, HD)
    queries = apply_rotary(split_heads[:, :, :, 0], cosine, sine_table, ROT).astype(jnp.bfloat16)
    key_rows = apply_rotary(split_heads[:, :, :, 1], cosine, sine_table, ROT).astype(jnp.bfloat16)
    value_rows = split_heads[:, :, :, 2].astype(jnp.bfloat16)
    query_items = to_items(queries)
    key_items = to_items(key_rows)
    value_items = to_items(value_rows)
    seg_items = jnp.repeat(seg_rows, head_count, axis=0)
    block_rows = min(512, length)
    score_scale = 1.0 / math.sqrt(HD)

    def forward_item(packed):
        query_one, key_one, value_one, seg_one = packed
        scores = (
            jnp.einsum("qd,kd->qk", query_one, key_one, preferred_element_type=jnp.float32)
            * score_scale
        )
        scores = jnp.where(mask_block(seg_one, block_rows), scores, -jnp.inf)
        row_peak = jnp.max(scores, axis=1, keepdims=True)
        raised = jnp.exp(scores - row_peak)
        denominator = jnp.sum(raised, axis=1, keepdims=True)
        probability = (raised / denominator).astype(jnp.bfloat16)
        outputs = [
            jnp.dot(probability, value_one, preferred_element_type=jnp.float32).astype(jnp.bfloat16)
        ]
        totals = [(row_peak + jnp.log(denominator))[:, 0]]
        return (jnp.concatenate(outputs, axis=0), jnp.concatenate(totals, axis=0))

    attn_items, log_totals = lax.map(forward_item, (query_items, key_items, value_items, seg_items))
    attn_out = from_items(attn_items, seq_count).reshape(seq_count * length, head_count * HD)
    return (attn_out, (query_items, key_items, value_items, seg_items, log_totals))


def attend_backward(saved, d_attn, seg_rows):
    query_items, key_items, value_items, seg_items, log_totals = saved
    seq_count, length = seg_rows.shape
    head_count = d_attn.shape[1] // HD
    grad_items = to_items(d_attn.reshape(seq_count, length, head_count, HD))
    block_rows = min(512, length)
    score_scale = 1.0 / math.sqrt(HD)

    def backward_item(packed):
        query_one, key_one, value_one, seg_one, log_one, grad_one = packed
        key_grad = jnp.zeros((length, HD), jnp.float32)
        value_grad = jnp.zeros((length, HD), jnp.float32)
        scores = (
            jnp.einsum("qd,kd->qk", query_one, key_one, preferred_element_type=jnp.float32)
            * score_scale
        )
        scores = jnp.where(mask_block(seg_one, block_rows), scores, -jnp.inf)
        probability = jnp.exp(scores - log_one[0:block_rows, None])
        value_grad = value_grad + jnp.einsum(
            "qk,qd->kd",
            probability.astype(jnp.bfloat16),
            grad_one,
            preferred_element_type=jnp.float32,
        )
        prob_grad = jnp.einsum("qd,kd->qk", grad_one, value_one, preferred_element_type=jnp.float32)
        centre = jnp.sum(probability * prob_grad, axis=1, keepdims=True)
        score_grad = (probability * (prob_grad - centre)).astype(jnp.bfloat16)
        query_grads = [
            jnp.dot(score_grad, key_one, preferred_element_type=jnp.float32) * score_scale
        ]
        key_grad = (
            key_grad
            + jnp.einsum("qk,qd->kd", score_grad, query_one, preferred_element_type=jnp.float32)
            * score_scale
        )
        return (jnp.concatenate(query_grads, axis=0), key_grad, value_grad)

    query_grad, key_grad, value_grad = lax.map(
        backward_item, (query_items, key_items, value_items, seg_items, log_totals, grad_items)
    )
    cosine, sine_table = rotary_tables(seg_rows, ROT)
    query_back = rotary_back(from_items(query_grad, seq_count), cosine, sine_table, ROT)
    key_back = rotary_back(from_items(key_grad, seq_count), cosine, sine_table, ROT)
    stacked = jnp.stack([query_back, key_back, from_items(value_grad, seq_count)], axis=3)
    return stacked.reshape(seq_count * length, head_count * 3 * HD).astype(jnp.bfloat16)


def normalize(x_float):
    center = x_float - jnp.mean(x_float, axis=1, keepdims=True)
    inv_std = lax.rsqrt(jnp.mean(center * center, axis=1, keepdims=True) + EPSILON)
    return (center * inv_std, inv_std)


def gelu_slope(hidden):
    return 0.5 * (1.0 + lax.erf(hidden * (1.0 / math.sqrt(2.0)))) + hidden * jnp.exp(
        -0.5 * hidden * hidden
    ) * (1.0 / math.sqrt(2.0 * math.pi))


def reduce_grads(grad_qkv, grad_out, grad_up, grad_down, qkv_term, up_term, stat_terms):
    summed = lax.psum((grad_qkv, grad_out, grad_up, grad_down), "dp")
    smalls = lax.psum((qkv_term, up_term, stat_terms), ("dp", "row", "col"))
    return (summed, smalls)


def on_device(
    tokens_in,
    segment_ids,
    attn_gain,
    attn_shift,
    mlp_gain,
    mlp_shift,
    qkv_weight,
    qkv_bias,
    out_weight,
    out_bias,
    up_weight,
    up_bias,
    down_weight,
    down_bias,
    out_cotangent,
):
    row_size = lax.axis_size("row")
    col_size = lax.axis_size("col")
    per_block = segment_ids.shape[0] // (row_size * col_size)
    x_float = tokens_in.astype(jnp.float32)
    grad_float = out_cotangent.astype(jnp.float32)
    normed, inv_std = normalize(x_float)
    norm_attn = (normed * attn_gain + attn_shift).astype(jnp.bfloat16)
    norm_mlp = (normed * mlp_gain + mlp_shift).astype(jnp.bfloat16)
    col_id = lax.axis_index("col")
    qkv_cols = qkv_weight.shape[1]
    up_cols = up_weight.shape[1]
    out_cols = out_weight.shape[0]
    stacked = jnp.stack([norm_attn, norm_mlp, out_cotangent])
    grid_rows = lax.all_to_all(stacked, "row", split_axis=2, concat_axis=1, tiled=True)
    wide_rows = lax.all_gather(grid_rows, "col", axis=1, tiled=True)
    attn_wide_in = wide_rows[0]
    mlp_wide_in = wide_rows[1]
    grad_wide = wide_rows[2]
    mixed_rows = lax.psum_scatter(
        jnp.concatenate(
            [
                jnp.dot(attn_wide_in, qkv_weight, preferred_element_type=jnp.float32),
                jnp.dot(mlp_wide_in, up_weight, preferred_element_type=jnp.float32),
            ],
            axis=1,
        ),
        "row",
        scatter_dimension=0,
        tiled=True,
    )
    qkv_proj = mixed_rows[:, :qkv_cols] + lax.dynamic_slice_in_dim(
        qkv_bias, col_id * qkv_cols, qkv_cols
    )
    hidden = mixed_rows[:, qkv_cols:] + lax.dynamic_slice_in_dim(up_bias, col_id * up_cols, up_cols)
    slot_ids = lax.axis_index("row") * col_size + jnp.arange(col_size, dtype=jnp.int32)
    block_ids = slot_ids % row_size * col_size + slot_ids // row_size
    wanted = (
        block_ids[:, None] * per_block + jnp.arange(per_block, dtype=jnp.int32)[None, :]
    ).reshape(-1)
    seg_rows = jnp.take(segment_ids, wanted, axis=0)
    attn_out, saved = attend_forward(qkv_proj, seg_rows)
    active = jax.nn.gelu(hidden, approximate=False).astype(jnp.bfloat16)
    attn_wide, act_wide = (
        lax.all_gather(as_sent(attn_out), "row", axis=0, tiled=True).astype(attn_out.dtype),
        lax.all_gather(active, "row", axis=0, tiled=True),
    )
    row_count = lax.axis_size("col") * (attn_wide.shape[0] // col_size)
    attn_part = lax.slice_in_dim(attn_wide, 0, row_count, axis=0)
    act_part = lax.slice_in_dim(act_wide, 0, row_count, axis=0)
    branch_grid = lax.psum_scatter(
        jnp.dot(attn_part, out_weight, preferred_element_type=jnp.float32)
        + jnp.dot(act_part, down_weight, preferred_element_type=jnp.float32),
        "col",
        scatter_dimension=0,
        tiled=True,
    )
    back_rows = lax.psum_scatter(
        jnp.concatenate(
            [
                lax.dot_general(
                    grad_wide, out_weight, CONTRACT_LAST, preferred_element_type=jnp.float32
                ),
                lax.dot_general(
                    grad_wide, down_weight, CONTRACT_LAST, preferred_element_type=jnp.float32
                ),
            ],
            axis=1,
        ),
        "row",
        scatter_dimension=0,
        tiled=True,
    )
    d_attn = back_rows[:, :out_cols].astype(jnp.bfloat16)
    d_hidden = (back_rows[:, out_cols:] * gelu_slope(hidden)).astype(jnp.bfloat16)
    d_qkv = attend_backward(saved, d_attn, seg_rows)
    qkv_grad_wide, hidden_grad_wide = (
        lax.all_gather(d_qkv, "row", axis=0, tiled=True),
        lax.all_gather(d_hidden, "row", axis=0, tiled=True),
    )
    norm_back = lax.psum_scatter(
        jnp.concatenate(
            [
                lax.dot_general(
                    qkv_grad_wide, qkv_weight, CONTRACT_LAST, preferred_element_type=jnp.float32
                ),
                lax.dot_general(
                    hidden_grad_wide, up_weight, CONTRACT_LAST, preferred_element_type=jnp.float32
                ),
            ],
            axis=1,
        ),
        "col",
        scatter_dimension=0,
        tiled=True,
    )
    feature_cols = norm_back.shape[1] // 2
    back_stack = jnp.stack([branch_grid, norm_back[:, :feature_cols], norm_back[:, feature_cols:]])
    token_rows = lax.all_to_all(back_stack, "row", split_axis=1, concat_axis=2, tiled=True)
    branch = token_rows[0]
    d_norm_attn = token_rows[1]
    d_norm_mlp = token_rows[2]
    grad_qkv = lax.dot_general(
        attn_wide_in, qkv_grad_wide, CONTRACT_FIRST, preferred_element_type=jnp.float32
    )
    grad_out = lax.dot_general(
        attn_wide, grad_wide, CONTRACT_FIRST, preferred_element_type=jnp.float32
    )
    grad_up = lax.dot_general(
        mlp_wide_in, hidden_grad_wide, CONTRACT_FIRST, preferred_element_type=jnp.float32
    )
    grad_down = lax.dot_general(
        act_wide, grad_wide, CONTRACT_FIRST, preferred_element_type=jnp.float32
    )
    qkv_term = lax.dynamic_update_slice(
        jnp.zeros(qkv_bias.shape, jnp.float32),
        jnp.sum(d_qkv, axis=0, dtype=jnp.float32),
        (col_id * qkv_cols,),
    )
    up_term = lax.dynamic_update_slice(
        jnp.zeros(up_bias.shape, jnp.float32),
        jnp.sum(d_hidden, axis=0, dtype=jnp.float32),
        (col_id * up_cols,),
    )
    stat_terms = jnp.stack(
        [
            jnp.sum(grad_float, axis=0),
            jnp.sum(d_norm_attn * normed, axis=0),
            jnp.sum(d_norm_attn, axis=0),
            jnp.sum(d_norm_mlp * normed, axis=0),
            jnp.sum(d_norm_mlp, axis=0),
        ]
    )
    summed, smalls = reduce_grads(
        grad_qkv, grad_out, grad_up, grad_down, qkv_term, up_term, stat_terms
    )
    block_out = (x_float + branch + out_bias + down_bias).astype(jnp.bfloat16)
    d_normed = d_norm_attn * attn_gain + d_norm_mlp * mlp_gain
    in_grad = (
        grad_float
        + inv_std
        * (
            d_normed
            - jnp.mean(d_normed, axis=1, keepdims=True)
            - normed * jnp.mean(d_normed * normed, axis=1, keepdims=True)
        )
    ).astype(jnp.bfloat16)
    stat_sums = smalls[2]
    return (
        block_out,
        in_grad,
        stat_sums[1],
        stat_sums[2],
        stat_sums[3],
        stat_sums[4],
        summed[0],
        smalls[0],
        summed[1],
        stat_sums[0],
        summed[2],
        smalls[1],
        summed[3],
        stat_sums[0],
    )


def solution(mesh):
    return jax.shard_map(
        on_device,
        mesh=mesh,
        in_specs=(
            P(("dp", "row", "col"), None),
            P("dp", None),
            P(),
            P(),
            P(),
            P(),
            P("row", "col"),
            P(),
            P("col", "row"),
            P(),
            P("row", "col"),
            P(),
            P("col", "row"),
            P(),
            P(("dp", "row", "col"), None),
        ),
        out_specs=(
            P(("dp", "row", "col"), None),
            P(("dp", "row", "col"), None),
            P(),
            P(),
            P(),
            P(),
            P("row", "col"),
            P(),
            P("col", "row"),
            P(),
            P("row", "col"),
            P(),
            P("col", "row"),
            P(),
        ),
        check_vma=False,
    )
```

profile of v0, /device:TPU:0, one launch (start us, length us, event | category | flops | bytes accessed | tf_op | source)
XLA Modules:
  0.0 1732.0 jit_solution(10847321632112017351)
XLA Ops:
  11.4 2.0 copy.132
  13.5 40.9 %all_to_all.33 = bf16[3,512,768]{1,0,2:T(4,128)(2,1)S(1)} all-to-all(bf16[3,512,768]{1,0,2:T(4,128)(2,1)S(1)} %copy.132), channel_id=1, replica_groups=mesh['dp'=2,'row'=4,'col'=4] {'row'}, dimensions={2} | all-to-all | bytes 4718592 | tf_op jit(solution)/shard_map/all_to_all | solution.py:217
  56.8 167.2 %all-gather.6.cloned.1.call-done = bf16[3,8192,192]{1,2,0:T(8,128)(2,1)} async-done(((bf16[3,2048,192]{1,2,0:T(8,128)(2,1)}), bf16[3,8192,192]{1,2,0:T(8,128)(2,1)}) %all-gather.6.cloned.1.call-update) | async-done | bytes 9437200 | tf_op jit(solution)/shard_map/all_gather | solution.py:218
  224.0 12.0 fusion.65
  236.0 2.9 fusion.66
  238.9 20.1 %pad_maximum_fusion.1 = f32[8192,960]{0,1:T(8,128)} fusion(f32[8192,768]{0,1:T(8,128)} %fusion.65, f32[8192,192]{0,1:T(8,128)S(1)} %fusion.66), kind=kLoop, calls=%fused_computation.61 | loop fusion | flops 7864320 | bytes 62914560 | tf_op jit(solution)/shard_map/concatenate | solution.py:261
  259.9 15.8 fusion.60
  275.7 19.1 %fusion.62 = f32[8192,768]{0,1:T(8,128)} fusion(bf16[192,768]{1,0:T(8,128)(2,1)S(1)} %copy-done, bf16[3,8192,192]{1,2,0:T(8,128)(2,1)} %all-gather.6.cloned.1.call-done), kind=kOutput, calls=%fused_computation.102 | convolution fusion | flops 2415919104 | bytes 28606464 | tf_op jit(solution)/shard_map/dot_general | solution.py:226
  294.7 30.4 %pad_maximum_fusion = f32[8192,1344]{0,1:T(8,128)} fusion(f32[8192,768]{0,1:T(8,128)} %fusion.62, f32[8192,576]{0,1:T(8,128)} %fusion.60), kind=kLoop, calls=%fused_computation.60 | loop fusion | flops 11010048 | bytes 88080384 | tf_op jit(solution)/shard_map/concatenate | solution.py:223
  329.8 149.0 %reduce-scatter.9.cloned.1.call-done = f32[2048,960]{0,1:T(8,128)} async-done(((f32[8192,960]{0,1:T(8,128)}), f32[2048,960]{0,1:T(8,128)}) %reduce-scatter.9.cloned.1.call-update) | async-done | bytes 7864336 | tf_op jit(solution)/shard_map/reduce_scatter | solution.py:260
  483.6 300.4 %reduce-scatter.5.cloned.1.call-done = f32[2048,1344]{0,1:T(8,128)} async-done(((f32[8192,1344]{0,1:T(8,128)}), f32[2048,1344]{0,1:T(8,128)}) %reduce-scatter.5.cloned.1.call-update) | async-done | bytes 11010064 | tf_op jit(solution)/shard_map/reduce_scatter | solution.py:222
  784.0 4.9 slice_add_fusion.1
  788.9 6.9 reshape.286
  795.8 2.4 slice_bitcast_fusion.13
  800.6 2.2 maximum_bitcast_fusion.2
  802.8 2.5 copy.136
  805.3 2.5 copy.138
  809.5 41.2 %while.26 = (s32[]{:T(128)}, bf16[12,512,64]{1,2,0:T(8,128)(2,1)}, f32[12,512]{1,0:T(8,128)S(1)}, s32[12,512]{1,0:T(8,128)S(1)}, bf16[12,512,64]{2,1,0:T(8,128)(...) while((s32[]{:T(128)}, bf16[12,512,64]{1,2,0:T(8,128)(2,1)}, ...), condition=%wide.region_8.9_spmd, body=%wide.region_5.8_spmd.sunk | while | flops 70024704 | bytes 3635301 | solution.py:117
  850.7 90.3 %while.27 = (s32[]{:T(128)}, f32[12,512,64]{1,2,0:T(8,128)}, f32[12,512,64]{1,2,0:T(8,128)}, bf16[12,512,64]{1,2,0:T(8,128)(2,1)}, s32[12,512]{1,0:T(8,128)S(1)}...) while((s32[]{:T(128)}, f32[12,512,64]{1,2,0:T(8,128)}, ...), condition=%wide.region_13.14_spmd, body=%wide.region_11.13_spmd.sunk | while | flops 170982912 | bytes 9198709 | solution.py:159
  941.0 2.5 copy.170
  943.5 2.4 copy.171
  948.3 4.4 convert_reduce_fusion.1
  952.7 2.1 copy.164
  955.7 19.9 %convert_reduce_fusion = (f32[768]{0:T(1024)S(1)}, bf16[2048,768]{0,1:T(8,128)(2,1)}, bf16[2048,768]{0,1:T(8,128)(2,1)}) fusion(f32[768]{0:T(1024)S(1)} %dynamic_slice.40, f32[2048,1344]{0,1:T(8,128)} %reduce-scatter.5.cloned.1.call-done, f32[2048,960]{0,1:T(8,128)} %reduce-scatter.9.cloned.1.call-done), kind=kLoop, calls=%fused_computation.76 | loop fusion | flops 122682624 | bytes 18880512 | tf_op jit(solution)/shard_map/reduce_sum | solution.py:324
  978.9 40.3 %all-gather.12.cloned.1.call-done = bf16[8192,576]{0,1:T(8,128)(2,1)} async-done(((bf16[2048,576]{0,1:T(8,128)(2,1)}), bf16[8192,576]{0,1:T(8,128)(2,1)}) %all-gather.12.cloned.1.call-update) | async-done | bytes 9437200 | tf_op jit(solution)/shard_map/all_gather | solution.py:280
  1019.3 9.4 fusion.105
  1028.7 74.1 %all-gather.14.cloned.1.call-done = bf16[8192,768]{0,1:T(8,128)(2,1)} async-done(((bf16[2048,768]{0,1:T(8,128)(2,1)}), bf16[8192,768]{0,1:T(8,128)(2,1)}) %all-gather.14.cloned.1.call-update) | async-done | bytes 12582928 | tf_op jit(solution)/shard_map/all_gather | solution.py:281
  1102.8 10.4 fusion.106
  1113.2 13.2 pad_maximum_fusion.2
  1126.5 59.9 %all-gather.10.cloned.1.call-done = bf16[8192,768]{0,1:T(8,128)(2,1)} async-done(((bf16[2048,768]{0,1:T(8,128)(2,1)}), bf16[8192,768]{0,1:T(8,128)(2,1)}) %all-gather.10.cloned.1.call-update) | async-done | bytes 12582928 | tf_op jit(solution)/shard_map/all_gather | solution.py:248
  1186.4 10.1 fusion.104
  1196.5 20.0 %all-gather.8.cloned.1.call-done = bf16[8192,192]{0,1:T(8,128)(2,1)} async-done(((bf16[2048,192]{0,1:T(8,128)(2,1)}), bf16[8192,192]{0,1:T(8,128)(2,1)}) %all-gather.8.cloned.1.call-update) | async-done | bytes 3145744 | tf_op jit(solution)/shard_map/all_gather | solution.py:247
  1216.5 7.5 convolution_add_fusion
  1224.0 206.8 %reduce-scatter.11.cloned.1.call-done = f32[2048,384]{0,1:T(8,128)} async-done(((f32[8192,384]{0,1:T(8,128)}), f32[2048,384]{0,1:T(8,128)}) %reduce-scatter.11.cloned.1.call-update) | async-done | bytes 3145744 | tf_op jit(solution)/shard_map/reduce_scatter | solution.py:283
  1430.8 2.1 slice_bitcast_fusion.12
  1432.9 112.0 %reduce-scatter.7.cloned.1.call-done = f32[2048,192]{0,1:T(8,128)} async-done(((f32[8192,192]{0,1:T(8,128)}), f32[2048,192]{0,1:T(8,128)}) %reduce-scatter.7.cloned.1.call-update) | async-done | bytes 1572880 | tf_op jit(solution)/shard_map/reduce_scatter | solution.py:253
  1544.9 3.9 pad_maximum_fusion.3
  1548.7 8.5 copy.146
  1557.2 5.8 all-to-all-start.1
  1563.2 4.7 fusion.64
  1567.9 9.1 fusion.59
  1577.0 9.7 fusion.61
  1586.6 9.7 fusion.63
  1597.6 58.5 %all-to-all-done.1 = f32[3,2048,192]{2,0,1:T(4,128)} async-done(((f32[3,2048,192]{2,0,1:T(4,128)}), f32[3,2048,192]{2,0,1:T(4,128)}, u32[]{:S(2)}, u32[]{:S(2)}) %all-to-all-start.1) | async-done | bytes 4718624 | tf_op jit(solution)/shard_map/all_to_all | solution.py:301
  1656.1 8.8 copy.158
  1664.9 3.6 slice_reduce_fusion.6
  1673.0 41.1 %all-reduce = (f32[5,768]{1,0:T(8,128)S(1)}, f32[2304]{0:T(1024)}, f32[3072]{0:T(1024)}) all-reduce(f32[5,768]{1,0:T(8,128)S(1)} %stack.71, f32[2304]{0:T(1024)S(1)} %dynamic_update_slice.24, f32[3072]{0:T(1024)S(1)} %dynamic_update_slice.25), channel_id=1, replica_groups=mesh['dp'=2,'row'=4,'col'=4] {'dp','row','col'}, use_global_device_ids=true, to_apply=%region_22.23 | all-reduce | flops 9216 | bytes 73728 | tf_op jit(solution)/shard_map/psum | solution.py:183
  1721.1 1.9 copy.208
  (332 shorter events, 172.8 us)
Async XLA Ops:
  7.2 268.5 %copy-start = (bf16[192,768]{1,0:T(8,128)(2,1)S(1)}, bf16[192,768]{1,0:T(8,128)(2,1)}, u32[]{:S(2)}) copy-start(bf16[192,768]{1,0:T(8,128)(2,1)} %param.29) | copy-start | bytes 884740
  7.2 3.4 copy-start.13
  7.2 3.4 copy-start.22
  7.2 3.4 copy-start.15
  7.2 3.4 copy-start.23
  7.2 216.8 %all-gather.6.cloned.1.call-start = ((), (), s32[]{:S(2)}) async-start(), calls=%async_computation.6 | async-start | bytes 11796480 | tf_op jit(solution)/shard_map/all_gather | solution.py:218
  8.7 2.7 copy-start.1
  8.9 2.5 copy-start.17
  9.2 4.3 copy-start.19
  10.7 2.8 copy-start.3
  55.0 169.0 %copy-start.6 = (bf16[768,192]{0,1:T(8,128)(2,1)S(1)}, bf16[768,192]{0,1:T(8,128)(2,1)}, u32[]{:S(2)}) copy-start(bf16[768,192]{0,1:T(8,128)(2,1)} %param.31) | copy-start | bytes 884740
  56.8 179.2 %copy-start.10 = (bf16[192,192]{1,0:T(8,128)(2,1)S(1)}, bf16[192,192]{1,0:T(8,128)(2,1)}, u32[]{:S(2)}) copy-start(bf16[192,192]{1,0:T(8,128)(2,1)} %param.27) | copy-start | bytes 221188
  56.8 422.1 %reduce-scatter.9.cloned.1.call-start = ((), (), s32[]{:S(2)}) async-start(), calls=%async_computation.11 | async-start | bytes 39321600 | tf_op jit(solution)/shard_map/reduce_scatter | solution.py:260
  258.9 0.9 copy-start.5
  258.9 525.1 %reduce-scatter.5.cloned.1.call-start = ((), (), s32[]{:S(2)}) async-start(), calls=%async_computation.7 | async-start | bytes 55050240 | tf_op jit(solution)/shard_map/reduce_scatter | solution.py:222
  325.2 0.8 copy-start.12
  325.2 694.1 %all-gather.12.cloned.1.call-start = ((), (), s32[]{:S(2)}) async-start(), calls=%async_computation.12 | async-start | bytes 11796480 | tf_op jit(solution)/shard_map/all_gather | solution.py:280
  941.0 5.6 copy-start.8
  954.9 148.0 %all-gather.14.cloned.1.call-start = ((), (), s32[]{:S(2)}) async-start(), calls=%async_computation.13 | async-start | bytes 15728640 | tf_op jit(solution)/shard_map/all_gather | solution.py:281
  975.6 1.1 copy-start.9
  975.7 210.7 %all-gather.10.cloned.1.call-start = ((), (), s32[]{:S(2)}) async-start(), calls=%async_computation.9 | async-start | bytes 15728640 | tf_op jit(solution)/shard_map/all_gather | solution.py:248
  976.3 240.3 %all-gather.8.cloned.1.call-start = ((), (), s32[]{:S(2)}) async-start(), calls=%async_computation.8 | async-start | bytes 3932160 | tf_op jit(solution)/shard_map/all_gather | solution.py:247
  978.5 452.3 %reduce-scatter.11.cloned.1.call-start = ((), (), s32[]{:S(2)}) async-start(), calls=%async_computation.14 | async-start | bytes 15728640 | tf_op jit(solution)/shard_map/reduce_scatter | solution.py:283
  1126.4 60.0 %copy-start.7 = (bf16[768,192]{0,1:T(8,128)(2,1)S(1)}, bf16[768,192]{0,1:T(8,128)(2,1)}, u32[]{:S(2)}) copy-start(bf16[768,192]{0,1:T(8,128)(2,1)} %param.31) | copy-start | bytes 884740
  1126.4 90.1 %copy-start.11 = (bf16[192,192]{1,0:T(8,128)(2,1)S(1)}, bf16[192,192]{1,0:T(8,128)(2,1)}, u32[]{:S(2)}) copy-start(bf16[192,192]{1,0:T(8,128)(2,1)} %param.27) | copy-start | bytes 221188
  1126.4 418.4 %reduce-scatter.7.cloned.1.call-start = ((), (), s32[]{:S(2)}) async-start(), calls=%async_computation.10 | async-start | bytes 7864320 | tf_op jit(solution)/shard_map/reduce_scatter | solution.py:253
  1557.2 98.9 %all-to-all-start.1 = ((f32[3,2048,192]{2,0,1:T(4,128)}), f32[3,2048,192]{2,0,1:T(4,128)}, u32[]{:S(2)}, u32[]{:S(2)}) async-start(f32[3,2048,192]{2,0,1:T(4,128)} %copy.146), calls=%async_computation.5 | async-start | bytes 16777216 | tf_op jit(solution)/shard_map/all_to_all | solution.py:301
  1563.0 154.1 %all-reduce.4.cloned.1.call-start = ((), (), s32[]{:S(2)}) async-start(), calls=%async_computation.15 | async-start | bytes 3735552 | tf_op jit(solution)/shard_map/psum | solution.py:182
  1563.2 13.8 slice-start
  1563.2 13.7 slice-start.1
  1567.9 9.1 slice-start.2
  1586.6 9.7 copy-start.14
  1586.6 9.8 copy-start.16
  1668.5 1.6 copy-start.2
  1668.5 1.6 copy-start.18
  1668.5 1.6 copy-start.20
  1669.1 2.1 copy-start.4
  1669.1 2.1 copy-start.24
  1669.1 2.1 copy-start.25
  1714.8 10.2 copy-start.21
Sparse Core Ops, SparseCore 0:
  56.9 167.0 all-gather.5
  259.1 219.7 reduce-scatter.8
  481.6 302.3 reduce-scatter.4
  955.0 64.2 all-gather.11
  1020.7 82.0 all-gather.13
  1104.2 82.0 all-gather.9
  1187.9 28.5 all-gather.7
  1218.9 211.8 reduce-scatter.10
  1433.1 111.7 reduce-scatter.6
  1596.5 59.4 all-reduce.3
where the time goes:
time: 1740 us; the launch traced here: 1730 us
  waiting for transfers between devices  1190 us (68%)
  matrix products  244 us (14%)
  other arithmetic  116 us (7%)
  blocking collectives  82.1 us (5%)
  local copies, waits for them, and re-layouts  78.5 us (5%)
    reduce_scatter x1, waiting for transfers between devices, on_device(): lax.psum_scatter(jnp.concatenate([jnp.dot(attn_wide_in, qkv_weight, prefe...  300 us
    reduce_scatter x1, waiting for transfers between devices, on_device(): lax.psum_scatter(jnp.concatenate([lax.dot_general(qkv_grad_wide, qkv_weig...  207 us
    all_gather x1, waiting for transfers between devices, on_device(): wide_rows = lax.all_gather(grid_rows, 'col', axis=1, tiled=True)  167 us
    reduce_scatter x1, waiting for transfers between devices, on_device(): lax.psum_scatter(jnp.concatenate([lax.dot_general(grad_wide, out_weight,...  149 us
    reduce_scatter x1, waiting for transfers between devices, on_device(): lax.psum_scatter(jnp.dot(attn_part, out_weight, preferred_element_type=jn...  112 us
    all_gather x1, waiting for transfers between devices, on_device(): lax.all_gather(d_hidden, 'row', axis=0, tiled=True)  74.1 us
    all_gather x1, waiting for transfers between devices, on_device(): lax.all_gather(active, 'row', axis=0, tiled=True)  59.9 us
    all_to_all x1, waiting for transfers between devices, on_device(): lax.all_to_all(back_stack, 'row', split_axis=1, concat_axis=2, tiled=True)  58.5 us
  transfers between devices with their start and end apart: 11, of which 10 were waited for; matrix products, arithmetic and copies ran while one was open for 12% of the time, Pallas kernels for 0%

commit v1 on v0

v1 whole, which is shorter than its diff:
```python
import functools
import math

import jax
import jax.numpy as jnp
from jax import lax
from jax.experimental import pallas as pl
from jax.experimental.pallas import tpu as pltpu
from jax.sharding import PartitionSpec as P

HD = 64
ROT = 16
QKV = 3 * HD
HEAD = 4 * HD
EPSILON = 1e-05
ROPE_BASE = 10000.0
NEAR = 128
LONGEST = 256
F32 = jnp.float32
BF16 = jnp.bfloat16


def dot_nn(a, b):
    return lax.dot_general(a, b, (((1,), (0,)), ((), ())), preferred_element_type=F32)


def dot_nt(a, b):
    return lax.dot_general(a, b, (((1,), (1,)), ((), ())), preferred_element_type=F32)


def rotary_tables(seg_row):
    length = seg_row.shape[0]
    ids = lax.iota(jnp.int32, length)
    previous = jnp.concatenate([seg_row[:1] - 1, seg_row[:-1]])
    starts = lax.cummax(jnp.where(seg_row != previous, ids, 0))
    places = (ids - starts).astype(F32)
    halves = ROT // 2
    lane = lax.iota(jnp.int32, 2 * HD) % HD
    step = (lane % halves).astype(F32)
    frequency = ROPE_BASE ** (-(step * (2.0 / ROT)))
    angles = places[:, None] * frequency[None, :]
    cosine, sine = jnp.cos(angles), jnp.sin(angles)
    turned = (lane < ROT)[None, :]
    first = (lane < halves)[None, :]
    keep = jnp.where(turned, cosine, 1.0)
    ahead = jnp.where(first, -sine, 0.0)
    behind = jnp.where(turned & ~first, sine, 0.0)
    return keep, ahead, behind


def assemble(me_ref, w_refs, w_scr):
    rows = w_refs[0].shape[1]
    for j, ref in enumerate(w_refs):
        at = pl.multiple_of((me_ref[0] ^ j) * rows, 16)
        w_scr[pl.ds(at, rows), :] = ref[0]


def hand_out(me_ref, g_scr, g_refs):
    rows = g_refs[0].shape[1]
    for j, ref in enumerate(g_refs):
        at = pl.multiple_of((me_ref[0] ^ j) * rows, 16)
        ref[0] = g_scr[pl.ds(at, rows), :]


def attention_kernel(
    na_ref, naT_ref, cot_ref, cotT_ref, w_ref, bias_ref, keep_ref, ahead_ref, behind_ref, segc_ref, segr_ref,
    branch_ref, dna_ref, g_ref, dbias_ref,
    bias_scr, qkv_scr, dattn_scr, dqkv_scr, mix_scr,
):
    length, width = na_ref.shape
    block_cols = w_ref.shape[-1]
    heads = block_cols // HEAD
    step = pl.program_id(0)

    @pl.when(step == 0)
    def _():
        branch_ref[...] = jnp.zeros_like(branch_ref)
        dna_ref[...] = jnp.zeros_like(dna_ref)
        rows = lax.broadcasted_iota(jnp.int32, (length, length), 0)
        cols = lax.broadcasted_iota(jnp.int32, (length, length), 1)
        inside = (cols <= rows) & (segc_ref[...] == segr_ref[...])
        bias_scr[...] = jnp.where(inside, 0.0, -jnp.inf)

    w = w_ref[...].reshape(width, block_cols)
    w_vo = jnp.concatenate([w[:, i * HEAD + 2 * HD : (i + 1) * HEAD] for i in range(heads)], axis=1)
    qkv_scr[...] = dot_nn(na_ref[...], w) + bias_ref[0]
    dattn_scr[...] = dot_nn(cot_ref[...], w_vo).astype(BF16)

    low = lax.broadcasted_iota(jnp.int32, (length, 2 * HD), 1) < HD
    keep, ahead, behind = keep_ref[...], ahead_ref[...], behind_ref[...]
    none = jnp.zeros((length, 2 * HD), BF16)
    blocks = length // NEAR
    for i in range(heads):
        qk = qkv_scr[:, i * HEAD : i * HEAD + 2 * HD]
        qk = qk * keep + pltpu.roll(qk, 2 * HD - ROT // 2, 1) * ahead + pltpu.roll(qk, ROT // 2, 1) * behind
        q32 = jnp.where(low, qk * (1.0 / math.sqrt(HD)), 0.0)
        k32 = jnp.where(low, pltpu.roll(qk, HD, 1), 0.0)
        v32 = jnp.where(low, 0.0, pltpu.roll(qkv_scr[:, i * HEAD + 2 * HD : (i + 1) * HEAD], HD, 1))
        q0 = q32.astype(BF16)
        k0 = k32.astype(BF16)
        v1 = v32.astype(BF16)
        go = dattn_scr[:, i * 2 * HD : (i + 1) * 2 * HD]
        go1 = jnp.where(low, none, go)
        qT = q32.T[:HD].astype(BF16)
        goT = go.astype(F32).T[HD:].astype(BF16)
        dq_parts = []
        mix_parts = []
        dk_sum = [None] * blocks
        dv_sum = [None] * blocks
        for b in range(blocks):
            r0, r1 = b * NEAR, (b + 1) * NEAR
            lo = max(0, r0 - LONGEST)
            s = dot_nt(q0[r0:r1], k0[lo:r1]) + bias_scr[r0:r1, lo:r1]
            e = jnp.exp(s - jnp.max(s, axis=1, keepdims=True))
            p = e * (1.0 / jnp.sum(e, axis=1, keepdims=True))
            p_low = p.astype(BF16)
            mix = dot_nn(p_low, v1[lo:r1])
            mix_parts.append(mix.astype(BF16))
            dp = dot_nt(go1[r0:r1], v1[lo:r1])
            delta = jnp.sum(mix * go1[r0:r1].astype(F32), axis=1, keepdims=True)
            ds = (p * (dp - delta)).astype(BF16)
            dq_parts.append(dot_nn(ds, k0[lo:r1]))
            dkT = dot_nn(qT[:, r0:r1], ds)
            dvT = dot_nn(goT[:, r0:r1], p_low)
            for n in range(lo // NEAR, b + 1):
                at = n * NEAR - lo
                dk_one, dv_one = dkT[:, at : at + NEAR], dvT[:, at : at + NEAR]
                dk_sum[n] = dk_one if dk_sum[n] is None else dk_sum[n] + dk_one
                dv_sum[n] = dv_one if dv_sum[n] is None else dv_sum[n] + dv_one
        dvk = jnp.concatenate(
            [jnp.concatenate([jnp.concatenate(dv_sum, axis=1), jnp.concatenate(dk_sum, axis=1)], axis=0)], axis=0
        ).T
        dqk = jnp.where(low, jnp.concatenate(dq_parts, axis=0) * (1.0 / math.sqrt(HD)), dvk)
        dqk = dqk * keep - pltpu.roll(dqk, 2 * HD - ROT // 2, 1) * ahead - pltpu.roll(dqk, ROT // 2, 1) * behind
        dqkv_scr[:, i * HEAD : i * HEAD + 2 * HD] = dqk.astype(BF16)
        dqkv_scr[:, i * HEAD + 2 * HD : (i + 1) * HEAD] = jnp.where(low, dvk, 0.0).astype(BF16)
        mix_scr[:, i * 2 * HD : (i + 1) * 2 * HD] = jnp.concatenate(mix_parts, axis=0)

    dqkv = dqkv_scr[...]
    mix = mix_scr[...]
    branch_ref[...] += dot_nt(mix, w_vo)
    dna_ref[...] += dot_nt(dqkv, w)
    dbias_ref[0] = jnp.sum(dqkv.astype(F32), axis=0, keepdims=True)
    for i in range(heads):
        g_qk = dot_nn(naT_ref[...], dqkv[:, i * HEAD : i * HEAD + 2 * HD])
        g_vo = dot_nn(naT_ref[...], dqkv[:, i * HEAD + 2 * HD : (i + 1) * HEAD]) + dot_nn(
            cotT_ref[...], mix[:, i * 2 * HD : (i + 1) * 2 * HD]
        )
        both = jnp.concatenate([g_qk, g_vo], axis=1).astype(BF16)
        g_ref[..., i * HEAD : (i + 1) * HEAD] = both.reshape(g_ref.shape[:-1] + (HEAD,))


def attention_part(norm_attn, norm_attn_t, cot, cot_t, w_all, bias, tables, seg_row):
    length, width = norm_attn.shape
    row_size, col_size, rows, block_cols = w_all.shape
    heads = block_cols // HEAD
    whole = lambda *shape: pl.BlockSpec(shape, lambda c: (0,) * len(shape))
    w_spec = pl.BlockSpec((row_size, 1, rows, block_cols), lambda c: (0, c, 0, 0))
    vec_spec = pl.BlockSpec((1, 1, block_cols), lambda c: (c, 0, 0))
    flops = col_size * 2 * length * width * block_cols * 5
    return pl.pallas_call(
        attention_kernel,
        grid=(col_size,),
        in_specs=[
            whole(length, width), whole(width, length), whole(length, width), whole(width, length),
            w_spec, vec_spec,
            whole(length, 2 * HD), whole(length, 2 * HD), whole(length, 2 * HD),
            whole(length, 1), whole(1, length),
        ],
        out_specs=[whole(length, width), whole(length, width), w_spec, vec_spec],
        out_shape=[
            jax.ShapeDtypeStruct((length, width), F32),
            jax.ShapeDtypeStruct((length, width), F32),
            jax.ShapeDtypeStruct(w_all.shape, BF16),
            jax.ShapeDtypeStruct((col_size, 1, block_cols), F32),
        ],
        scratch_shapes=[
            pltpu.VMEM((length, length), F32),
            pltpu.VMEM((length, block_cols), F32),
            pltpu.VMEM((length, heads * 2 * HD), BF16),
            pltpu.VMEM((length, block_cols), BF16),
            pltpu.VMEM((length, heads * 2 * HD), BF16),
        ],
        compiler_params=pltpu.CompilerParams(vmem_limit_bytes=48 * 2**20),
        cost_estimate=pl.CostEstimate(flops=flops, bytes_accessed=20 * 2**20, transcendentals=0),
    )(norm_attn, norm_attn_t, cot, cot_t, w_all, bias, *tables, seg_row[:, None], seg_row[None, :])


def mlp_kernel(pieces, me_ref, nm_ref, nmT_ref, cot_ref, cotT_ref, *rest):
    up_refs, down_refs = rest[:pieces], rest[pieces : 2 * pieces]
    bias_ref, branch_ref, dnm_ref, dbias_ref = rest[2 * pieces : 2 * pieces + 4]
    gu_refs = rest[2 * pieces + 4 : 3 * pieces + 4]
    gd_refs = rest[3 * pieces + 4 : 4 * pieces + 4]
    wu_scr, wd_scr, act_scr, dh_scr, g_scr = rest[4 * pieces + 4 :]
    length, width = nm_ref.shape
    step = pl.program_id(0)
    tile = 256

    @pl.when(step == 0)
    def _():
        branch_ref[...] = jnp.zeros_like(branch_ref)
        dnm_ref[...] = jnp.zeros_like(dnm_ref)

    assemble(me_ref, up_refs, wu_scr)
    assemble(me_ref, down_refs, wd_scr)
    dbias_ref[0] = jnp.zeros_like(dbias_ref[0])

    @pl.loop(0, length // tile)
    def _(t):
        rows = pl.ds(pl.multiple_of(t * tile, tile), tile)
        hidden = dot_nn(nm_ref[rows, :], wu_scr[...]) + bias_ref[0]
        d_act = dot_nn(cot_ref[rows, :], wd_scr[...])
        gate = 0.5 * (1.0 + lax.erf(hidden * (1.0 / math.sqrt(2.0))))
        act = (hidden * gate).astype(BF16)
        slope = gate + hidden * jnp.exp(-0.5 * hidden * hidden) * (1.0 / math.sqrt(2.0 * math.pi))
        dh = (d_act * slope).astype(BF16)
        act_scr[rows, :] = act
        dh_scr[rows, :] = dh
        dbias_ref[0] += jnp.sum(dh.astype(F32), axis=0, keepdims=True)
        branch_ref[rows, :] += dot_nt(act, wd_scr[...])
        dnm_ref[rows, :] += dot_nt(dh, wu_scr[...])

    for left, right, outs in ((nmT_ref, dh_scr, gu_refs), (cotT_ref, act_scr, gd_refs)):

        @pl.loop(0, width // tile)
        def _(t):
            rows = pl.ds(pl.multiple_of(t * tile, tile), tile)
            g_scr[rows, :] = dot_nn(left[rows, :], right[...]).astype(BF16)

        hand_out(me_ref, g_scr, outs)


def mlp_part(me, norm_mlp, norm_mlp_t, cot, cot_t, up_pieces, down_pieces, bias):
    length, width = norm_mlp.shape
    col_size, rows, block_cols = up_pieces[0].shape
    pieces = len(up_pieces)
    whole = lambda *shape: pl.BlockSpec(shape, lambda c: (0,) * len(shape))
    piece_spec = pl.BlockSpec((1, rows, block_cols), lambda c: (c, 0, 0))
    vec_spec = pl.BlockSpec((1, 1, block_cols), lambda c: (c, 0, 0))
    flops = col_size * 2 * length * width * block_cols * 6
    outs = pl.pallas_call(
        functools.partial(mlp_kernel, pieces),
        grid=(col_size,),
        in_specs=[
            pl.BlockSpec(memory_space=pltpu.SMEM),
            whole(length, width), whole(width, length), whole(length, width), whole(width, length),
        ]
        + [piece_spec] * (2 * pieces)
        + [vec_spec],
        out_specs=[whole(length, width), whole(length, width), vec_spec] + [piece_spec] * (2 * pieces),
        out_shape=[
            jax.ShapeDtypeStruct((length, width), F32),
            jax.ShapeDtypeStruct((length, width), F32),
            jax.ShapeDtypeStruct((col_size, 1, block_cols), F32),
        ]
        + [jax.ShapeDtypeStruct((col_size, rows, block_cols), BF16)] * (2 * pieces),
        scratch_shapes=[
            pltpu.VMEM((width, block_cols), BF16),
            pltpu.VMEM((width, block_cols), BF16),
            pltpu.VMEM((length, block_cols), BF16),
            pltpu.VMEM((length, block_cols), BF16),
            pltpu.VMEM((width, block_cols), BF16),
        ],
        compiler_params=pltpu.CompilerParams(vmem_limit_bytes=48 * 2**20),
        cost_estimate=pl.CostEstimate(flops=flops, bytes_accessed=30 * 2**20, transcendentals=0),
    )(me, norm_mlp, norm_mlp_t, cot, cot_t, *up_pieces, *down_pieces, bias)
    return outs[0], outs[1], outs[2], outs[3 : 3 + pieces], outs[3 + pieces :]


def swap(value, bit):
    axis, flip = ("dp", 1) if bit == 1 else ("row", bit // 2)
    size = lax.axis_size(axis)
    return lax.ppermute(value, axis, [(i, i ^ flip) for i in range(size)])


def gather_pieces(own, order):
    pieces = {0: own}
    for bit in order:
        for j in list(pieces):
            pieces[j ^ bit] = swap(pieces[j], bit)
    return [pieces[j] for j in range(len(pieces))]


def scatter_pieces(pieces, order):
    pieces = dict(enumerate(pieces))
    for bit in order:
        for j in [j for j in pieces if j & bit]:
            came = swap(pieces.pop(j), bit)
            kept = pieces[j ^ bit]
            pieces[j ^ bit] = (kept.astype(F32) + came.astype(F32)).astype(BF16)
    return pieces[0]


def sum_other_pairs(value):
    flip = 2
    while flip < lax.axis_size("dp"):
        value = value + lax.ppermute(value, "dp", [(i, i ^ flip) for i in range(lax.axis_size("dp"))])
        flip *= 2
    return value


def on_device(
    tokens_in,
    segment_ids,
    attn_gain,
    attn_shift,
    mlp_gain,
    mlp_shift,
    qkv_weight,
    qkv_bias,
    out_weight,
    out_bias,
    up_weight,
    up_bias,
    down_weight,
    down_bias,
    out_cotangent,
):
    row_size = lax.axis_size("row")
    col_size = lax.axis_size("col")
    length, width = tokens_in.shape
    rows = qkv_weight.shape[0]
    half_rows = rows // 2
    local_heads = qkv_weight.shape[1] // QKV
    block_cols = local_heads * HEAD
    up_cols = up_weight.shape[1]
    row_id = lax.axis_index("row")
    col_id = lax.axis_index("col")
    half = lax.axis_index("dp") % 2
    me = row_id * 2 + half
    row_bits = [2 << i for i in range(row_size.bit_length() - 1)]
    far_bits = row_bits[1:][::-1]

    head_weight = jnp.concatenate(
        [qkv_weight.reshape(rows, local_heads, QKV), out_weight.T.reshape(rows, local_heads, HD)], axis=2
    ).reshape(rows, block_cols)
    w_attn = lax.all_gather(head_weight, ("row", "col"), axis=0, tiled=False)
    w_attn = w_attn.reshape(row_size, col_size, rows, block_cols)
    up_half = lax.dynamic_slice_in_dim(up_weight, half * half_rows, half_rows, axis=0)
    down_half = lax.dynamic_slice_in_dim(down_weight, half * half_rows, half_rows, axis=1).T
    up_own = lax.all_gather(up_half, "col", axis=0, tiled=False)
    down_own = lax.all_gather(down_half, "col", axis=0, tiled=False)
    up_pieces = gather_pieces(up_own, [1] + far_bits + row_bits[:1])
    down_pieces = gather_pieces(down_own, far_bits + [1] + row_bits[:1])

    x_float = tokens_in.astype(F32)
    grad_float = out_cotangent.astype(F32)
    center = x_float - jnp.mean(x_float, axis=1, keepdims=True)
    inv_std = lax.rsqrt(jnp.mean(center * center, axis=1, keepdims=True) + EPSILON)
    normed = center * inv_std
    norm_attn = (normed * attn_gain + attn_shift).astype(BF16)
    norm_mlp = (normed * mlp_gain + mlp_shift).astype(BF16)
    cot_t = out_cotangent.T
    seg_row = lax.dynamic_index_in_dim(segment_ids, row_id * col_size + col_id, axis=0, keepdims=False)
    tables = rotary_tables(seg_row)
    head_bias = jnp.pad(
        qkv_bias.reshape(col_size, local_heads, QKV), ((0, 0), (0, 0), (0, HEAD - QKV))
    ).reshape(col_size, 1, block_cols)

    attn_branch, d_norm_attn, g_attn, d_bias_attn = attention_part(
        norm_attn, norm_attn.T, out_cotangent, cot_t, w_attn, head_bias, tables, seg_row
    )
    g_attn = lax.psum_scatter(
        g_attn.reshape(row_size * col_size * rows, block_cols), ("row", "col"), scatter_dimension=0, tiled=True
    )
    g_attn = lax.psum(g_attn, "dp").astype(F32)

    mlp_branch, d_norm_mlp, d_bias_up, g_up, g_down = mlp_part(
        me.reshape(1).astype(jnp.int32), norm_mlp, norm_mlp.T, out_cotangent, cot_t, up_pieces, down_pieces,
        up_bias.reshape(col_size, 1, up_cols),
    )
    g_up = scatter_pieces(g_up, row_bits[:1] + far_bits + [1])
    g_down = scatter_pieces(g_down, row_bits[:1] + [1] + far_bits)
    g_mlp = lax.psum_scatter(
        jnp.concatenate([g_up, g_down], axis=2).reshape(col_size * half_rows, 2 * up_cols),
        "col", scatter_dimension=0, tiled=True,
    )
    g_mlp = sum_other_pairs(g_mlp.astype(F32)).astype(BF16)
    g_other = swap(g_mlp, 1)
    g_mlp = jnp.where(
        half == 0, jnp.concatenate([g_mlp, g_other], axis=0), jnp.concatenate([g_other, g_mlp], axis=0)
    ).astype(F32)

    block_out = (x_float + (attn_branch + mlp_branch) + out_bias + down_bias).astype(BF16)
    d_normed = d_norm_attn * attn_gain + d_norm_mlp * mlp_gain
    in_grad = (
        grad_float
        + inv_std
        * (
            d_normed
            - jnp.mean(d_normed, axis=1, keepdims=True)
            - normed * jnp.mean(d_normed * normed, axis=1, keepdims=True)
        )
    ).astype(BF16)
    smalls = jnp.concatenate(
        [
            jnp.sum(grad_float, axis=0),
            jnp.sum(d_norm_attn * normed, axis=0),
            jnp.sum(d_norm_attn, axis=0),
            jnp.sum(d_norm_mlp * normed, axis=0),
            jnp.sum(d_norm_mlp, axis=0),
            d_bias_up.reshape(-1),
            d_bias_attn.reshape(col_size * local_heads, HEAD)[:, :QKV].reshape(-1),
        ]
    ).astype(BF16)
    smalls = jnp.sum(
        lax.all_gather(smalls, ("dp", "row", "col"), axis=0, tiled=False).astype(F32), axis=0
    )
    stats = smalls[: 5 * width].reshape(5, width)
    grad_up_bias = smalls[5 * width : 5 * width + up_bias.shape[0]]
    grad_qkv_bias = smalls[5 * width + up_bias.shape[0] :]
    g_heads = g_attn.reshape(rows, local_heads, HEAD)
    return (
        block_out,
        in_grad,
        stats[1],
        stats[2],
        stats[3],
        stats[4],
        g_heads[:, :, :QKV].reshape(rows, local_heads * QKV),
        grad_qkv_bias,
        g_heads[:, :, QKV:].reshape(rows, local_heads * HD).T,
        stats[0],
        g_mlp[:, :up_cols],
        grad_up_bias,
        g_mlp[:, up_cols:].T,
        stats[0],
    )


def solution(mesh):
    return jax.shard_map(
        on_device,
        mesh=mesh,
        in_specs=(
            P(("dp", "row", "col"), None),
            P("dp", None),
            P(),
            P(),
            P(),
            P(),
            P("row", "col"),
            P(),
            P("col", "row"),
            P(),
            P("row", "col"),
            P(),
            P("col", "row"),
            P(),
            P(("dp", "row", "col"), None),
        ),
        out_specs=(
            P(("dp", "row", "col"), None),
            P(("dp", "row", "col"), None),
            P(),
            P(),
            P(),
            P(),
            P("row", "col"),
            P(),
            P("col", "row"),
            P(),
            P("row", "col"),
            P(),
            P("col", "row"),
            P(),
        ),
        check_vma=False,
    )
```

time: 1740 us -> 374 us (0.21)
  waiting for transfers between devices: 1190 us -> 75.8 us
  matrix products: 244 us -> 0 us
  other arithmetic: 116 us -> 23.2 us
  Pallas kernels: 0 us -> 78.4 us
  local copies, waits for them, and re-layouts: 78.5 us -> 36.7 us
  blocking collectives: 82.1 us -> 121 us
    reduce_scatter x4 -> x2, waiting for transfers between devices: 768 us -> 0.03 us  [the longest x1 0.03 us: on_device(): lax.psum_scatter(jnp.concatenate([g_up, g_down], axis=2).reshape(col_size...]
    all_gather x5 -> x1, waiting for transfers between devices: 362 us -> 0.01 us  [on_device(): w_attn = lax.all_gather(head_weight, ('row', 'col'), axis=0, tiled=False)]
    dot_general x96 -> x0, matrix products: 244 us -> none  [the longest x12 22.2 us: backward_item(): jnp.einsum('qk,qd->kd', score_grad, query_one, preferred_element_type=jnp...]
    all_gather x0 -> x3, blocking collectives: none -> 121 us  [the longest x1 82.6 us: on_device(): lax.all_gather(smalls, ('dp', 'row', 'col'), axis=0, tiled=False)]
    pallas_call x0 -> x2, Pallas kernels: none -> 78.4 us  [the longest x1 51.5 us: attention_part(): pl.pallas_call(attention_kernel, grid=(col_size,), in_specs=[whole(length...]
    concatenate x4 -> x2, other arithmetic: 63.8 us -> 2.11 us  [the longest x1 1.15 us: on_device(): jnp.concatenate([g_up, g_down], axis=2)]
    all_to_all x1 -> x0, waiting for transfers between devices: 58.5 us -> none  [on_device(): lax.all_to_all(back_stack, 'row', split_axis=1, concat_axis=2, tiled=True)]
    ppermute x0 -> x29, waiting for transfers between devices: none -> 57 us  [swap(): return lax.ppermute(value, axis, [(i, i ^ flip) for i in range(size)])]
  transfers between devices with their start and end apart: 11 -> 33, of which waited for: 10 -> 11; matrix products, arithmetic and copies ran while one was open for 12% -> 12% of each run, Pallas kernels for 0% -> 21%
where the time goes in v1:
time: 374 us; the launch traced here: 373 us
  blocking collectives  121 us (32%)
  Pallas kernels  78.4 us (21%)
  waiting for transfers between devices  75.8 us (20%)
  local copies, waits for them, and re-layouts  36.7 us (10%)
  other arithmetic  23.2 us (6%)
  starting transfers between devices  21.2 us (6%)
  between operations  16.1 us (4%)
    all_gather x1, blocking collectives, on_device(): lax.all_gather(smalls, ('dp', 'row', 'col'), axis=0, tiled=False)  82.6 us
    ppermute x29, waiting for transfers between devices, swap(): return lax.ppermute(value, axis, [(i, i ^ flip) for i in range(size)])  57 us
    pallas_call x1, Pallas kernels, attention_part(): pl.pallas_call(attention_kernel, grid=(col_size,), in_specs=[whole(length...  51.5 us
    pallas_call x1, Pallas kernels, mlp_part(): pl.pallas_call(functools.partial(mlp_kernel, pieces), grid=(col_size,), i...  26.9 us
    all_gather x1, blocking collectives, on_device(): down_own = lax.all_gather(down_half, 'col', axis=0, tiled=False)  21.3 us
    ppermute x29, starting transfers between devices, swap(): return lax.ppermute(value, axis, [(i, i ^ flip) for i in range(size)])  20.7 us
    psum x1, waiting for transfers between devices, on_device(): g_attn = lax.psum(g_attn, 'dp').astype(F32)  18.7 us
    all_gather x1, blocking collectives, on_device(): up_own = lax.all_gather(up_half, 'col', axis=0, tiled=False)  17.5 us
  transfers between devices with their start and end apart: 33, of which 11 were waited for; matrix products, arithmetic and copies ran while one was open for 12% of the time, Pallas kernels for 21%

profile of v1, /device:TPU:0, one launch (start us, length us, event | category | flops | bytes accessed | tf_op | source)
XLA Modules:
  0.0 372.8 jit_solution(14385058946691650748)
XLA Ops:
  8.1 1.1 copy.87
  11.2 21.3 %all-gather.1 = bf16[384,768]{1,0:T(8,128)(2,1)S(1)} all-gather(bf16[96,768]{1,0:T(8,128)(2,1)S(1)} %dynamic-slice_bitcast_fusion), channel_id=3, replica_groups=mesh['dp'=2,'row'=4,'col'=4] {'col'}, dimensions={0}, use_global_device_ids=true | all-gather | bytes 737280 | tf_op jit(solution)/shard_map/all_gather | solution.py:342
  32.5 1.5 collective-permute-start.10
  34.1 17.5 %all-gather = bf16[384,768]{1,0:T(8,128)(2,1)S(1)} all-gather(bf16[96,768]{1,0:T(8,128)(2,1)S(1)} %constant_dynamic-slice_fusion.2), channel_id=2, replica_groups=mesh['dp'=2,'row'=4,'col'=4] {'col'}, dimensions={0}, use_global_device_ids=true | all-gather | bytes 737280 | tf_op jit(solution)/shard_map/all_gather | solution.py:341
  51.6 1.5 collective-permute-start
  53.1 1.6 collective-permute-start.3
  55.8 12.2 %collective-permute-done.rest_1_ = bf16[4,96,768]{2,1,0:T(8,128)(2,1)} collective-permute-done((bf16[4,96,768]{2,1,0:T(8,128)(2,1)S(1)}, bf16[4,96,768]{2,1,0:T(8,128)(2,1)}, u32[]{:S(2)}, u32[]{:S(2)}) %collective-permute-start) | collective-permute-done | bytes 589856 | tf_op jit(solution)/shard_map/ppermute | solution.py:273
  68.1 1.5 collective-permute-start.11
  69.5 3.6 collective-permute-done.3.rest_4_
  73.4 6.5 %collective-permute-done.7.rest_9_ = bf16[4,96,768]{2,1,0:T(8,128)(2,1)S(1)} collective-permute-done((bf16[4,96,768]{2,1,0:T(8,128)(2,1)S(1)}, bf16[4,96,768]{2,1,0:T(8,128)(2,1)S(1)}, u32[]{:S(2)}, u32[]{:S(2)}) %collective-permute-start.7) | collective-permute-done | bytes 589856 | tf_op jit(solution)/shard_map/ppermute | solution.py:273
  82.0 4.4 %collective-permute-done.11.rest_13_ = bf16[4,96,768]{2,1,0:T(8,128)(2,1)} collective-permute-done((bf16[4,96,768]{2,1,0:T(8,128)(2,1)}, bf16[4,96,768]{2,1,0:T(8,128)(2,1)}, u32[]{:S(2)}, u32[]{:S(2)}) %collective-permute-start.11) | collective-permute-done | bytes 589856 | tf_op jit(solution)/shard_map/ppermute | solution.py:273
  88.1 1.2 copy.92.nm_ref
  89.3 1.2 copy.86
  90.6 26.9 %shard_map.255 = (f32[512,768]{1,0:T(8,128)}, f32[512,768]{1,0:T(8,128)}, f32[4,1,768]{2,1,0:T(1,128)S(1)}, bf16[4,96,768]{2,1,0:T(8,128)(2,1)S(1)}, bf16[4,96,7...) custom-call(s32[1]{0:T(128)} %bitcast.13.me_ref, ...), custom_call_target="tpu_custom_call" | custom-call | flops 14495514624 | bytes 31457280 | tf_op jit(solution)/shard_map/pallas_call | solution.py:241
  118.6 1.0 collective-permute-done.18
  119.7 2.4 collective-permute-start.19
  122.8 1.8 collective-permute-start.26
  125.6 10.4 %collective-permute-done.19 = bf16[4,96,768]{2,1,0:T(8,128)(2,1)S(1)} collective-permute-done((bf16[4,96,768]{2,1,0:T(8,128)(2,1)S(1)}, bf16[4,96,768]{2,1,0:T(8,128)(2,1)S(1)}, u32[]{:S(2)}, u32[]{:S(2)}) %collective-permute-start.19) | collective-permute-done | bytes 589856 | tf_op jit(solution)/shard_map/ppermute | solution.py:273
  136.0 1.7 collective-permute-start.16
  137.7 1.0 add_convert_fusion.8
  138.8 1.7 collective-permute-start.20
  141.1 1.0 add_convert_fusion.1
  143.5 1.2 fusion.37
  146.1 6.4 %collective-permute-done.16 = bf16[4,96,768]{2,1,0:T(8,128)(2,1)} collective-permute-done((bf16[4,96,768]{2,1,0:T(8,128)(2,1)}, bf16[4,96,768]{2,1,0:T(8,128)(2,1)}, u32[]{:S(2)}, u32[]{:S(2)}) %collective-permute-start.16) | collective-permute-done | bytes 589856 | tf_op jit(solution)/shard_map/ppermute | solution.py:273
  152.5 2.8 collective-permute-done.20
  155.4 1.7 add_convert_fusion.7
  157.1 9.1 %collective-permute-done.23 = bf16[4,96,768]{2,1,0:T(8,128)(2,1)} collective-permute-done((bf16[4,96,768]{2,1,0:T(8,128)(2,1)S(1)}, bf16[4,96,768]{2,1,0:T(8,128)(2,1)}, u32[]{:S(2)}, u32[]{:S(2)}) %collective-permute-start.23) | collective-permute-done | bytes 589856 | tf_op jit(solution)/shard_map/ppermute | solution.py:273
  166.2 1.7 add_convert_fusion
  167.9 1.1 pad_maximum_fusion
  172.9 1.8 fusion.24
  177.6 51.5 %shard_map.254 = (f32[512,768]{1,0:T(8,128)S(1)}, f32[512,768]{1,0:T(8,128)}, bf16[4,4,192,768]{3,2,1,0:T(8,128)(2,1)}, f32[4,1,768]{2,1,0:T(1,128)S(1)}) custom-call(bf16[512,768]{1,0:T(8,128)(2,1)S(1)} %copy.89.na_ref, bf16[768,512]{1,0:T(8,128)(2,1)S(1)} %bitcast.41, bf16[512,768]{1,0:T(8,128)(2,1)S(1)} %copy-done.3, bf16[768,512]{1,0:T(8,128)(2,1)S(1)} %bitcast.43, ...), custom_call_target="tpu_custom_call" | custom-call | flops 12079595520 | bytes 20971520 | tf_op jit(solution)/shard_map/pallas_call | solution.py:161
  229.0 1.1 copy-done.5
  230.5 1.8 collective-permute-start.28
  232.5 3.2 copy.97
  235.8 3.2 copy.94
  239.1 1.1 slice_bitcast_fusion
  241.0 1.6 copy.96
  243.8 3.9 %fusion.35 = (f32[512]{0:T(512)S(1)}, f32[512]{0:T(512)S(1)}, bf16[768]{0:T(1024)(128)(2,1)S(1)}, bf16[768]{0:T(1024)(128)(2,1)S(1)}, f32[512,768]{0,1:T(8,128)}) fusion(f32[512]{0:T(512)S(1)} %add_rsqrt_fusion, f32[512]{0:T(512)S(1)} %broadcast_multiply_fusion.2, bf16[512,768]{0,1:T(8,128)(2,1)S(1)} %copy-done.12, f32[512,768]{0,1:T(8,128)} %copy.97, ...), kind=kLoop, calls=%fused_computation.88 | loop fusion | flops 5109248 | bytes 5522432 | tf_op jit(solution)/shard_map/reduce_sum | solution.py:391
  247.9 82.6 %all-gather.2 = bf16[32,1,9216]{2,1,0:T(2,128)(2,1)S(1)} all-gather(bf16[1,1,9216]{2,1,0:T(2,128)(2,1)S(1)} %bitcast.63), channel_id=1, replica_groups=mesh['dp'=2,'row'=4,'col'=4] {'dp','row','col'}, dimensions={0}, use_global_device_ids=true | all-gather | bytes 608256 | tf_op jit(solution)/shard_map/all_gather | solution.py:407
  330.5 1.3 convert_reduce_fusion.1
  333.7 1.6 copy.93
  335.3 1.8 reshape.294
  337.2 3.1 fusion.16
  340.3 1.2 copy.102
  341.5 1.2 copy.103
  342.6 18.7 %all-reduce.3.cloned.1.call-done = bf16[192,3,256]{2,1,0:T(4,128)(2,1)} async-done(((bf16[192,3,256]{2,1,0:T(4,128)(2,1)}), bf16[192,3,256]{2,1,0:T(4,128)(2,1)}) %all-reduce.3.cloned.1.call-update) | async-done | bytes 294928 | tf_op jit(solution)/shard_map/psum | solution.py:366
  361.3 1.1 slice.88
  362.7 1.0 copy.104
  (179 shorter events, 26.3 us)
Async XLA Ops:
  8.0 26.0 %copy-start.24 = (bf16[192,768]{1,0:T(8,128)(2,1)S(1)}, bf16[192,768]{1,0:T(8,128)(2,1)}, u32[]{:S(2)}) copy-start(bf16[192,768]{1,0:T(8,128)(2,1)} %param.25) | copy-start | bytes 884740
  8.0 166.7 %all-gather.5.cloned.1.call-start = ((), (), s32[]{:S(2)}) async-start(), calls=%async_computation.2 | async-start | bytes 5013504 | tf_op jit(solution)/shard_map/all_gather | solution.py:337
  10.2 70.6 %copy-start.17 = (bf16[512,768]{1,0:T(8,128)(2,1)S(1)}, bf16[512,768]{1,0:T(8,128)(2,1)}, u32[]{:S(2)}) copy-start(bf16[512,768]{1,0:T(8,128)(2,1)} %param.15) | copy-start | bytes 2359300
  11.1 219.4 %reduce-scatter.5.cloned.1.call-start = ((), (), s32[]{:S(2)}) async-start(), calls=%async_computation.5 | async-start | bytes 1474560 | tf_op jit(solution)/shard_map/reduce_scatter | solution.py:374
  32.5 48.8 %copy-start.19 = (bf16[384,768]{1,0:T(8,128)(2,1)}, bf16[384,768]{1,0:T(8,128)(2,1)S(1)}, u32[]{:S(2)}) copy-start(bf16[384,768]{1,0:T(8,128)(2,1)S(1)} %all-gather.1) | copy-start | bytes 1769476
  32.5 22.8 %collective-permute-start.10 = (bf16[4,96,768]{2,1,0:T(8,128)(2,1)S(1)}, bf16[4,96,768]{2,1,0:T(8,128)(2,1)}, u32[]{:S(2)}, u32[]{:S(2)}) collective-permute-start(bf16[4,96,768]{2,1,0:T(8,128)(2,1)S(1)} %bitcast.52), channel_id=1, source_target_pairs={{0,8},{4,12},{8,0},{12,4},{1,9},{5,13},{9,1},{13,5},{2,10},{6,14},... | collective-permute-start | bytes 1769480 | tf_op jit(solution)/shard_map/ppermute | solution.py:273
  51.6 35.9 %copy-start.20 = (bf16[384,768]{1,0:T(8,128)(2,1)}, bf16[384,768]{1,0:T(8,128)(2,1)S(1)}, u32[]{:S(2)}) copy-start(bf16[384,768]{1,0:T(8,128)(2,1)S(1)} %all-gather) | copy-start | bytes 1769476
  51.6 36.0 %copy-start.25 = (f32[768]{0:T(1024)S(1)}, f32[768]{0:T(1024)}, u32[]{:S(2)}) copy-start(f32[768]{0:T(1024)} %param.19) | copy-start | bytes 9220
  51.6 36.0 %copy-start.26 = (f32[768]{0:T(1024)S(1)}, f32[768]{0:T(1024)}, u32[]{:S(2)}) copy-start(f32[768]{0:T(1024)} %param.17) | copy-start | bytes 9220
  51.6 36.0 %copy-start.29 = (f32[768]{0:T(1024)S(1)}, f32[768]{0:T(1024)}, u32[]{:S(2)}) copy-start(f32[768]{0:T(1024)} %param.20) | copy-start | bytes 9220
  51.6 36.0 %copy-start.30 = (f32[768]{0:T(1024)S(1)}, f32[768]{0:T(1024)}, u32[]{:S(2)}) copy-start(f32[768]{0:T(1024)} %param.18) | copy-start | bytes 9220
  51.6 16.4 %collective-permute-start = (bf16[4,96,768]{2,1,0:T(8,128)(2,1)S(1)}, bf16[4,96,768]{2,1,0:T(8,128)(2,1)}, u32[]{:S(2)}, u32[]{:S(2)}) collective-permute-start(bf16[4,96,768]{2,1,0:T(8,128)(2,1)S(1)} %bitcast.56), channel_id=1, source_target_pairs={{0,16},{16,0},{1,17},{17,1},{2,18},{18,2},{3,19},{19,3},{4,20},{20... | collective-permute-start | bytes 1769480 | tf_op jit(solution)/shard_map/ppermute | solution.py:273
  53.1 20.0 %collective-permute-start.3 = (bf16[4,96,768]{2,1,0:T(8,128)(2,1)S(1)}, bf16[4,96,768]{2,1,0:T(8,128)(2,1)S(1)}, u32[]{:S(2)}, u32[]{:S(2)}) collective-permute-start(bf16[4,96,768]{2,1,0:T(8,128)(2,1)S(1)} %bitcast.57), channel_id=1, source_target_pairs={{0,8},{4,12},{8,0},{12,4},{1,9},{5,13},{9,1},{13,5},{2,10},{6,14},... | collective-permute-start | bytes 1769480 | tf_op jit(solution)/shard_map/ppermute | solution.py:273
  54.7 25.2 %collective-permute-start.7 = (bf16[4,96,768]{2,1,0:T(8,128)(2,1)S(1)}, bf16[4,96,768]{2,1,0:T(8,128)(2,1)S(1)}, u32[]{:S(2)}, u32[]{:S(2)}) collective-permute-start(bf16[4,96,768]{2,1,0:T(8,128)(2,1)S(1)} %bitcast.53), channel_id=1, source_target_pairs={{0,16},{16,0},{1,17},{17,1},{2,18},{18,2},{3,19},{19,3},{4,20},{20... | collective-permute-start | bytes 1769480 | tf_op jit(solution)/shard_map/ppermute | solution.py:273
  55.3 26.0 %collective-permute-start.1 = (bf16[4,96,768]{2,1,0:T(8,128)(2,1)S(1)}, bf16[4,96,768]{2,1,0:T(8,128)(2,1)}, u32[]{:S(2)}, u32[]{:S(2)}) collective-permute-start(bf16[4,96,768]{2,1,0:T(8,128)(2,1)S(1)} %bitcast.58), channel_id=1, source_target_pairs={{0,4},{4,0},{8,12},{12,8},{1,5},{5,1},{9,13},{13,9},{2,6},{6,2},{1... | collective-permute-start | bytes 1769480 | tf_op jit(solution)/shard_map/ppermute | solution.py:273
  55.3 26.6 %collective-permute-start.8 = (bf16[4,96,768]{2,1,0:T(8,128)(2,1)S(1)}, bf16[4,96,768]{2,1,0:T(8,128)(2,1)}, u32[]{:S(2)}, u32[]{:S(2)}) collective-permute-start(bf16[4,96,768]{2,1,0:T(8,128)(2,1)S(1)} %bitcast.54), channel_id=1, source_target_pairs={{0,4},{4,0},{8,12},{12,8},{1,5},{5,1},{9,13},{13,9},{2,6},{6,2},{1... | collective-permute-start | bytes 1769480 | tf_op jit(solution)/shard_map/ppermute | solution.py:273
  68.1 18.3 %collective-permute-start.11 = (bf16[4,96,768]{2,1,0:T(8,128)(2,1)}, bf16[4,96,768]{2,1,0:T(8,128)(2,1)}, u32[]{:S(2)}, u32[]{:S(2)}) collective-permute-start(bf16[4,96,768]{2,1,0:T(8,128)(2,1)} %collective-permute-done.10.rest_12_), channel_id=1, source_target_pairs={{0,16},{16,0},{1,17},{17,1},{2,18},{18,2},{3,19},{19,3},{4,20},{20... | collective-permute-start | bytes 1769480 | tf_op jit(solution)/shard_map/ppermute | solution.py:273
  73.1 6.9 %copy-start.33 = (bf16[4,96,768]{2,1,0:T(8,128)(2,1)}, bf16[4,96,768]{2,1,0:T(8,128)(2,1)S(1)}, u32[]{:S(2)}) copy-start(bf16[4,96,768]{2,1,0:T(8,128)(2,1)S(1)} %collective-permute-done.3.rest_4_) | copy-start | bytes 1769476
  73.1 13.7 %collective-permute-start.4 = (bf16[4,96,768]{2,1,0:T(8,128)(2,1)}, bf16[4,96,768]{2,1,0:T(8,128)(2,1)}, u32[]{:S(2)}, u32[]{:S(2)}) collective-permute-start(bf16[4,96,768]{2,1,0:T(8,128)(2,1)} %collective-permute-done.rest_1_), channel_id=1, source_target_pairs={{0,8},{4,12},{8,0},{12,4},{1,9},{5,13},{9,1},{13,5},{2,10},{6,14},... | collective-permute-start | bytes 1769480 | tf_op jit(solution)/shard_map/ppermute | solution.py:273
  80.8 6.1 %collective-permute-start.12 = (bf16[4,96,768]{2,1,0:T(8,128)(2,1)}, bf16[4,96,768]{2,1,0:T(8,128)(2,1)}, u32[]{:S(2)}, u32[]{:S(2)}) collective-permute-start(bf16[4,96,768]{2,1,0:T(8,128)(2,1)} %collective-permute-done.10.rest_12_), channel_id=1, source_target_pairs={{0,4},{4,0},{8,12},{12,8},{1,5},{5,1},{9,13},{13,9},{2,6},{6,2},{1... | collective-permute-start | bytes 1769480 | tf_op jit(solution)/shard_map/ppermute | solution.py:273
  81.1 7.0 %copy-start.11 = (bf16[512,768]{0,1:T(8,128)(2,1)}, bf16[512,768]{0,1:T(8,128)(2,1)S(1)}, u32[]{:S(2)}) copy-start(bf16[512,768]{0,1:T(8,128)(2,1)S(1)} %copy.85) | copy-start | bytes 2359300
  81.3 9.2 %collective-permute-start.2 = (bf16[4,96,768]{2,1,0:T(8,128)(2,1)}, bf16[4,96,768]{2,1,0:T(8,128)(2,1)}, u32[]{:S(2)}, u32[]{:S(2)}) collective-permute-start(bf16[4,96,768]{2,1,0:T(8,128)(2,1)} %collective-permute-done.rest_1_), channel_id=1, source_target_pairs={{0,4},{4,0},{8,12},{12,8},{1,5},{5,1},{9,13},{13,9},{2,6},{6,2},{1... | collective-permute-start | bytes 1769480 | tf_op jit(solution)/shard_map/ppermute | solution.py:273
  81.9 8.6 %collective-permute-start.5 = (bf16[4,96,768]{2,1,0:T(8,128)(2,1)}, bf16[4,96,768]{2,1,0:T(8,128)(2,1)}, u32[]{:S(2)}, u32[]{:S(2)}) collective-permute-start(bf16[4,96,768]{2,1,0:T(8,128)(2,1)} %copy-done.33), channel_id=1, source_target_pairs={{0,4},{4,0},{8,12},{12,8},{1,5},{5,1},{9,13},{13,9},{2,6},{6,2},{1... | collective-permute-start | bytes 1769480 | tf_op jit(solution)/shard_map/ppermute | solution.py:273
  86.4 4.1 %collective-permute-start.9 = (bf16[4,96,768]{2,1,0:T(8,128)(2,1)}, bf16[4,96,768]{2,1,0:T(8,128)(2,1)}, u32[]{:S(2)}, u32[]{:S(2)}) collective-permute-start(bf16[4,96,768]{2,1,0:T(8,128)(2,1)} %copy-done.34), channel_id=1, source_target_pairs={{0,4},{4,0},{8,12},{12,8},{1,5},{5,1},{9,13},{13,9},{2,6},{6,2},{1... | collective-permute-start | bytes 1769480 | tf_op jit(solution)/shard_map/ppermute | solution.py:273
  86.8 3.8 %collective-permute-start.13 = (bf16[4,96,768]{2,1,0:T(8,128)(2,1)}, bf16[4,96,768]{2,1,0:T(8,128)(2,1)}, u32[]{:S(2)}, u32[]{:S(2)}) collective-permute-start(bf16[4,96,768]{2,1,0:T(8,128)(2,1)} %collective-permute-done.11.rest_13_), channel_id=1, source_target_pairs={{0,4},{4,0},{8,12},{12,8},{1,5},{5,1},{9,13},{13,9},{2,6},{6,2},{1... | collective-permute-start | bytes 1769480 | tf_op jit(solution)/shard_map/ppermute | solution.py:273
  86.9 3.6 collective-permute-start.6
  117.5 5.2 %copy-start.18 = (bf16[4,96,768]{2,1,0:T(8,128)(2,1)S(1)}, bf16[4,96,768]{2,1,0:T(8,128)(2,1)}, u32[]{:S(2)}) copy-start(bf16[4,96,768]{2,1,0:T(8,128)(2,1)} %get-tuple-element.58) | copy-start | bytes 1769476
  117.5 2.1 collective-permute-start.18
  117.7 4.5 %collective-permute-start.25 = (bf16[4,96,768]{2,1,0:T(8,128)(2,1)}, bf16[4,96,768]{2,1,0:T(8,128)(2,1)S(1)}, u32[]{:S(2)}, u32[]{:S(2)}) collective-permute-start(bf16[4,96,768]{2,1,0:T(8,128)(2,1)} %get-tuple-element.59), channel_id=1, source_target_pairs={{0,4},{4,0},{8,12},{12,8},{1,5},{5,1},{9,13},{13,9},{2,6},{6,2},{1... | collective-permute-start | bytes 1769480 | tf_op jit(solution)/shard_map/ppermute | solution.py:273
  118.1 4.8 %collective-permute-start.15 = (bf16[4,96,768]{2,1,0:T(8,128)(2,1)S(1)}, bf16[4,96,768]{2,1,0:T(8,128)(2,1)S(1)}, u32[]{:S(2)}, u32[]{:S(2)}) collective-permute-start(bf16[4,96,768]{2,1,0:T(8,128)(2,1)S(1)} %get-tuple-element.47), channel_id=1, source_target_pairs={{0,4},{4,0},{8,12},{12,8},{1,5},{5,1},{9,13},{13,9},{2,6},{6,2},{1... | collective-permute-start | bytes 1769480 | tf_op jit(solution)/shard_map/ppermute | solution.py:273
  118.2 7.4 %collective-permute-start.17 = (bf16[4,96,768]{2,1,0:T(8,128)(2,1)S(1)}, bf16[4,96,768]{2,1,0:T(8,128)(2,1)S(1)}, u32[]{:S(2)}, u32[]{:S(2)}) collective-permute-start(bf16[4,96,768]{2,1,0:T(8,128)(2,1)S(1)} %get-tuple-element.49), channel_id=1, source_target_pairs={{0,4},{4,0},{8,12},{12,8},{1,5},{5,1},{9,13},{13,9},{2,6},{6,2},{1... | collective-permute-start | bytes 1769480 | tf_op jit(solution)/shard_map/ppermute | solution.py:273
  119.7 16.3 %collective-permute-start.19 = (bf16[4,96,768]{2,1,0:T(8,128)(2,1)S(1)}, bf16[4,96,768]{2,1,0:T(8,128)(2,1)S(1)}, u32[]{:S(2)}, u32[]{:S(2)}) collective-permute-start(bf16[4,96,768]{2,1,0:T(8,128)(2,1)S(1)} %add_convert_fusion.9), channel_id=1, source_target_pairs={{0,8},{4,12},{8,0},{12,4},{1,9},{5,13},{9,1},{13,5},{2,10},{6,14},... | collective-permute-start | bytes 1769480 | tf_op jit(solution)/shard_map/ppermute | solution.py:273
  122.2 18.5 %collective-permute-start.24 = (bf16[4,96,768]{2,1,0:T(8,128)(2,1)S(1)}, bf16[4,96,768]{2,1,0:T(8,128)(2,1)S(1)}, u32[]{:S(2)}, u32[]{:S(2)}) collective-permute-start(bf16[4,96,768]{2,1,0:T(8,128)(2,1)S(1)} %copy-done.35), channel_id=1, source_target_pairs={{0,4},{4,0},{8,12},{12,8},{1,5},{5,1},{9,13},{13,9},{2,6},{6,2},{1... | collective-permute-start | bytes 1769480 | tf_op jit(solution)/shard_map/ppermute | solution.py:273
  122.2 16.5 %collective-permute-start.22 = (bf16[4,96,768]{2,1,0:T(8,128)(2,1)S(1)}, bf16[4,96,768]{2,1,0:T(8,128)(2,1)S(1)}, u32[]{:S(2)}, u32[]{:S(2)}) collective-permute-start(bf16[4,96,768]{2,1,0:T(8,128)(2,1)S(1)} %copy-done.36), channel_id=1, source_target_pairs={{0,4},{4,0},{8,12},{12,8},{1,5},{5,1},{9,13},{13,9},{2,6},{6,2},{1... | collective-permute-start | bytes 1769480 | tf_op jit(solution)/shard_map/ppermute | solution.py:273
  122.8 17.9 %collective-permute-start.26 = (bf16[4,96,768]{2,1,0:T(8,128)(2,1)S(1)}, bf16[4,96,768]{2,1,0:T(8,128)(2,1)S(1)}, u32[]{:S(2)}, u32[]{:S(2)}) collective-permute-start(bf16[4,96,768]{2,1,0:T(8,128)(2,1)S(1)} %add_convert_fusion.2), channel_id=1, source_target_pairs={{0,16},{16,0},{1,17},{17,1},{2,18},{18,2},{3,19},{19,3},{4,20},{20... | collective-permute-start | bytes 1769480 | tf_op jit(solution)/shard_map/ppermute | solution.py:273
  125.6 16.5 %collective-permute-start.14 = (bf16[4,96,768]{2,1,0:T(8,128)(2,1)S(1)}, bf16[4,96,768]{2,1,0:T(8,128)(2,1)S(1)}, u32[]{:S(2)}, u32[]{:S(2)}) collective-permute-start(bf16[4,96,768]{2,1,0:T(8,128)(2,1)S(1)} %get-tuple-element.45), channel_id=1, source_target_pairs={{0,4},{4,0},{8,12},{12,8},{1,5},{5,1},{9,13},{13,9},{2,6},{6,2},{1... | collective-permute-start | bytes 1769480 | tf_op jit(solution)/shard_map/ppermute | solution.py:273
  136.0 16.5 %collective-permute-start.16 = (bf16[4,96,768]{2,1,0:T(8,128)(2,1)}, bf16[4,96,768]{2,1,0:T(8,128)(2,1)}, u32[]{:S(2)}, u32[]{:S(2)}) collective-permute-start(bf16[4,96,768]{2,1,0:T(8,128)(2,1)} %add_convert_fusion.12), channel_id=1, source_target_pairs={{0,8},{4,12},{8,0},{12,4},{1,9},{5,13},{9,1},{13,5},{2,10},{6,14},... | collective-permute-start | bytes 1769480 | tf_op jit(solution)/shard_map/ppermute | solution.py:273
  138.8 16.6 %collective-permute-start.20 = (bf16[4,96,768]{2,1,0:T(8,128)(2,1)}, bf16[4,96,768]{2,1,0:T(8,128)(2,1)}, u32[]{:S(2)}, u32[]{:S(2)}) collective-permute-start(bf16[4,96,768]{2,1,0:T(8,128)(2,1)} %add_convert_fusion.8), channel_id=1, source_target_pairs={{0,16},{16,0},{1,17},{17,1},{2,18},{18,2},{3,19},{19,3},{4,20},{20... | collective-permute-start | bytes 1769480 | tf_op jit(solution)/shard_map/ppermute | solution.py:273
  140.7 16.4 %collective-permute-start.21 = (bf16[4,96,768]{2,1,0:T(8,128)(2,1)}, bf16[4,96,768]{2,1,0:T(8,128)(2,1)}, u32[]{:S(2)}, u32[]{:S(2)}) collective-permute-start(bf16[4,96,768]{2,1,0:T(8,128)(2,1)} %get-tuple-element.53), channel_id=1, source_target_pairs={{0,4},{4,0},{8,12},{12,8},{1,5},{5,1},{9,13},{13,9},{2,6},{6,2},{1... | collective-permute-start | bytes 1769480 | tf_op jit(solution)/shard_map/ppermute | solution.py:273
  140.8 25.5 %collective-permute-start.23 = (bf16[4,96,768]{2,1,0:T(8,128)(2,1)S(1)}, bf16[4,96,768]{2,1,0:T(8,128)(2,1)}, u32[]{:S(2)}, u32[]{:S(2)}) collective-permute-start(bf16[4,96,768]{2,1,0:T(8,128)(2,1)S(1)} %add_convert_fusion.5), channel_id=1, source_target_pairs={{0,16},{16,0},{1,17},{17,1},{2,18},{18,2},{3,19},{19,3},{4,20},{20... | collective-permute-start | bytes 1769480 | tf_op jit(solution)/shard_map/ppermute | solution.py:273
  143.0 23.2 %collective-permute-start.27 = (bf16[4,96,768]{2,1,0:T(8,128)(2,1)}, bf16[4,96,768]{2,1,0:T(8,128)(2,1)}, u32[]{:S(2)}, u32[]{:S(2)}) collective-permute-start(bf16[4,96,768]{2,1,0:T(8,128)(2,1)} %add_convert_fusion.1), channel_id=1, source_target_pairs={{0,8},{4,12},{8,0},{12,4},{1,9},{5,13},{9,1},{13,5},{2,10},{6,14},... | collective-permute-start | bytes 1769480 | tf_op jit(solution)/shard_map/ppermute | solution.py:273
  169.1 5.6 %copy-start.3 = (bf16[512,768]{1,0:T(8,128)(2,1)S(1)}, bf16[512,768]{1,0:T(8,128)(2,1)}, u32[]{:S(2)}) copy-start(bf16[512,768]{1,0:T(8,128)(2,1)} %cot_ref.3) | copy-start | bytes 2359300
  169.1 5.6 %copy-start.4 = (bf16[512,768]{0,1:T(8,128)(2,1)S(1)}, bf16[512,768]{0,1:T(8,128)(2,1)}, u32[]{:S(2)}) copy-start(bf16[512,768]{0,1:T(8,128)(2,1)} %copy.86) | copy-start | bytes 2359300
  169.1 166.2 %reduce-scatter.3.cloned.1.call-start = ((), (), s32[]{:S(2)}) async-start(), calls=%async_computation.3 | async-start | bytes 5013504 | tf_op jit(solution)/shard_map/reduce_scatter | solution.py:363
  230.2 131.1 %all-reduce.3.cloned.1.call-start = ((), (), s32[]{:S(2)}) async-start(), calls=%async_computation.4 | async-start | bytes 786432 | tf_op jit(solution)/shard_map/psum | solution.py:366
  230.5 8.5 %collective-permute-start.28 = (bf16[96,1536]{1,0:T(8,128)(2,1)}, bf16[96,1536]{1,0:T(8,128)(2,1)S(1)}, u32[]{:S(2)}, u32[]{:S(2)}) collective-permute-start(bf16[96,1536]{1,0:T(8,128)(2,1)} %reduce-scatter.5.cloned.1.call-done), channel_id=1, source_target_pairs={{0,16},{16,0},{1,17},{17,1},{2,18},{18,2},{3,19},{19,3},{4,20},{20... | collective-permute-start | bytes 884744 | tf_op jit(solution)/shard_map/ppermute | solution.py:273
  247.8 85.9 %copy-start.6 = (f32[512,768]{1,0:T(8,128)S(1)}, f32[512,768]{1,0:T(8,128)}, u32[]{:S(2)}) copy-start(f32[512,768]{1,0:T(8,128)} %copy-done.5) | copy-start | bytes 4718596
  333.7 31.1 %copy-start.27 = (f32[768]{0:T(1024)}, f32[768]{0:T(1024)S(1)}, u32[]{:S(2)}) copy-start(f32[768]{0:T(1024)S(1)} %get-tuple-element.164) | copy-start | bytes 9220
  (22 other events, 52.3 us)
Sparse Core Ops, SparseCore 0:
  11.8 69.4 all-gather.4
  337.3 23.9 all-reduce.2
Sparse Core Ops, SparseCore 1:
  169.2 28.1 reduce-scatter.4
  230.3 79.9 reduce-scatter.2

commit v2 on v1

v2 whole, which is shorter than its diff:
```python
import functools
import math

import jax
import jax.numpy as jnp
from jax import lax
from jax.experimental import pallas as pl
from jax.experimental.pallas import tpu as pltpu
from jax.sharding import PartitionSpec as P

HD = 64
ROT = 16
QKV = 3 * HD
HEAD = 4 * HD
EPSILON = 1e-05
ROPE_BASE = 10000.0
NEAR = 128
LONGEST = 256
F32 = jnp.float32
BF16 = jnp.bfloat16


def dot_nn(a, b):
    return lax.dot_general(a, b, (((1,), (0,)), ((), ())), preferred_element_type=F32)


def dot_nt(a, b):
    return lax.dot_general(a, b, (((1,), (1,)), ((), ())), preferred_element_type=F32)


def piece_order(order):
    firsts = [0]
    for bit in order[::-1]:
        firsts = firsts + [j | bit for j in firsts]
    return firsts


def assemble(me_ref, w_refs, w_scr, at_col):
    _, rows, cols = w_refs[0].shape
    for j, ref in enumerate(w_refs):
        at = pl.multiple_of((me_ref[0] ^ j) * rows, 16)
        w_scr[pl.ds(at, rows), at_col : at_col + cols] = ref[0]


def hand_out(me_ref, g_scr, at_col, keep_ref, send_ref, order, core_bit):
    _, _, rows, cols = keep_ref.shape
    for t, j in enumerate(piece_order(order)):
        for ref, piece in ((keep_ref, j), (send_ref, j | core_bit)):
            at = pl.multiple_of((me_ref[0] ^ piece) * rows, 16)
            ref[t, 0] = g_scr[pl.ds(at, rows), at_col : at_col + cols]


def normalize(x):
    center = x - jnp.mean(x, axis=1, keepdims=True)
    inv_std = lax.rsqrt(jnp.mean(center * center, axis=1, keepdims=True) + EPSILON)
    return center * inv_std, inv_std


def prep_kernel(
    x_ref, cot_ref, ga_ref, sa_ref, gm_ref, sm_ref, segc_ref, segr_ref, freq_ref, _up_in, _down_in,
    na_ref, naT_ref, nm_ref, nmT_ref, cotT_ref, keep_ref, ahead_ref, behind_ref, mask_ref, _up_out, _down_out,
):
    length = x_ref.shape[0]
    tile = 128

    @pl.loop(0, length // tile)
    def _(t):
        rows = pl.ds(pl.multiple_of(t * tile, tile), tile)
        normed, _ = normalize(x_ref[rows, :].astype(F32))
        na_ref[rows, :] = (normed * ga_ref[...] + sa_ref[...]).astype(BF16)
        nm_ref[rows, :] = (normed * gm_ref[...] + sm_ref[...]).astype(BF16)
        same = segc_ref[rows, :] == segr_ref[...]
        cols = lax.broadcasted_iota(jnp.int32, (tile, length), 1)
        ids = lax.broadcasted_iota(jnp.int32, (tile, length), 0) + t * tile
        mask_ref[rows, :] = jnp.where(same & (cols <= ids), 0.0, -jnp.inf)
        starts = jnp.min(jnp.where(same, cols, length).astype(F32), axis=1, keepdims=True)
        places = ids[:, :1].astype(F32) - starts
        angles = places * freq_ref[...]
        lane = lax.broadcasted_iota(jnp.int32, (tile, 2 * HD), 1) % HD
        cosine, sine = jnp.cos(angles), jnp.sin(angles)
        keep_ref[rows, :] = jnp.where(lane < ROT, cosine, 1.0)
        ahead_ref[rows, :] = jnp.where(lane < ROT // 2, -sine, 0.0)
        behind_ref[rows, :] = jnp.where((lane < ROT) & (lane >= ROT // 2), sine, 0.0)

    naT_ref[...] = na_ref[...].T
    nmT_ref[...] = nm_ref[...].T
    cotT_ref[...] = cot_ref[...].T


def full(*shape):
    return pl.BlockSpec(shape, lambda *_: (0,) * len(shape))


ANY = pl.BlockSpec(memory_space=pl.ANY)
SCALAR = pl.BlockSpec(memory_space=pltpu.SMEM)


def cost(us):
    return pl.CostEstimate(flops=int(us * 1.15e9), bytes_accessed=2**20, transcendentals=0)


def shaped(shape, dtype):
    return jax.ShapeDtypeStruct(shape, dtype)


def prep_part(tokens, cot, gains, seg_row, up0, down0):
    length, width = tokens.shape
    halves = ROT // 2
    step = (lax.iota(jnp.int32, 2 * HD) % HD % halves).astype(F32)
    freq = (ROPE_BASE ** (-(step * (2.0 / ROT))))[None, :]
    table = shaped((length, 2 * HD), F32)
    return pl.pallas_call(
        prep_kernel,
        grid=(1,),
        in_specs=[full(length, width)] * 2 + [full(1, width)] * 4
        + [full(length, 1), full(1, length), full(1, 2 * HD), ANY, ANY],
        out_specs=[full(length, width), full(width, length)] * 2 + [full(width, length)]
        + [full(length, 2 * HD)] * 3 + [full(length, length), ANY, ANY],
        out_shape=[shaped((length, width), BF16), shaped((width, length), BF16)] * 2
        + [shaped((width, length), BF16)] + [table] * 3 + [shaped((length, length), F32)]
        + [shaped(up0.shape, BF16), shaped(down0.shape, BF16)],
        input_output_aliases={9: 9, 10: 10},
        compiler_params=pltpu.CompilerParams(vmem_limit_bytes=48 * 2**20),
        cost_estimate=cost(6),
    )(tokens, cot, *gains, seg_row[:, None], seg_row[None, :], freq, up0, down0)


def attention_kernel(orders, core_bit, waits, me_ref, na_ref, naT_ref, cot_ref, cotT_ref, *rest):
    pieces = (len(rest) - 16 - waits) // 2
    left, right = rest[:pieces], rest[pieces : 2 * pieces]
    bias_ref, keep_ref, ahead_ref, behind_ref, mask_ref = rest[2 * pieces : 2 * pieces + 5]
    dqkv_ref, mix_ref, dbias_ref, lk_ref, ls_ref, rk_ref, rs_ref = rest[2 * pieces + 5 + waits : 2 * pieces + 12 + waits]
    w_scr, qkv_scr, dattn_scr, g_scr = rest[2 * pieces + 12 + waits : 2 * pieces + 16 + waits]
    length, width = na_ref.shape
    block_cols = w_scr.shape[1]
    heads = block_cols // HEAD
    assemble(me_ref, left, w_scr, 0)
    assemble(me_ref, right, w_scr, block_cols // 2)

    w_vo = jnp.concatenate([w_scr[:, i * HEAD + 2 * HD : (i + 1) * HEAD] for i in range(heads)], axis=1)
    qkv_scr[...] = dot_nn(na_ref[...], w_scr[...]) + bias_ref[0]
    dattn_scr[...] = dot_nn(cot_ref[...], w_vo).astype(BF16)

    low = lax.broadcasted_iota(jnp.int32, (length, 2 * HD), 1) < HD
    keep, ahead, behind = keep_ref[...], ahead_ref[...], behind_ref[...]
    none = jnp.zeros((length, 2 * HD), BF16)
    blocks = length // NEAR
    for i in range(heads):
        qk = qkv_scr[:, i * HEAD : i * HEAD + 2 * HD]
        qk = qk * keep + pltpu.roll(qk, 2 * HD - ROT // 2, 1) * ahead + pltpu.roll(qk, ROT // 2, 1) * behind
        q32 = jnp.where(low, qk * (1.0 / math.sqrt(HD)), 0.0)
        k32 = jnp.where(low, pltpu.roll(qk, HD, 1), 0.0)
        v32 = jnp.where(low, 0.0, pltpu.roll(qkv_scr[:, i * HEAD + 2 * HD : (i + 1) * HEAD], HD, 1))
        q0 = q32.astype(BF16)
        k0 = k32.astype(BF16)
        v1 = v32.astype(BF16)
        go = dattn_scr[:, i * 2 * HD : (i + 1) * 2 * HD]
        go1 = jnp.where(low, none, go)
        qT = q0.T[:HD]
        goT = go.T[HD:]
        dq_parts = []
        mix_parts = []
        dk_sum = [None] * blocks
        dv_sum = [None] * blocks
        for b in range(blocks):
            r0, r1 = b * NEAR, (b + 1) * NEAR
            lo = max(0, r0 - LONGEST)
            s = dot_nt(q0[r0:r1], k0[lo:r1]) + mask_ref[r0:r1, lo:r1]
            e = jnp.exp(s - jnp.max(s, axis=1, keepdims=True))
            p = e * (1.0 / jnp.sum(e, axis=1, keepdims=True))
            p_low = p.astype(BF16)
            mix = dot_nn(p_low, v1[lo:r1])
            mix_parts.append(mix.astype(BF16))
            dp = dot_nt(go1[r0:r1], v1[lo:r1])
            delta = jnp.sum(mix * go1[r0:r1].astype(F32), axis=1, keepdims=True)
            ds = (p * (dp - delta)).astype(BF16)
            dq_parts.append(dot_nn(ds, k0[lo:r1]))
            dkT = dot_nn(qT[:, r0:r1], ds)
            dvT = dot_nn(goT[:, r0:r1], p_low)
            for n in range(lo // NEAR, b + 1):
                at = n * NEAR - lo
                dk_one, dv_one = dkT[:, at : at + NEAR], dvT[:, at : at + NEAR]
                dk_sum[n] = dk_one if dk_sum[n] is None else dk_sum[n] + dk_one
                dv_sum[n] = dv_one if dv_sum[n] is None else dv_sum[n] + dv_one
        dvk = jnp.concatenate([jnp.concatenate(dv_sum, axis=1), jnp.concatenate(dk_sum, axis=1)], axis=0).T
        dqk = jnp.where(low, jnp.concatenate(dq_parts, axis=0) * (1.0 / math.sqrt(HD)), dvk)
        dqk = dqk * keep - pltpu.roll(dqk, 2 * HD - ROT // 2, 1) * ahead - pltpu.roll(dqk, ROT // 2, 1) * behind
        dqkv_ref[0, :, i * HEAD : i * HEAD + 2 * HD] = dqk.astype(BF16)
        dqkv_ref[0, :, i * HEAD + 2 * HD : (i + 1) * HEAD] = jnp.where(low, dvk, 0.0).astype(BF16)
        mix_ref[0, :, i * 2 * HD : (i + 1) * 2 * HD] = jnp.concatenate(mix_parts, axis=0)

    dqkv = dqkv_ref[0]
    mix = mix_ref[0]
    dbias_ref[0] = jnp.sum(dqkv.astype(F32), axis=0, keepdims=True)
    for i in range(heads):
        g_qk = dot_nn(naT_ref[...], dqkv[:, i * HEAD : i * HEAD + 2 * HD])
        g_vo = dot_nn(naT_ref[...], dqkv[:, i * HEAD + 2 * HD : (i + 1) * HEAD]) + dot_nn(
            cotT_ref[...], mix[:, i * 2 * HD : (i + 1) * 2 * HD]
        )
        g_scr[:, i * HEAD : (i + 1) * HEAD] = jnp.concatenate([g_qk, g_vo], axis=1).astype(BF16)
    hand_out(me_ref, g_scr, 0, lk_ref, ls_ref, orders[0], core_bit)
    hand_out(me_ref, g_scr, block_cols // 2, rk_ref, rs_ref, orders[1], core_bit)


def mlp_kernel(orders, core_bit, waits, me_ref, nm_ref, nmT_ref, cot_ref, cotT_ref, *rest):
    pieces = (len(rest) - 11 - waits) // 2
    left, right = rest[:pieces], rest[pieces : 2 * pieces]
    bias_ref = rest[2 * pieces]
    act_ref, dh_ref, dbias_ref, lk_ref, ls_ref, rk_ref, rs_ref = rest[2 * pieces + 1 + waits : 2 * pieces + 8 + waits]
    wu_scr, wd_scr, g_scr = rest[2 * pieces + 8 + waits : 2 * pieces + 11 + waits]
    length, width = nm_ref.shape
    tile = 256
    assemble(me_ref, left, wu_scr, 0)
    assemble(me_ref, right, wd_scr, 0)
    dbias_ref[0] = jnp.zeros_like(dbias_ref[0])

    @pl.loop(0, length // tile)
    def _(t):
        rows = pl.ds(pl.multiple_of(t * tile, tile), tile)
        hidden = dot_nn(nm_ref[rows, :], wu_scr[...]) + bias_ref[0]
        d_act = dot_nn(cot_ref[rows, :], wd_scr[...])
        gate = 0.5 * (1.0 + lax.erf(hidden * (1.0 / math.sqrt(2.0))))
        act_ref[0, rows, :] = (hidden * gate).astype(BF16)
        slope = gate + hidden * jnp.exp(-0.5 * hidden * hidden) * (1.0 / math.sqrt(2.0 * math.pi))
        dh = (d_act * slope).astype(BF16)
        dh_ref[0, rows, :] = dh
        dbias_ref[0] += jnp.sum(dh.astype(F32), axis=0, keepdims=True)

    sides = ((nmT_ref, dh_ref, lk_ref, ls_ref, orders[0]), (cotT_ref, act_ref, rk_ref, rs_ref, orders[1]))
    for lhs, rhs, keep, send, order in sides:

        @pl.loop(0, width // tile)
        def _(t):
            rows = pl.ds(pl.multiple_of(t * tile, tile), tile)
            g_scr[rows, :] = dot_nn(lhs[rows, :], rhs[0]).astype(BF16)

        hand_out(me_ref, g_scr, 0, keep, send, order, core_bit)


def block_part(kernel, k0, count, orders, core_bit, after, me, norm, norm_t, cot, cot_t, left, right, vectors, mid_cols,
               g_cols, scratch, us):
    length, width = norm.shape
    pieces = len(left)
    rows = left[0].shape[1]
    kept = pieces // 2
    cols = vectors[0].shape[-1]

    def piece_spec(array):
        return pl.BlockSpec((1,) + array.shape[1:], lambda s: (k0 + s, 0, 0))

    g_spec = pl.BlockSpec((kept, 1, rows, g_cols), lambda s: (0, s, 0, 0))
    return pl.pallas_call(
        functools.partial(kernel, orders, core_bit, len(after)),
        grid=(count,),
        in_specs=[SCALAR, full(length, width), full(width, length), full(length, width), full(width, length)]
        + [piece_spec(p) for p in left + right]
        + [pl.BlockSpec((1, 1, cols), lambda s: (k0 + s, 0, 0))]
        + [full(*v.shape) for v in vectors[1:]]
        + [ANY] * len(after),
        out_specs=[pl.BlockSpec((1, length, m), lambda s: (s, 0, 0)) for m in mid_cols]
        + [pl.BlockSpec((1, 1, cols), lambda s: (s, 0, 0))] + [g_spec] * 4,
        out_shape=[shaped((count, length, m), BF16) for m in mid_cols]
        + [shaped((count, 1, cols), F32)] + [shaped((kept, count, rows, g_cols), BF16)] * 4,
        scratch_shapes=scratch,
        compiler_params=pltpu.CompilerParams(vmem_limit_bytes=56 * 2**20),
        cost_estimate=cost(us * count),
    )(me, norm, norm_t, cot, cot_t, *left, *right, *vectors, *after)


def tail_kernel(first, last, pieces, waits, me_ref, *rest):
    attn_left, attn_right = rest[:pieces], rest[pieces : 2 * pieces]
    up, down = rest[2 * pieces : 3 * pieces], rest[3 * pieces : 4 * pieces]
    dqkv_ref, mix_ref, act_ref, dh_ref = rest[4 * pieces : 4 * pieces + 4]
    rest = rest[4 * pieces + 4 :]
    if not first:
        branch_in, dna_in, dnm_in = rest[:3]
        rest = rest[3:]
    if last:
        x_ref, cot_ref, ga_ref, gm_ref, bo_ref, bd_ref = rest[:6]
        rest = rest[6:]
    rest = rest[waits:]
    if last:
        block_ref, grad_ref, stats_ref = rest[:3]
        branch_ref, dna_ref, dnm_ref = rest[3:6]
        rest = rest[6:]
    else:
        branch_ref, dna_ref, dnm_ref = rest[:3]
        rest = rest[3:]
    wa_scr, wv_scr, wu_scr, wd_scr = rest
    length, width = branch_ref.shape
    block_cols = wa_scr.shape[1]
    step = pl.program_id(0)
    tile = 256

    @pl.when(step == 0)
    def _():
        if first:
            branch_ref[...] = jnp.zeros_like(branch_ref)
            dna_ref[...] = jnp.zeros_like(dna_ref)
            dnm_ref[...] = jnp.zeros_like(dnm_ref)
        else:
            branch_ref[...] = branch_in[...]
            dna_ref[...] = dna_in[...]
            dnm_ref[...] = dnm_in[...]

    assemble(me_ref, attn_left, wa_scr, 0)
    assemble(me_ref, attn_right, wa_scr, block_cols // 2)
    assemble(me_ref, up, wu_scr, 0)
    assemble(me_ref, down, wd_scr, 0)
    for i in range(block_cols // HEAD):
        wv_scr[:, i * 2 * HD : (i + 1) * 2 * HD] = wa_scr[:, i * HEAD + 2 * HD : (i + 1) * HEAD]

    @pl.loop(0, length // tile)
    def _(t):
        rows = pl.ds(pl.multiple_of(t * tile, tile), tile)
        branch_ref[rows, :] += dot_nt(mix_ref[0, rows, :], wv_scr[...]) + dot_nt(act_ref[0, rows, :], wd_scr[...])
        dna_ref[rows, :] += dot_nt(dqkv_ref[0, rows, :], wa_scr[...])
        dnm_ref[rows, :] += dot_nt(dh_ref[0, rows, :], wu_scr[...])

    if last:

        @pl.when(step == pl.num_programs(0) - 1)
        def _():
            stats_ref[...] = jnp.zeros_like(stats_ref)
            small = 128

            @pl.loop(0, length // small)
            def _(t):
                rows = pl.ds(pl.multiple_of(t * small, small), small)
                x = x_ref[rows, :].astype(F32)
                cot = cot_ref[rows, :].astype(F32)
                normed, inv_std = normalize(x)
                block_ref[rows, :] = (x + branch_ref[rows, :] + bo_ref[...] + bd_ref[...]).astype(BF16)
                dna, dnm = dna_ref[rows, :], dnm_ref[rows, :]
                d_normed = dna * ga_ref[...] + dnm * gm_ref[...]
                pulled = (
                    d_normed
                    - jnp.mean(d_normed, axis=1, keepdims=True)
                    - normed * jnp.mean(d_normed * normed, axis=1, keepdims=True)
                )
                grad_ref[rows, :] = (cot + inv_std * pulled).astype(BF16)
                for at, term in enumerate((cot, dna * normed, dna, dnm * normed, dnm)):
                    stats_ref[at : at + 1, :] += jnp.sum(term, axis=0, keepdims=True)


def tail_part(k0, count, after, me, weights, mids, sums, finals):
    length = mids[0].shape[1]
    pieces = len(weights[0])
    width = pieces * weights[0][0].shape[1]
    first, last = sums is None, finals is not None
    block_cols = mids[0].shape[2]
    up_cols = mids[2].shape[2]

    def piece_spec(array):
        return pl.BlockSpec((1,) + array.shape[1:], lambda s: (k0 + s, 0, 0))

    total = shaped((length, width), F32)
    out_specs, out_shape = [full(length, width)] * 3, [total] * 3
    scratch = [
        pltpu.VMEM((width, block_cols), BF16), pltpu.VMEM((width, block_cols // 2), BF16),
        pltpu.VMEM((width, up_cols), BF16), pltpu.VMEM((width, up_cols), BF16),
    ]
    if last:
        out_specs = [full(length, width)] * 2 + [full(8, width)]
        out_shape = [shaped((length, width), BF16)] * 2 + [shaped((8, width), F32)]
        scratch = [pltpu.VMEM((length, width), F32)] * 3 + scratch
    extra = ([] if first else list(sums)) + (list(finals) if last else [])
    return pl.pallas_call(
        functools.partial(tail_kernel, first, last, pieces, len(after)),
        grid=(count,),
        in_specs=[SCALAR] + [piece_spec(p) for group in weights for p in group]
        + [pl.BlockSpec((1, length, m.shape[2]), lambda s: (s, 0, 0)) for m in mids]
        + [full(*e.shape) for e in extra] + [ANY] * len(after),
        out_specs=out_specs,
        out_shape=out_shape,
        scratch_shapes=scratch,
        compiler_params=pltpu.CompilerParams(vmem_limit_bytes=56 * 2**20),
        cost_estimate=cost(4 * count),
    )(me, *[p for group in weights for p in group], *mids, *extra, *after)


def swap(value, bit):
    axis, flip = ("dp", 1) if bit == 1 else ("row", bit // 2)
    return flipped(value, axis, flip)


def flipped(value, axis, flip):
    return lax.ppermute(value, axis, [(i, i ^ flip) for i in range(lax.axis_size(axis))])


def shifted(value, by):
    size = lax.axis_size("col")
    return lax.ppermute(value, "col", [(i, (i + by) % size) for i in range(size)])


def gather_pieces(own, order):
    pieces = {0: own}
    for bit in order:
        for j in list(pieces):
            pieces[j ^ bit] = swap(pieces[j], bit)
    return [pieces[j] for j in range(len(pieces))]


def add(a, b):
    return (a.astype(F32) + b.astype(F32)).astype(BF16)


class Reduction:
    def __init__(self, keep, send, order, core_bit):
        self.keep, self.came, self.order = keep, swap(send, core_bit), list(order)
        self.steps = [self.came]
        for bit in self.order:
            half = self.keep.shape[0] // 2
            send = add(self.keep[half:], self.came[half:])
            self.keep = add(self.keep[:half], self.came[:half])
            self.came = swap(send, bit)
            self.steps.append(self.came)
        self.total = add(self.keep[0], self.came[0])


def all_sum(value):
    for axis in ("row", "dp", "col"):
        flip = 1
        while flip < lax.axis_size(axis):
            value = value + flipped(value, axis, flip)
            flip *= 2
    return value


def on_device(
    tokens_in,
    segment_ids,
    attn_gain,
    attn_shift,
    mlp_gain,
    mlp_shift,
    qkv_weight,
    qkv_bias,
    out_weight,
    out_bias,
    up_weight,
    up_bias,
    down_weight,
    down_bias,
    out_cotangent,
):
    row_size = lax.axis_size("row")
    col_size = lax.axis_size("col")
    length, width = tokens_in.shape
    rows = qkv_weight.shape[0]
    half_rows = rows // 2
    local_heads = qkv_weight.shape[1] // QKV
    block_cols = local_heads * HEAD
    up_cols = up_weight.shape[1]
    row_id = lax.axis_index("row")
    col_id = lax.axis_index("col")
    half = lax.axis_index("dp") % 2
    me = (row_id * 2 + half).reshape(1).astype(jnp.int32)
    row_bits = [2 << i for i in range(row_size.bit_length() - 1)]
    core_bit, far_bits = row_bits[0], row_bits[1:][::-1]
    orders = (far_bits + [1], [1] + far_bits)

    head_weight = jnp.concatenate(
        [qkv_weight.reshape(rows, local_heads, QKV), out_weight.T.reshape(rows, local_heads, HD)], axis=2
    ).reshape(rows, block_cols)
    attn_own = lax.dynamic_slice_in_dim(head_weight, half * half_rows, half_rows, axis=0)
    mlp_own = jnp.concatenate(
        [
            lax.dynamic_slice_in_dim(up_weight, half * half_rows, half_rows, axis=0),
            lax.dynamic_slice_in_dim(down_weight, half * half_rows, half_rows, axis=1).T,
        ],
        axis=1,
    )
    attn_all = jnp.stack([attn_own] + [shifted(attn_own, k) for k in range(1, col_size)])
    mlp_all = jnp.stack([mlp_own] + [shifted(mlp_own, k) for k in range(1, col_size)])
    cut = block_cols // 2
    attn_left = gather_pieces(attn_all[:, :, :cut], orders[0] + [core_bit])
    attn_right = gather_pieces(attn_all[:, :, cut:], orders[1] + [core_bit])

    seg_row = lax.dynamic_index_in_dim(segment_ids, row_id * col_size + col_id, axis=0, keepdims=False)
    na, na_t, nm, nm_t, cot_t, keep, ahead, behind, mask, up_own, down_own = prep_part(
        tokens_in, out_cotangent, [v[None, :] for v in (attn_gain, attn_shift, mlp_gain, mlp_shift)], seg_row,
        mlp_all[:, :, :up_cols], mlp_all[:, :, up_cols:],
    )
    up = gather_pieces(up_own, orders[0] + [core_bit])
    down = gather_pieces(down_own, orders[1] + [core_bit])

    blocks_here = (col_id - jnp.arange(col_size)) % col_size
    head_bias = jnp.pad(
        qkv_bias.reshape(col_size, local_heads, QKV), ((0, 0), (0, 0), (0, HEAD - QKV))
    ).reshape(col_size, 1, block_cols)
    head_bias = jnp.take(head_bias, blocks_here, axis=0)
    hidden_bias = jnp.take(up_bias.reshape(col_size, 1, up_cols), blocks_here, axis=0)

    per_call = 2 if col_size % 2 == 0 else 1
    attn_calls, mlp_calls, attn_sums, mlp_sums = [], [], [], []
    last = None
    for k0 in range(0, col_size, per_call):
        after = [] if last is None else [last, up[orders[0][0]], down[orders[1][0]]]
        outs = block_part(
            attention_kernel, k0, per_call, orders, core_bit, after, me, na, na_t, out_cotangent, cot_t,
            attn_left, attn_right, [head_bias, keep, ahead, behind, mask], [block_cols, block_cols // 2], cut,
            [
                pltpu.VMEM((width, block_cols), BF16), pltpu.VMEM((length, block_cols), F32),
                pltpu.VMEM((length, block_cols // 2), BF16), pltpu.VMEM((width, block_cols), BF16),
            ],
            11,
        )
        last = outs[2]
        attn_calls.append(outs[:3])
        attn_sums.append([
            Reduction(outs[3], outs[4], orders[0], core_bit), Reduction(outs[5], outs[6], orders[1], core_bit)
        ])
    for n, k0 in enumerate(range(0, col_size, per_call)):
        after = [last]
        if n == 0:
            after += [r.steps[0] for r in attn_sums[0]]
        else:
            after += [r.steps[0] for r in attn_sums[1]] + [r.steps[1] for r in attn_sums[0]]
        outs = block_part(
            mlp_kernel, k0, per_call, orders, core_bit, after, me, nm, nm_t, out_cotangent, cot_t,
            up, down, [hidden_bias], [up_cols, up_cols], up_cols,
            [
                pltpu.VMEM((width, up_cols), BF16), pltpu.VMEM((width, up_cols), BF16),
                pltpu.VMEM((width, up_cols), BF16),
            ],
            6,
        )
        last = outs[2]
        mlp_calls.append(outs[:3])
        mlp_sums.append([
            Reduction(outs[3], outs[4], orders[0], core_bit), Reduction(outs[5], outs[6], orders[1], core_bit)
        ])

    sums, weights = None, (attn_left, attn_right, up, down)
    for n, k0 in enumerate(range(0, col_size, per_call)):
        finals = None
        after = [last]
        if k0 + per_call == col_size:
            finals = (
                tokens_in, out_cotangent, attn_gain[None, :], mlp_gain[None, :], out_bias[None, :], down_bias[None, :]
            )
            after += [r.steps[0] for r in mlp_sums[-1]]
        mids = list(attn_calls[n][:2]) + list(mlp_calls[n][:2])
        sums = tail_part(k0, per_call, after, me, weights, mids, sums, finals)
    block_out, in_grad, stats = sums

    def settle(parts):
        total = None
        for n, pair in enumerate(parts):
            both = jnp.concatenate([r.total for r in pair], axis=2)
            for i in range(per_call):
                k = n * per_call + i
                term = (both[i] if k == 0 else shifted(both[i], -k)).astype(F32)
                total = term if total is None else total + term
        flip = 2
        while flip < lax.axis_size("dp"):
            total = total + flipped(total, "dp", flip)
            flip *= 2
        mine = total.astype(BF16)
        other = swap(mine, 1)
        first = half == 0
        return jnp.concatenate([jnp.where(first, mine, other), jnp.where(first, other, mine)], axis=0).astype(F32)

    g_heads = settle(attn_sums).reshape(rows, local_heads, HEAD)
    g_mlp = settle(mlp_sums)

    d_bias_up = jnp.take(jnp.concatenate([c[2] for c in mlp_calls]), blocks_here, axis=0)
    d_bias_attn = jnp.take(jnp.concatenate([c[2] for c in attn_calls]), blocks_here, axis=0)
    smalls = jnp.concatenate(
        [
            stats[:5].reshape(-1),
            d_bias_up.reshape(-1),
            d_bias_attn.reshape(col_size * local_heads, HEAD)[:, :QKV].reshape(-1),
        ]
    )
    smalls = all_sum(smalls.reshape(-1, 128)).reshape(-1)
    stats = smalls[: 5 * width].reshape(5, width)
    grad_up_bias = smalls[5 * width : 5 * width + up_bias.shape[0]]
    grad_qkv_bias = smalls[5 * width + up_bias.shape[0] :]
    return (
        block_out,
        in_grad,
        stats[1],
        stats[2],
        stats[3],
        stats[4],
        g_heads[:, :, :QKV].reshape(rows, local_heads * QKV),
        grad_qkv_bias,
        g_heads[:, :, QKV:].reshape(rows, local_heads * HD).T,
        stats[0],
        g_mlp[:, :up_cols],
        grad_up_bias,
        g_mlp[:, up_cols:].T,
        stats[0],
    )


def solution(mesh):
    return jax.shard_map(
        on_device,
        mesh=mesh,
        in_specs=(
            P(("dp", "row", "col"), None),
            P("dp", None),
            P(),
            P(),
            P(),
            P(),
            P("row", "col"),
            P(),
            P("col", "row"),
            P(),
            P("row", "col"),
            P(),
            P("col", "row"),
            P(),
            P(("dp", "row", "col"), None),
        ),
        out_specs=(
            P(("dp", "row", "col"), None),
            P(("dp", "row", "col"), None),
            P(),
            P(),
            P(),
            P(),
            P("row", "col"),
            P(),
            P("col", "row"),
            P(),
            P("row", "col"),
            P(),
            P("col", "row"),
            P(),
        ),
        check_vma=False,
    )
```

time: 374 us -> 359 us (0.960)
  blocking collectives: 121 us -> 0 us
  starting transfers between devices: 21.2 us -> 70.6 us
  waiting for transfers between devices: 75.8 us -> 125 us
  Pallas kernels: 78.4 us -> 119 us
  between operations: 16.1 us -> 2.07 us
  local copies, waits for them, and re-layouts: 36.7 us -> 24.3 us
  other arithmetic: 23.2 us -> 14.1 us
    all_gather x3 -> x0, blocking collectives: 121 us -> none  [the longest x1 82.6 us: on_device(): lax.all_gather(smalls, ('dp', 'row', 'col'), axis=0, tiled=False)]
    ppermute x29 -> x71, waiting for transfers between devices: 57 us -> 125 us  [the longest x59 89.5 us: flipped(): lax.ppermute(value, axis, [(i, i ^ flip) for i in range(lax.axis_size(axi...]
    ppermute x29 -> x71, starting transfers between devices: 20.7 us -> 70.6 us  [the longest x59 46.3 us: flipped(): lax.ppermute(value, axis, [(i, i ^ flip) for i in range(lax.axis_size(axi...]
    pallas_call x2 -> x7, Pallas kernels: 78.4 us -> 119 us  [the longest x4 88.8 us: block_part(): pl.pallas_call(functools.partial(kernel, orders, core_bit, len(after)), g...]
    psum x1 -> x0, waiting for transfers between devices: 18.7 us -> none  [on_device(): g_attn = lax.psum(g_attn, 'dp').astype(F32)]
    pallas_call x4 -> x0, local copies, waits for them, and re-layouts: 9.58 us -> none  [the longest x2 6.34 us: mlp_part(): pl.pallas_call(functools.partial(mlp_kernel, pieces), grid=(col_size,), i...]
    reduce_sum x7 -> x0, other arithmetic: 6.13 us -> none  [the longest x1 3.93 us: on_device(): jnp.mean(d_normed, axis=1, keepdims=True)]
    convert_element_type x12 -> x28, other arithmetic: 10.7 us -> 9.62 us  [the longest x24 8.08 us: add(): return (a.astype(F32) + b.astype(F32)).astype(BF16)]
  transfers between devices with their start and end apart: 33 -> 71, of which waited for: 11 -> 22; matrix products, arithmetic and copies ran while one was open for 12% -> 6% of each run, Pallas kernels for 21% -> 33%
where the time goes in v2:
time: 359 us; the launch traced here: 355 us
  waiting for transfers between devices  125 us (35%)
  Pallas kernels  119 us (33%)
  starting transfers between devices  70.6 us (20%)
  local copies, waits for them, and re-layouts  24.3 us (7%)
  other arithmetic  14.1 us (4%)
    ppermute x59, waiting for transfers between devices, flipped(): lax.ppermute(value, axis, [(i, i ^ flip) for i in range(lax.axis_size(axi...  89.5 us
    pallas_call x4, Pallas kernels, block_part(): pl.pallas_call(functools.partial(kernel, orders, core_bit, len(after)), g...  88.8 us
    ppermute x59, starting transfers between devices, flipped(): lax.ppermute(value, axis, [(i, i ^ flip) for i in range(lax.axis_size(axi...  46.3 us
    ppermute x12, waiting for transfers between devices, shifted(): lax.ppermute(value, 'col', [(i, (i + by) % size) for i in range(size)])  36 us
    pallas_call x2, Pallas kernels, tail_part(): pl.pallas_call(functools.partial(tail_kernel, first, last, pieces, len(af...  25.6 us
    ppermute x12, starting transfers between devices, shifted(): lax.ppermute(value, 'col', [(i, (i + by) % size) for i in range(size)])  24.3 us
    unnamed x152, local copies, waits for them, and re-layouts  13.5 us
    convert_element_type x24, other arithmetic, add(): return (a.astype(F32) + b.astype(F32)).astype(BF16)  8.08 us
  transfers between devices with their start and end apart: 71, of which 22 were waited for; matrix products, arithmetic and copies ran while one was open for 6% of the time, Pallas kernels for 33%

profile of v2, /device:TPU:0, one launch (start us, length us, event | category | flops | bytes accessed | tf_op | source)
XLA Modules:
  0.0 355.3 jit_solution(8717659780580277884)
XLA Ops:
  3.2 5.1 %collective-permute-start.2 = (bf16[96,768]{1,0:T(8,128)(2,1)S(1)}, bf16[96,768]{1,0:T(8,128)(2,1)S(1)}, u32[]{:S(2)}, u32[]{:S(2)}) collective-permute-start(bf16[96,768]{1,0:T(8,128)(2,1)S(1)} %copy.48), channel_id=1, source_target_pairs={{0,3},{1,0},{2,1},{3,2},{4,7},{5,4},{6,5},{7,6},{8,11},{9,8},{10,9... | collective-permute-start | bytes 442376 | tf_op jit(solution)/shard_map/ppermute | solution.py:393
  9.4 2.0 collective-permute-start.18
  17.1 2.4 collective-permute-start.19
  19.4 14.8 %collective-permute-done.1 = bf16[96,768]{1,0:T(8,128)(2,1)S(1)} collective-permute-done((bf16[96,768]{1,0:T(8,128)(2,1)S(1)}, bf16[96,768]{1,0:T(8,128)(2,1)S(1)}, u32[]{:S(2)}, u32[]{:S(2)}) %collective-permute-start.1) | collective-permute-done | bytes 147488 | tf_op jit(solution)/shard_map/ppermute | solution.py:393
  34.4 1.6 collective-permute-start.13
  36.0 4.5 %collective-permute-done.18 = bf16[96,1536]{1,0:T(8,128)(2,1)S(1)} collective-permute-done((bf16[96,1536]{1,0:T(8,128)(2,1)S(1)}, bf16[96,1536]{1,0:T(8,128)(2,1)S(1)}, u32[]{:S(2)}, u32[]{:S(2)}) %collective-permute-start.18) | collective-permute-done | bytes 294944 | tf_op jit(solution)/shard_map/ppermute | solution.py:393
  45.0 3.8 %collective-permute-done.10.rest_9_ = bf16[4,96,384]{2,1,0:T(8,128)(2,1)S(1)} collective-permute-done((bf16[4,96,384]{2,1,0:T(8,128)(2,1)S(1)}, bf16[4,96,384]{2,1,0:T(8,128)(2,1)S(1)}, u32[]{:S(2)}, u32[]{:S(2)}) %collective-permute-start.10) | collective-permute-done | bytes 294944 | tf_op jit(solution)/shard_map/ppermute | solution.py:388
  48.8 2.4 collective-permute-start.14
  51.2 2.2 collective-permute-start.7
  55.9 4.8 %collective-permute-done.7.rest_5_ = bf16[4,96,384]{2,1,0:T(8,128)(2,1)S(1)} collective-permute-done((bf16[4,96,384]{2,1,0:T(8,128)(2,1)S(1)}, bf16[4,96,384]{2,1,0:T(8,128)(2,1)S(1)}, u32[]{:S(2)}, u32[]{:S(2)}) %collective-permute-start.7) | collective-permute-done | bytes 294944 | tf_op jit(solution)/shard_map/ppermute | solution.py:388
  60.7 4.3 %shard_map.254 = (bf16[512,768]{1,0:T(8,128)(2,1)S(1)}, bf16[768,512]{1,0:T(8,128)(2,1)S(1)}, bf16[512,768]{1,0:T(8,128)(2,1)S(1)}, bf16[768,512]{1,0:T(8,128)(2...) custom-call(bf16[512,768]{1,0:T(8,128)(2,1)} %rest_39_.1, ...), custom_call_target="tpu_custom_call", output_to_operand_aliasing={{9}: (9, {}), {10}: (10, {})} | custom-call | flops 6899999744 | bytes 1048576 | tf_op jit(solution)/shard_map/pallas_call | solution.py:112
  71.7 1.6 collective-permute-start.23
  76.1 26.0 %shard_map.255 = (bf16[2,512,768]{2,1,0:T(8,128)(2,1)}, bf16[2,512,384]{2,1,0:T(8,128)(2,1)}, f32[2,1,768]{2,1,0:T(1,128)}, bf16[4,2,96,384]{3,2,1,0:T(8,128)(2,...) custom-call(s32[1]{0:T(128)} %bitcast.me_ref, ...), custom_call_target="tpu_custom_call" | custom-call | flops 25300000768 | bytes 1048576 | tf_op jit(solution)/shard_map/pallas_call | solution.py:252
  103.5 26.3 %shard_map.256 = (bf16[2,512,768]{2,1,0:T(8,128)(2,1)}, bf16[2,512,384]{2,1,0:T(8,128)(2,1)}, f32[2,1,768]{2,1,0:T(1,128)}, bf16[4,2,96,384]{3,2,1,0:T(8,128)(2,...) custom-call(s32[1]{0:T(128)} %bitcast.me_ref, ...), custom_call_target="tpu_custom_call" | custom-call | flops 25300000768 | bytes 1048576 | tf_op jit(solution)/shard_map/pallas_call | solution.py:252
  134.8 1.6 collective-permute-start.38
  136.5 1.6 collective-permute-start.39
  138.3 16.5 %collective-permute-done.38.rest_20_ = bf16[2,2,96,384]{3,2,1,0:T(8,128)(2,1)S(1)} collective-permute-done((bf16[2,2,96,384]{3,2,1,0:T(8,128)(2,1)S(1)}, bf16[2,2,96,384]{3,2,1,0:T(8,128)(2,1)S(1)}, u32[]{:S(2)}, u32[]{:S(2)}) %collective-permute-start.38) | collective-permute-done | bytes 294944 | tf_op jit(solution)/shard_map/ppermute | solution.py:388
  155.4 1.6 collective-permute-start.52
  157.0 6.1 %collective-permute-done.50 = bf16[2,2,96,384]{3,2,1,0:T(8,128)(2,1)S(1)} collective-permute-done((bf16[2,2,96,384]{3,2,1,0:T(8,128)(2,1)S(1)}, bf16[2,2,96,384]{3,2,1,0:T(8,128)(2,1)S(1)}, u32[]{:S(2)}, u32[]{:S(2)}) %collective-permute-start.50) | collective-permute-done | bytes 294944 | tf_op jit(solution)/shard_map/ppermute | solution.py:388
  167.3 2.9 collective-permute-done.47
  170.6 2.5 collective-permute-start.51
  173.2 11.2 %collective-permute-done.48 = bf16[1,2,96,384]{3,2,1,0:T(8,128)(2,1)S(1)} collective-permute-done((bf16[1,2,96,384]{3,2,1,0:T(8,128)(2,1)S(1)}, bf16[1,2,96,384]{3,2,1,0:T(8,128)(2,1)S(1)}, u32[]{:S(2)}, u32[]{:S(2)}) %collective-permute-start.48) | collective-permute-done | bytes 147488 | tf_op jit(solution)/shard_map/ppermute | solution.py:388
  187.0 2.4 collective-permute-done.53
  190.3 3.5 collective-permute-start.49
  193.9 2.7 collective-permute-start.54
  196.6 1.9 collective-permute-start.55
  199.5 23.2 %shard_map.257 = (bf16[2,512,768]{2,1,0:T(8,128)(2,1)}, bf16[2,512,768]{2,1,0:T(8,128)(2,1)}, f32[2,1,768]{2,1,0:T(1,128)}, bf16[4,2,96,768]{3,2,1,0:T(8,128)(2,...) custom-call(s32[1]{0:T(128)} %bitcast.me_ref, ...), custom_call_target="tpu_custom_call" | custom-call | flops 13799999488 | bytes 1048576 | tf_op jit(solution)/shard_map/pallas_call | solution.py:252
  222.7 13.3 %shard_map.258 = (bf16[2,512,768]{2,1,0:T(8,128)(2,1)}, bf16[2,512,768]{2,1,0:T(8,128)(2,1)}, f32[2,1,768]{2,1,0:T(1,128)}, bf16[4,2,96,768]{3,2,1,0:T(8,128)(2,...) custom-call(s32[1]{0:T(128)} %bitcast.me_ref, ...), custom_call_target="tpu_custom_call" | custom-call | flops 13799999488 | bytes 1048576 | tf_op jit(solution)/shard_map/pallas_call | solution.py:252
  236.6 11.5 %shard_map.259 = (f32[512,768]{1,0:T(8,128)}, f32[512,768]{1,0:T(8,128)}, f32[512,768]{1,0:T(8,128)}) custom-call(s32[1]{0:T(128)} %bitcast.me_ref, bf16[4,96,384]{2,1,0:T(8,128)(2,1)} %copy-done.30, bf16[4,96,384]{2,1,0:T(8,128)(2,1)} %copy-done.63, bf16[4,96,384]{2,1,0:T(8,128)(2,1)} %copy-done.62, bf16[4,96,384]{2,1,0:T(8,128)(2,1)} %copy-done.69, ...), custom_call_target="tpu_custom_call" | custom-call | flops 9200000000 | bytes 1048576 | tf_op jit(solution)/shard_map/pallas_call | solution.py:368
  249.4 1.6 collective-permute-start.56
  251.2 4.1 %collective-permute-done.56 = bf16[96,768]{1,0:T(8,128)(2,1)S(1)} collective-permute-done((bf16[96,768]{1,0:T(8,128)(2,1)S(1)}, bf16[96,768]{1,0:T(8,128)(2,1)S(1)}, u32[]{:S(2)}, u32[]{:S(2)}) %collective-permute-start.56) | collective-permute-done | bytes 147488 | tf_op jit(solution)/shard_map/ppermute | solution.py:388
  256.9 14.1 %shard_map.260 = (bf16[512,768]{1,0:T(8,128)(2,1)}, bf16[512,768]{1,0:T(8,128)(2,1)}, f32[8,768]{1,0:T(8,128)}) custom-call(s32[1]{0:T(128)} %bitcast.me_ref, bf16[4,96,384]{2,1,0:T(8,128)(2,1)} %copy-done.30, bf16[4,96,384]{2,1,0:T(8,128)(2,1)} %copy-done.63, bf16[4,96,384]{2,1,0:T(8,128)(2,1)} %copy-done.62, bf16[4,96,384]{2,1,0:T(8,128)(2,1)} %copy-done.69, ...), custom_call_target="tpu_custom_call" | custom-call | flops 9200000000 | bytes 1048576 | tf_op jit(solution)/shard_map/pallas_call | solution.py:368
  271.9 2.0 add_convert_fusion.7
  276.1 1.7 add_convert_fusion.5
  277.8 1.6 collective-permute-start.61
  279.4 11.1 %collective-permute-done.43 = f32[72,128]{1,0:T(8,128)S(1)} collective-permute-done((f32[72,128]{1,0:T(8,128)S(1)}, f32[72,128]{1,0:T(8,128)S(1)}, u32[]{:S(2)}, u32[]{:S(2)}) %collective-permute-start.43) | collective-permute-done | bytes 36896 | tf_op jit(solution)/shard_map/ppermute | solution.py:388
  290.5 1.6 collective-permute-start.44
  295.0 1.6 collective-permute-start.66
  296.6 1.9 collective-permute-done.45
  301.2 7.5 %collective-permute-done.64 = bf16[2,2,96,768]{3,2,1,0:T(8,128)(2,1)S(1)} collective-permute-done((bf16[2,2,96,768]{3,2,1,0:T(8,128)(2,1)S(1)}, bf16[2,2,96,768]{3,2,1,0:T(8,128)(2,1)S(1)}, u32[]{:S(2)}, u32[]{:S(2)}) %collective-permute-start.64) | collective-permute-done | bytes 589856 | tf_op jit(solution)/shard_map/ppermute | solution.py:388
  309.4 2.0 collective-permute-done.66
  312.0 5.6 %collective-permute-done.59 = bf16[1,2,96,768]{3,2,1,0:T(8,128)(2,1)S(1)} collective-permute-done((bf16[1,2,96,768]{3,2,1,0:T(8,128)(2,1)S(1)}, bf16[1,2,96,768]{3,2,1,0:T(8,128)(2,1)S(1)}, u32[]{:S(2)}, u32[]{:S(2)}) %collective-permute-start.59) | collective-permute-done | bytes 294944 | tf_op jit(solution)/shard_map/ppermute | solution.py:388
  317.9 1.8 collective-permute-start.63
  319.7 1.8 collective-permute-done.65
  322.6 2.1 collective-permute-start.68
  328.3 16.6 %collective-permute-done.68 = bf16[96,1536]{1,0:T(8,128)(2,1)S(1)} collective-permute-done((bf16[96,1536]{1,0:T(8,128)(2,1)}, bf16[96,1536]{1,0:T(8,128)(2,1)S(1)}, u32[]{:S(2)}, u32[]{:S(2)}) %collective-permute-start.68) | collective-permute-done | bytes 294944 | tf_op jit(solution)/shard_map/ppermute | solution.py:393
  346.0 1.6 collective-permute-start.70
  348.8 4.3 %collective-permute-done.70 = bf16[96,1536]{1,0:T(8,128)(2,1)S(1)} collective-permute-done((bf16[96,1536]{1,0:T(8,128)(2,1)S(1)}, bf16[96,1536]{1,0:T(8,128)(2,1)S(1)}, u32[]{:S(2)}, u32[]{:S(2)}) %collective-permute-start.70) | collective-permute-done | bytes 294944 | tf_op jit(solution)/shard_map/ppermute | solution.py:388
  (338 shorter events, 64.3 us)
Async XLA Ops:
  3.2 13.9 %collective-permute-start.2 = (bf16[96,768]{1,0:T(8,128)(2,1)S(1)}, bf16[96,768]{1,0:T(8,128)(2,1)S(1)}, u32[]{:S(2)}, u32[]{:S(2)}) collective-permute-start(bf16[96,768]{1,0:T(8,128)(2,1)S(1)} %copy.48), channel_id=1, source_target_pairs={{0,3},{1,0},{2,1},{3,2},{4,7},{5,4},{6,5},{7,6},{8,11},{9,8},{10,9... | collective-permute-start | bytes 442376 | tf_op jit(solution)/shard_map/ppermute | solution.py:393
  8.3 25.9 %collective-permute-start.1 = (bf16[96,768]{1,0:T(8,128)(2,1)S(1)}, bf16[96,768]{1,0:T(8,128)(2,1)S(1)}, u32[]{:S(2)}, u32[]{:S(2)}) collective-permute-start(bf16[96,768]{1,0:T(8,128)(2,1)S(1)} %copy.48), channel_id=1, source_target_pairs={{0,2},{1,3},{2,0},{3,1},{4,6},{5,7},{6,4},{7,5},{8,10},{9,11},{10,... | collective-permute-start | bytes 442376 | tf_op jit(solution)/shard_map/ppermute | solution.py:393
  8.3 25.9 %collective-permute-start = (bf16[96,768]{1,0:T(8,128)(2,1)S(1)}, bf16[96,768]{1,0:T(8,128)(2,1)S(1)}, u32[]{:S(2)}, u32[]{:S(2)}) collective-permute-start(bf16[96,768]{1,0:T(8,128)(2,1)S(1)} %copy.48), channel_id=1, source_target_pairs={{0,1},{1,2},{2,3},{3,0},{4,5},{5,6},{6,7},{7,4},{8,9},{9,10},{10,1... | collective-permute-start | bytes 442376 | tf_op jit(solution)/shard_map/ppermute | solution.py:393
  9.4 31.1 %collective-permute-start.18 = (bf16[96,1536]{1,0:T(8,128)(2,1)S(1)}, bf16[96,1536]{1,0:T(8,128)(2,1)S(1)}, u32[]{:S(2)}, u32[]{:S(2)}) collective-permute-start(bf16[96,1536]{1,0:T(8,128)(2,1)S(1)} %get-tuple-element.164), channel_id=1, source_target_pairs={{0,2},{1,3},{2,0},{3,1},{4,6},{5,7},{6,4},{7,5},{8,10},{9,11},{10,... | collective-permute-start | bytes 884744 | tf_op jit(solution)/shard_map/ppermute | solution.py:393
  11.4 30.6 %collective-permute-start.17 = (bf16[96,1536]{1,0:T(8,128)(2,1)S(1)}, bf16[96,1536]{1,0:T(8,128)(2,1)S(1)}, u32[]{:S(2)}, u32[]{:S(2)}) collective-permute-start(bf16[96,1536]{1,0:T(8,128)(2,1)S(1)} %get-tuple-element.164), channel_id=1, source_target_pairs={{0,1},{1,2},{2,3},{3,0},{4,5},{5,6},{6,7},{7,4},{8,9},{9,10},{10,1... | collective-permute-start | bytes 884744 | tf_op jit(solution)/shard_map/ppermute | solution.py:393
  17.1 27.1 %collective-permute-start.19 = (bf16[96,1536]{1,0:T(8,128)(2,1)S(1)}, bf16[96,1536]{1,0:T(8,128)(2,1)S(1)}, u32[]{:S(2)}, u32[]{:S(2)}) collective-permute-start(bf16[96,1536]{1,0:T(8,128)(2,1)S(1)} %get-tuple-element.164), channel_id=1, source_target_pairs={{0,3},{1,0},{2,1},{3,2},{4,7},{5,4},{6,5},{7,6},{8,11},{9,8},{10,9... | collective-permute-start | bytes 884744 | tf_op jit(solution)/shard_map/ppermute | solution.py:393
  44.2 10.9 %collective-permute-start.3 = (bf16[4,96,384]{2,1,0:T(8,128)(2,1)S(1)}, bf16[4,96,384]{2,1,0:T(8,128)(2,1)S(1)}, u32[]{:S(2)}, u32[]{:S(2)}) collective-permute-start(bf16[4,96,384]{2,1,0:T(8,128)(2,1)S(1)} %get-tuple-element.158.rest_0_), channel_id=1, source_target_pairs={{0,16},{16,0},{1,17},{17,1},{2,18},{18,2},{3,19},{19,3},{4,20},{20... | collective-permute-start | bytes 884744 | tf_op jit(solution)/shard_map/ppermute | solution.py:388
  44.8 10.3 %collective-permute-start.15 = (bf16[4,96,384]{2,1,0:T(8,128)(2,1)S(1)}, bf16[4,96,384]{2,1,0:T(8,128)(2,1)S(1)}, u32[]{:S(2)}, u32[]{:S(2)}) collective-permute-start(bf16[4,96,384]{2,1,0:T(8,128)(2,1)S(1)} %collective-permute-done.13.rest_12_), channel_id=1, source_target_pairs={{0,4},{4,0},{8,12},{12,8},{1,5},{5,1},{9,13},{13,9},{2,6},{6,2},{1... | collective-permute-start | bytes 884744 | tf_op jit(solution)/shard_map/ppermute | solution.py:388
  53.8 17.9 %collective-permute-start.12 = (bf16[4,96,384]{2,1,0:T(8,128)(2,1)S(1)}, bf16[4,96,384]{2,1,0:T(8,128)(2,1)S(1)}, u32[]{:S(2)}, u32[]{:S(2)}) collective-permute-start(bf16[4,96,384]{2,1,0:T(8,128)(2,1)S(1)} %collective-permute-done.10.rest_9_), channel_id=1, source_target_pairs={{0,4},{4,0},{8,12},{12,8},{1,5},{5,1},{9,13},{13,9},{2,6},{6,2},{1... | collective-permute-start | bytes 884744 | tf_op jit(solution)/shard_map/ppermute | solution.py:388
  55.1 18.1 %collective-permute-start.8 = (bf16[4,96,384]{2,1,0:T(8,128)(2,1)S(1)}, bf16[4,96,384]{2,1,0:T(8,128)(2,1)S(1)}, u32[]{:S(2)}, u32[]{:S(2)}) collective-permute-start(bf16[4,96,384]{2,1,0:T(8,128)(2,1)S(1)} %collective-permute-done.6.rest_4_), channel_id=1, source_target_pairs={{0,4},{4,0},{8,12},{12,8},{1,5},{5,1},{9,13},{13,9},{2,6},{6,2},{1... | collective-permute-start | bytes 884744 | tf_op jit(solution)/shard_map/ppermute | solution.py:388
  55.2 18.2 %collective-permute-start.5 = (bf16[4,96,384]{2,1,0:T(8,128)(2,1)S(1)}, bf16[4,96,384]{2,1,0:T(8,128)(2,1)S(1)}, u32[]{:S(2)}, u32[]{:S(2)}) collective-permute-start(bf16[4,96,384]{2,1,0:T(8,128)(2,1)S(1)} %collective-permute-done.3.rest_1_), channel_id=1, source_target_pairs={{0,4},{4,0},{8,12},{12,8},{1,5},{5,1},{9,13},{13,9},{2,6},{6,2},{1... | collective-permute-start | bytes 884744 | tf_op jit(solution)/shard_map/ppermute | solution.py:388
  55.9 18.9 %collective-permute-start.16 = (bf16[4,96,384]{2,1,0:T(8,128)(2,1)S(1)}, bf16[4,96,384]{2,1,0:T(8,128)(2,1)S(1)}, u32[]{:S(2)}, u32[]{:S(2)}) collective-permute-start(bf16[4,96,384]{2,1,0:T(8,128)(2,1)S(1)} %collective-permute-done.14.rest_13_), channel_id=1, source_target_pairs={{0,4},{4,0},{8,12},{12,8},{1,5},{5,1},{9,13},{13,9},{2,6},{6,2},{1... | collective-permute-start | bytes 884744 | tf_op jit(solution)/shard_map/ppermute | solution.py:388
  60.7 14.7 %collective-permute-start.9 = (bf16[4,96,384]{2,1,0:T(8,128)(2,1)S(1)}, bf16[4,96,384]{2,1,0:T(8,128)(2,1)S(1)}, u32[]{:S(2)}, u32[]{:S(2)}) collective-permute-start(bf16[4,96,384]{2,1,0:T(8,128)(2,1)S(1)} %collective-permute-done.7.rest_5_), channel_id=1, source_target_pairs={{0,4},{4,0},{8,12},{12,8},{1,5},{5,1},{9,13},{13,9},{2,6},{6,2},{1... | collective-permute-start | bytes 884744 | tf_op jit(solution)/shard_map/ppermute | solution.py:388
  71.7 30.5 %collective-permute-start.23 = (bf16[4,96,768]{2,1,0:T(8,128)(2,1)S(1)}, bf16[4,96,768]{2,1,0:T(8,128)(2,1)S(1)}, u32[]{:S(2)}, u32[]{:S(2)}) collective-permute-start(bf16[4,96,768]{2,1,0:T(8,128)(2,1)S(1)} %get-tuple-element.60.rest_0_.rest_16_), channel_id=1, source_target_pairs={{0,8},{4,12},{8,0},{12,4},{1,9},{5,13},{9,1},{13,5},{2,10},{6,14},... | collective-permute-start | bytes 1769480 | tf_op jit(solution)/shard_map/ppermute | solution.py:388
  73.3 91.8 %collective-permute-start.21 = (bf16[4,96,768]{2,1,0:T(8,128)(2,1)S(1)}, bf16[4,96,768]{2,1,0:T(8,128)(2,1)}, u32[]{:S(2)}, u32[]{:S(2)}) collective-permute-start(bf16[4,96,768]{2,1,0:T(8,128)(2,1)S(1)} %get-tuple-element.60.rest_0_.rest_16_), channel_id=1, source_target_pairs={{0,4},{4,0},{8,12},{12,8},{1,5},{5,1},{9,13},{13,9},{2,6},{6,2},{1... | collective-permute-start | bytes 1769480 | tf_op jit(solution)/shard_map/ppermute | solution.py:388
  73.3 91.8 %collective-permute-start.20 = (bf16[4,96,768]{2,1,0:T(8,128)(2,1)S(1)}, bf16[4,96,768]{2,1,0:T(8,128)(2,1)}, u32[]{:S(2)}, u32[]{:S(2)}) collective-permute-start(bf16[4,96,768]{2,1,0:T(8,128)(2,1)S(1)} %get-tuple-element.60.rest_0_.rest_16_), channel_id=1, source_target_pairs={{0,16},{16,0},{1,17},{17,1},{2,18},{18,2},{3,19},{19,3},{4,20},{20... | collective-permute-start | bytes 1769480 | tf_op jit(solution)/shard_map/ppermute | solution.py:388
  74.9 27.8 %collective-permute-start.27 = (bf16[4,96,768]{2,1,0:T(8,128)(2,1)S(1)}, bf16[4,96,768]{2,1,0:T(8,128)(2,1)S(1)}, u32[]{:S(2)}, u32[]{:S(2)}) collective-permute-start(bf16[4,96,768]{2,1,0:T(8,128)(2,1)S(1)} %get-tuple-element.61.rest_8_.rest_24_), channel_id=1, source_target_pairs={{0,16},{16,0},{1,17},{17,1},{2,18},{18,2},{3,19},{19,3},{4,20},{20... | collective-permute-start | bytes 1769480 | tf_op jit(solution)/shard_map/ppermute | solution.py:388
  102.1 29.2 %collective-permute-start.34 = (bf16[4,2,96,384]{3,2,1,0:T(8,128)(2,1)}, bf16[4,2,96,384]{3,2,1,0:T(8,128)(2,1)S(1)}, u32[]{:S(2)}, u32[]{:S(2)}) collective-permute-start(bf16[4,2,96,384]{3,2,1,0:T(8,128)(2,1)} %get-tuple-element.75), channel_id=1, source_target_pairs={{0,4},{4,0},{8,12},{12,8},{1,5},{5,1},{9,13},{13,9},{2,6},{6,2},{1... | collective-permute-start | bytes 1769480 | tf_op jit(solution)/shard_map/ppermute | solution.py:388
  102.2 30.7 %collective-permute-start.35 = (bf16[4,2,96,384]{3,2,1,0:T(8,128)(2,1)}, bf16[4,2,96,384]{3,2,1,0:T(8,128)(2,1)S(1)}, u32[]{:S(2)}, u32[]{:S(2)}) collective-permute-start(bf16[4,2,96,384]{3,2,1,0:T(8,128)(2,1)} %get-tuple-element.76), channel_id=1, source_target_pairs={{0,4},{4,0},{8,12},{12,8},{1,5},{5,1},{9,13},{13,9},{2,6},{6,2},{1... | collective-permute-start | bytes 1769480 | tf_op jit(solution)/shard_map/ppermute | solution.py:388
  133.0 32.8 %collective-permute-start.30 = (bf16[4,96,768]{2,1,0:T(8,128)(2,1)S(1)}, bf16[4,96,768]{2,1,0:T(8,128)(2,1)S(1)}, u32[]{:S(2)}, u32[]{:S(2)}) collective-permute-start(bf16[4,96,768]{2,1,0:T(8,128)(2,1)S(1)} %get-tuple-element.61.rest_8_.rest_24_), channel_id=1, source_target_pairs={{0,8},{4,12},{8,0},{12,4},{1,9},{5,13},{9,1},{13,5},{2,10},{6,14},... | collective-permute-start | bytes 1769480 | tf_op jit(solution)/shard_map/ppermute | solution.py:388
  134.8 20.0 %collective-permute-start.38 = (bf16[2,2,96,384]{3,2,1,0:T(8,128)(2,1)S(1)}, bf16[2,2,96,384]{3,2,1,0:T(8,128)(2,1)S(1)}, u32[]{:S(2)}, u32[]{:S(2)}) collective-permute-start(bf16[2,2,96,384]{3,2,1,0:T(8,128)(2,1)S(1)} %get-tuple-element.144), channel_id=1, source_target_pairs={{0,8},{4,12},{8,0},{12,4},{1,9},{5,13},{9,1},{13,5},{2,10},{6,14},... | collective-permute-start | bytes 884744 | tf_op jit(solution)/shard_map/ppermute | solution.py:388
  136.5 18.8 %collective-permute-start.39 = (bf16[2,2,96,384]{3,2,1,0:T(8,128)(2,1)S(1)}, bf16[2,2,96,384]{3,2,1,0:T(8,128)(2,1)S(1)}, u32[]{:S(2)}, u32[]{:S(2)}) collective-permute-start(bf16[2,2,96,384]{3,2,1,0:T(8,128)(2,1)S(1)} %get-tuple-element.146), channel_id=1, source_target_pairs={{0,16},{16,0},{1,17},{17,1},{2,18},{18,2},{3,19},{19,3},{4,20},{20... | collective-permute-start | bytes 884744 | tf_op jit(solution)/shard_map/ppermute | solution.py:388
  165.0 20.9 %collective-permute-start.25 = (bf16[4,96,768]{2,1,0:T(8,128)(2,1)S(1)}, bf16[4,96,768]{2,1,0:T(8,128)(2,1)S(1)}, u32[]{:S(2)}, u32[]{:S(2)}) collective-permute-start(bf16[4,96,768]{2,1,0:T(8,128)(2,1)S(1)} %copy-done.45), channel_id=1, source_target_pairs={{0,4},{4,0},{8,12},{12,8},{1,5},{5,1},{9,13},{13,9},{2,6},{6,2},{1... | collective-permute-start | bytes 1769480 | tf_op jit(solution)/shard_map/ppermute | solution.py:388
  165.1 20.9 %collective-permute-start.24 = (bf16[4,96,768]{2,1,0:T(8,128)(2,1)S(1)}, bf16[4,96,768]{2,1,0:T(8,128)(2,1)S(1)}, u32[]{:S(2)}, u32[]{:S(2)}) collective-permute-start(bf16[4,96,768]{2,1,0:T(8,128)(2,1)S(1)} %copy-done.45), channel_id=1, source_target_pairs={{0,16},{16,0},{1,17},{17,1},{2,18},{18,2},{3,19},{19,3},{4,20},{20... | collective-permute-start | bytes 1769480 | tf_op jit(solution)/shard_map/ppermute | solution.py:388
  165.7 20.8 %collective-permute-start.31 = (bf16[4,96,768]{2,1,0:T(8,128)(2,1)S(1)}, bf16[4,96,768]{2,1,0:T(8,128)(2,1)S(1)}, u32[]{:S(2)}, u32[]{:S(2)}) collective-permute-start(bf16[4,96,768]{2,1,0:T(8,128)(2,1)S(1)} %copy-done.47), channel_id=1, source_target_pairs={{0,8},{4,12},{8,0},{12,4},{1,9},{5,13},{9,1},{13,5},{2,10},{6,14},... | collective-permute-start | bytes 1769480 | tf_op jit(solution)/shard_map/ppermute | solution.py:388
  170.2 14.2 %collective-permute-start.48 = (bf16[1,2,96,384]{3,2,1,0:T(8,128)(2,1)S(1)}, bf16[1,2,96,384]{3,2,1,0:T(8,128)(2,1)S(1)}, u32[]{:S(2)}, u32[]{:S(2)}) collective-permute-start(bf16[1,2,96,384]{3,2,1,0:T(8,128)(2,1)S(1)} %add_convert_fusion.35), channel_id=1, source_target_pairs={{0,8},{4,12},{8,0},{12,4},{1,9},{5,13},{9,1},{13,5},{2,10},{6,14},... | collective-permute-start | bytes 442376 | tf_op jit(solution)/shard_map/ppermute | solution.py:388
  170.6 16.0 %collective-permute-start.51 = (bf16[1,2,96,384]{3,2,1,0:T(8,128)(2,1)S(1)}, bf16[1,2,96,384]{3,2,1,0:T(8,128)(2,1)S(1)}, u32[]{:S(2)}, u32[]{:S(2)}) collective-permute-start(bf16[1,2,96,384]{3,2,1,0:T(8,128)(2,1)S(1)} %add_convert_fusion.32), channel_id=1, source_target_pairs={{0,16},{16,0},{1,17},{17,1},{2,18},{18,2},{3,19},{19,3},{4,20},{20... | collective-permute-start | bytes 442376 | tf_op jit(solution)/shard_map/ppermute | solution.py:388
  185.9 10.6 %collective-permute-start.29 = (bf16[4,96,768]{2,1,0:T(8,128)(2,1)S(1)}, bf16[4,96,768]{2,1,0:T(8,128)(2,1)S(1)}, u32[]{:S(2)}, u32[]{:S(2)}) collective-permute-start(bf16[4,96,768]{2,1,0:T(8,128)(2,1)S(1)} %copy-done.47), channel_id=1, source_target_pairs={{0,4},{4,0},{8,12},{12,8},{1,5},{5,1},{9,13},{13,9},{2,6},{6,2},{1... | collective-permute-start | bytes 1769480 | tf_op jit(solution)/shard_map/ppermute | solution.py:388
  186.6 11.9 %collective-permute-start.26 = (bf16[4,96,768]{2,1,0:T(8,128)(2,1)S(1)}, bf16[4,96,768]{2,1,0:T(8,128)(2,1)S(1)}, u32[]{:S(2)}, u32[]{:S(2)}) collective-permute-start(bf16[4,96,768]{2,1,0:T(8,128)(2,1)S(1)} %collective-permute-done.24.rest_5_.rest_21_), channel_id=1, source_target_pairs={{0,4},{4,0},{8,12},{12,8},{1,5},{5,1},{9,13},{13,9},{2,6},{6,2},{1... | collective-permute-start | bytes 1769480 | tf_op jit(solution)/shard_map/ppermute | solution.py:388
  190.3 58.4 %collective-permute-start.49 = (bf16[96,768]{1,0:T(8,128)(2,1)S(1)}, bf16[96,768]{1,0:T(8,128)(2,1)S(1)}, u32[]{:S(2)}, u32[]{:S(2)}) collective-permute-start(bf16[96,768]{1,0:T(8,128)(2,1)S(1)} %fusion.25), channel_id=1, source_target_pairs={{0,3},{1,0},{2,1},{3,2},{4,7},{5,4},{6,5},{7,6},{8,11},{9,8},{10,9... | collective-permute-start | bytes 442376 | tf_op jit(solution)/shard_map/ppermute | solution.py:393
  193.9 55.0 %collective-permute-start.54 = (bf16[96,768]{1,0:T(8,128)(2,1)}, bf16[96,768]{1,0:T(8,128)(2,1)S(1)}, u32[]{:S(2)}, u32[]{:S(2)}) collective-permute-start(bf16[96,768]{1,0:T(8,128)(2,1)} %get-tuple-element.161), channel_id=1, source_target_pairs={{0,2},{1,3},{2,0},{3,1},{4,6},{5,7},{6,4},{7,5},{8,10},{9,11},{10,... | collective-permute-start | bytes 442376 | tf_op jit(solution)/shard_map/ppermute | solution.py:393
  196.6 52.8 %collective-permute-start.55 = (bf16[96,768]{1,0:T(8,128)(2,1)S(1)}, bf16[96,768]{1,0:T(8,128)(2,1)S(1)}, u32[]{:S(2)}, u32[]{:S(2)}) collective-permute-start(bf16[96,768]{1,0:T(8,128)(2,1)S(1)} %get-tuple-element.162), channel_id=1, source_target_pairs={{0,1},{1,2},{2,3},{3,0},{4,5},{5,6},{6,7},{7,4},{8,9},{9,10},{10,1... | collective-permute-start | bytes 442376 | tf_op jit(solution)/shard_map/ppermute | solution.py:393
  236.1 19.4 %collective-permute-start.40 = (bf16[4,2,96,768]{3,2,1,0:T(8,128)(2,1)}, bf16[4,2,96,768]{3,2,1,0:T(8,128)(2,1)S(1)}, u32[]{:S(2)}, u32[]{:S(2)}) collective-permute-start(bf16[4,2,96,768]{3,2,1,0:T(8,128)(2,1)} %get-tuple-element.92), channel_id=1, source_target_pairs={{0,4},{4,0},{8,12},{12,8},{1,5},{5,1},{9,13},{13,9},{2,6},{6,2},{1... | collective-permute-start | bytes 3538952 | tf_op jit(solution)/shard_map/ppermute | solution.py:388
  236.1 19.4 %collective-permute-start.41 = (bf16[4,2,96,768]{3,2,1,0:T(8,128)(2,1)}, bf16[4,2,96,768]{3,2,1,0:T(8,128)(2,1)S(1)}, u32[]{:S(2)}, u32[]{:S(2)}) collective-permute-start(bf16[4,2,96,768]{3,2,1,0:T(8,128)(2,1)} %get-tuple-element.93), channel_id=1, source_target_pairs={{0,4},{4,0},{8,12},{12,8},{1,5},{5,1},{9,13},{13,9},{2,6},{6,2},{1... | collective-permute-start | bytes 3538952 | tf_op jit(solution)/shard_map/ppermute | solution.py:388
  248.8 23.1 %collective-permute-start.57 = (bf16[4,2,96,768]{3,2,1,0:T(8,128)(2,1)}, bf16[4,2,96,768]{3,2,1,0:T(8,128)(2,1)}, u32[]{:S(2)}, u32[]{:S(2)}) collective-permute-start(bf16[4,2,96,768]{3,2,1,0:T(8,128)(2,1)} %get-tuple-element.100), channel_id=1, source_target_pairs={{0,4},{4,0},{8,12},{12,8},{1,5},{5,1},{9,13},{13,9},{2,6},{6,2},{1... | collective-permute-start | bytes 3538952 | tf_op jit(solution)/shard_map/ppermute | solution.py:388
  248.9 27.2 %collective-permute-start.60 = (bf16[4,2,96,768]{3,2,1,0:T(8,128)(2,1)}, bf16[4,2,96,768]{3,2,1,0:T(8,128)(2,1)}, u32[]{:S(2)}, u32[]{:S(2)}) collective-permute-start(bf16[4,2,96,768]{3,2,1,0:T(8,128)(2,1)} %get-tuple-element.102), channel_id=1, source_target_pairs={{0,4},{4,0},{8,12},{12,8},{1,5},{5,1},{9,13},{13,9},{2,6},{6,2},{1... | collective-permute-start | bytes 3538952 | tf_op jit(solution)/shard_map/ppermute | solution.py:388
  273.9 25.1 %collective-permute-start.58 = (bf16[2,2,96,768]{3,2,1,0:T(8,128)(2,1)S(1)}, bf16[2,2,96,768]{3,2,1,0:T(8,128)(2,1)S(1)}, u32[]{:S(2)}, u32[]{:S(2)}) collective-permute-start(bf16[2,2,96,768]{3,2,1,0:T(8,128)(2,1)S(1)} %get-tuple-element.134), channel_id=1, source_target_pairs={{0,8},{4,12},{8,0},{12,4},{1,9},{5,13},{9,1},{13,5},{2,10},{6,14},... | collective-permute-start | bytes 1769480 | tf_op jit(solution)/shard_map/ppermute | solution.py:388
  274.5 16.0 %collective-permute-start.43 = (f32[72,128]{1,0:T(8,128)S(1)}, f32[72,128]{1,0:T(8,128)S(1)}, u32[]{:S(2)}, u32[]{:S(2)}) collective-permute-start(f32[72,128]{1,0:T(8,128)S(1)} %fusion.35), channel_id=1, source_target_pairs={{0,8},{4,12},{8,0},{12,4},{1,9},{5,13},{9,1},{13,5},{2,10},{6,14},... | collective-permute-start | bytes 110600 | tf_op jit(solution)/shard_map/ppermute | solution.py:388
  277.8 22.8 %collective-permute-start.61 = (bf16[2,2,96,768]{3,2,1,0:T(8,128)(2,1)S(1)}, bf16[2,2,96,768]{3,2,1,0:T(8,128)(2,1)S(1)}, u32[]{:S(2)}, u32[]{:S(2)}) collective-permute-start(bf16[2,2,96,768]{3,2,1,0:T(8,128)(2,1)S(1)} %get-tuple-element.136), channel_id=1, source_target_pairs={{0,16},{16,0},{1,17},{17,1},{2,18},{18,2},{3,19},{19,3},{4,20},{20... | collective-permute-start | bytes 1769480 | tf_op jit(solution)/shard_map/ppermute | solution.py:388
  292.4 16.3 %collective-permute-start.64 = (bf16[2,2,96,768]{3,2,1,0:T(8,128)(2,1)S(1)}, bf16[2,2,96,768]{3,2,1,0:T(8,128)(2,1)S(1)}, u32[]{:S(2)}, u32[]{:S(2)}) collective-permute-start(bf16[2,2,96,768]{3,2,1,0:T(8,128)(2,1)S(1)} %get-tuple-element.138), channel_id=1, source_target_pairs={{0,8},{4,12},{8,0},{12,4},{1,9},{5,13},{9,1},{13,5},{2,10},{6,14},... | collective-permute-start | bytes 1769480 | tf_op jit(solution)/shard_map/ppermute | solution.py:388
  295.0 16.3 %collective-permute-start.66 = (bf16[2,2,96,768]{3,2,1,0:T(8,128)(2,1)S(1)}, bf16[2,2,96,768]{3,2,1,0:T(8,128)(2,1)S(1)}, u32[]{:S(2)}, u32[]{:S(2)}) collective-permute-start(bf16[2,2,96,768]{3,2,1,0:T(8,128)(2,1)S(1)} %get-tuple-element.140), channel_id=1, source_target_pairs={{0,16},{16,0},{1,17},{17,1},{2,18},{18,2},{3,19},{19,3},{4,20},{20... | collective-permute-start | bytes 1769480 | tf_op jit(solution)/shard_map/ppermute | solution.py:388
  298.5 29.2 %collective-permute-start.46 = (f32[72,128]{1,0:T(8,128)S(1)}, f32[72,128]{1,0:T(8,128)S(1)}, u32[]{:S(2)}, u32[]{:S(2)}) collective-permute-start(f32[72,128]{1,0:T(8,128)S(1)} %add.228), channel_id=1, source_target_pairs={{0,2},{1,3},{2,0},{3,1},{4,6},{5,7},{6,4},{7,5},{8,10},{9,11},{10,... | collective-permute-start | bytes 110600 | tf_op jit(solution)/shard_map/ppermute | solution.py:388
  299.0 18.6 %collective-permute-start.59 = (bf16[1,2,96,768]{3,2,1,0:T(8,128)(2,1)S(1)}, bf16[1,2,96,768]{3,2,1,0:T(8,128)(2,1)S(1)}, u32[]{:S(2)}, u32[]{:S(2)}) collective-permute-start(bf16[1,2,96,768]{3,2,1,0:T(8,128)(2,1)S(1)} %add_convert_fusion.18), channel_id=1, source_target_pairs={{0,16},{16,0},{1,17},{17,1},{2,18},{18,2},{3,19},{19,3},{4,20},{20... | collective-permute-start | bytes 884744 | tf_op jit(solution)/shard_map/ppermute | solution.py:388
  300.6 17.1 %collective-permute-start.62 = (bf16[1,2,96,768]{3,2,1,0:T(8,128)(2,1)S(1)}, bf16[1,2,96,768]{3,2,1,0:T(8,128)(2,1)S(1)}, u32[]{:S(2)}, u32[]{:S(2)}) collective-permute-start(bf16[1,2,96,768]{3,2,1,0:T(8,128)(2,1)S(1)} %add_convert_fusion.15), channel_id=1, source_target_pairs={{0,8},{4,12},{8,0},{12,4},{1,9},{5,13},{9,1},{13,5},{2,10},{6,14},... | collective-permute-start | bytes 884744 | tf_op jit(solution)/shard_map/ppermute | solution.py:388
  308.8 12.7 %collective-permute-start.65 = (bf16[1,2,96,768]{3,2,1,0:T(8,128)(2,1)S(1)}, bf16[1,2,96,768]{3,2,1,0:T(8,128)(2,1)S(1)}, u32[]{:S(2)}, u32[]{:S(2)}) collective-permute-start(bf16[1,2,96,768]{3,2,1,0:T(8,128)(2,1)S(1)} %add_convert_fusion.12), channel_id=1, source_target_pairs={{0,16},{16,0},{1,17},{17,1},{2,18},{18,2},{3,19},{19,3},{4,20},{20... | collective-permute-start | bytes 884744 | tf_op jit(solution)/shard_map/ppermute | solution.py:388
  317.9 10.4 %collective-permute-start.63 = (bf16[96,1536]{1,0:T(8,128)(2,1)S(1)}, bf16[96,1536]{1,0:T(8,128)(2,1)S(1)}, u32[]{:S(2)}, u32[]{:S(2)}) collective-permute-start(bf16[96,1536]{1,0:T(8,128)(2,1)S(1)} %fusion.12), channel_id=1, source_target_pairs={{0,3},{1,0},{2,1},{3,2},{4,7},{5,4},{6,5},{7,6},{8,11},{9,8},{10,9... | collective-permute-start | bytes 884744 | tf_op jit(solution)/shard_map/ppermute | solution.py:393
  322.6 22.3 %collective-permute-start.68 = (bf16[96,1536]{1,0:T(8,128)(2,1)}, bf16[96,1536]{1,0:T(8,128)(2,1)S(1)}, u32[]{:S(2)}, u32[]{:S(2)}) collective-permute-start(bf16[96,1536]{1,0:T(8,128)(2,1)} %get-tuple-element.155), channel_id=1, source_target_pairs={{0,2},{1,3},{2,0},{3,1},{4,6},{5,7},{6,4},{7,5},{8,10},{9,11},{10,... | collective-permute-start | bytes 884744 | tf_op jit(solution)/shard_map/ppermute | solution.py:393
  324.7 20.2 %collective-permute-start.69 = (bf16[96,1536]{1,0:T(8,128)(2,1)}, bf16[96,1536]{1,0:T(8,128)(2,1)}, u32[]{:S(2)}, u32[]{:S(2)}) collective-permute-start(bf16[96,1536]{1,0:T(8,128)(2,1)} %get-tuple-element.156), channel_id=1, source_target_pairs={{0,1},{1,2},{2,3},{3,0},{4,5},{5,6},{6,7},{7,4},{8,9},{9,10},{10,1... | collective-permute-start | bytes 884744 | tf_op jit(solution)/shard_map/ppermute | solution.py:393
  (95 other events, 949.4 us)

commit v3 on v2

v3 whole, which is shorter than its diff:
```python
import functools
import math

import jax
import jax.numpy as jnp
from jax import lax
from jax.experimental import pallas as pl
from jax.experimental.pallas import tpu as pltpu
from jax.sharding import PartitionSpec as P

HD = 64
ROT = 16
QKV = 3 * HD
HEAD = 4 * HD
EPSILON = 1e-05
ROPE_BASE = 10000.0
NEAR = 128
LONGEST = 256
F32 = jnp.float32
BF16 = jnp.bfloat16


def dot_nn(a, b):
    return lax.dot_general(a, b, (((1,), (0,)), ((), ())), preferred_element_type=F32)


def dot_nt(a, b):
    return lax.dot_general(a, b, (((1,), (1,)), ((), ())), preferred_element_type=F32)


def gathered_order(order, core_bit):
    held = [0]
    for bit in order[:-1]:
        held = held + [j | bit for j in held]
    came = [j | order[-1] for j in held]
    return held, came, [j | core_bit for j in held], [j | core_bit for j in came]


def reduced_order(order):
    kept = [0]
    for bit in order[::-1]:
        kept = kept + [j | bit for j in kept]
    return kept


def assemble(me_ref, w_refs, held, w_scr, at_col):
    for ref, pieces in zip(w_refs, held):
        _, _, rows, cols = ref.shape
        for t, j in enumerate(pieces):
            at = pl.multiple_of((me_ref[0] ^ j) * rows, 16)
            w_scr[pl.ds(at, rows), at_col : at_col + cols] = ref[t, 0]


def hand_out(me_ref, g_scr, at_col, keep_ref, send_ref, first, order, core_bit):
    _, _, rows, cols = keep_ref.shape
    for t, j in enumerate(reduced_order(order)):
        for ref, piece in ((keep_ref, j), (send_ref, j | core_bit)):
            at = pl.multiple_of((me_ref[0] ^ piece) * rows, 16)
            ref[first + t, 0] = g_scr[pl.ds(at, rows), at_col : at_col + cols]


def normalize(x):
    center = x - jnp.mean(x, axis=1, keepdims=True)
    inv_std = lax.rsqrt(jnp.mean(center * center, axis=1, keepdims=True) + EPSILON)
    return center * inv_std, inv_std


def prep_kernel(
    x_ref, cot_ref, ga_ref, sa_ref, gm_ref, sm_ref, segc_ref, segr_ref, freq_ref, _mlp_in, _after,
    na_ref, naT_ref, nm_ref, nmT_ref, cotT_ref, keep_ref, ahead_ref, behind_ref, mask_ref, _mlp_out,
):
    length = x_ref.shape[0]
    tile = 128

    @pl.loop(0, length // tile)
    def _(t):
        rows = pl.ds(pl.multiple_of(t * tile, tile), tile)
        normed, _ = normalize(x_ref[rows, :].astype(F32))
        na_ref[rows, :] = (normed * ga_ref[...] + sa_ref[...]).astype(BF16)
        nm_ref[rows, :] = (normed * gm_ref[...] + sm_ref[...]).astype(BF16)
        same = segc_ref[rows, :] == segr_ref[...]
        cols = lax.broadcasted_iota(jnp.int32, (tile, length), 1)
        ids = lax.broadcasted_iota(jnp.int32, (tile, length), 0) + t * tile
        mask_ref[rows, :] = jnp.where(same & (cols <= ids), 0.0, -jnp.inf)
        starts = jnp.min(jnp.where(same, cols, length).astype(F32), axis=1, keepdims=True)
        places = ids[:, :1].astype(F32) - starts
        angles = places * freq_ref[...]
        lane = lax.broadcasted_iota(jnp.int32, (tile, 2 * HD), 1) % HD
        cosine, sine = jnp.cos(angles), jnp.sin(angles)
        keep_ref[rows, :] = jnp.where(lane < ROT, cosine, 1.0)
        ahead_ref[rows, :] = jnp.where(lane < ROT // 2, -sine, 0.0)
        behind_ref[rows, :] = jnp.where((lane < ROT) & (lane >= ROT // 2), sine, 0.0)

    naT_ref[...] = na_ref[...].T
    nmT_ref[...] = nm_ref[...].T
    cotT_ref[...] = cot_ref[...].T


def full(*shape):
    return pl.BlockSpec(shape, lambda *_: (0,) * len(shape))


ANY = pl.BlockSpec(memory_space=pl.ANY)
SCALAR = pl.BlockSpec(memory_space=pltpu.SMEM)


def cost(us):
    return pl.CostEstimate(flops=int(us * 1.15e9), bytes_accessed=2**20, transcendentals=0)


def shaped(shape, dtype):
    return jax.ShapeDtypeStruct(shape, dtype)


def prep_part(tokens, cot, gains, seg_row, mlp_own, after):
    length, width = tokens.shape
    halves = ROT // 2
    step = (lax.iota(jnp.int32, 2 * HD) % HD % halves).astype(F32)
    freq = (ROPE_BASE ** (-(step * (2.0 / ROT))))[None, :]
    table = shaped((length, 2 * HD), F32)
    return pl.pallas_call(
        prep_kernel,
        grid=(1,),
        in_specs=[full(length, width)] * 2 + [full(1, width)] * 4
        + [full(length, 1), full(1, length), full(1, 2 * HD), ANY, ANY],
        out_specs=[full(length, width), full(width, length)] * 2 + [full(width, length)]
        + [full(length, 2 * HD)] * 3 + [full(length, length), ANY],
        out_shape=[shaped((length, width), BF16), shaped((width, length), BF16)] * 2
        + [shaped((width, length), BF16)] + [table] * 3 + [shaped((length, length), F32)]
        + [shaped(mlp_own.shape, BF16)],
        input_output_aliases={9: 9},
        compiler_params=pltpu.CompilerParams(vmem_limit_bytes=48 * 2**20),
        cost_estimate=cost(6),
    )(tokens, cot, *gains, seg_row[:, None], seg_row[None, :], freq, mlp_own, after)


def attention_kernel(orders, core_bit, waits, me_ref, na_ref, naT_ref, cot_ref, cotT_ref, *rest):
    left, right, rest = rest[:4], rest[4:8], rest[8:]
    bias_ref, keep_ref, ahead_ref, behind_ref, mask_ref = rest[:5]
    dqkv_ref, mix_ref, dbias_ref, gk_ref, gs_ref, w_scr, wv_scr, qkv_scr, dattn_scr, g_scr = rest[5 + waits :]
    length, width = na_ref.shape
    block_cols = w_scr.shape[1]
    heads = block_cols // HEAD
    kept = gk_ref.shape[0] // 2
    tile = 256
    assemble(me_ref, left, gathered_order(orders[0], core_bit), w_scr, 0)
    assemble(me_ref, right, gathered_order(orders[1], core_bit), w_scr, block_cols // 2)
    for i in range(heads):
        wv_scr[:, i * 2 * HD : (i + 1) * 2 * HD] = w_scr[:, i * HEAD + 2 * HD : (i + 1) * HEAD]

    @pl.loop(0, length // tile)
    def _(t):
        rows = pl.ds(pl.multiple_of(t * tile, tile), tile)
        qkv_scr[rows, :] = dot_nn(na_ref[rows, :], w_scr[...]) + bias_ref[0]
        dattn_scr[rows, :] = dot_nn(cot_ref[rows, :], wv_scr[...]).astype(BF16)

    low = lax.broadcasted_iota(jnp.int32, (length, 2 * HD), 1) < HD
    keep, ahead, behind = keep_ref[...], ahead_ref[...], behind_ref[...]
    none = jnp.zeros((length, 2 * HD), BF16)
    spans = [(b * NEAR, (b + 1) * NEAR, max(0, b * NEAR - LONGEST)) for b in range(length // NEAR)]
    for i in range(heads):
        qk = qkv_scr[:, i * HEAD : i * HEAD + 2 * HD]
        qk = qk * keep + pltpu.roll(qk, 2 * HD - ROT // 2, 1) * ahead + pltpu.roll(qk, ROT // 2, 1) * behind
        q0 = jnp.where(low, qk * (1.0 / math.sqrt(HD)), 0.0).astype(BF16)
        k0 = jnp.where(low, pltpu.roll(qk, HD, 1), 0.0).astype(BF16)
        v1 = jnp.where(low, 0.0, pltpu.roll(qkv_scr[:, i * HEAD + 2 * HD : (i + 1) * HEAD], HD, 1)).astype(BF16)
        go = dattn_scr[:, i * 2 * HD : (i + 1) * 2 * HD]
        go1 = jnp.where(low, none, go)
        qT = q0.T[:HD]
        goT = go.T[HD:]
        s = [dot_nt(q0[r0:r1], k0[lo:r1]) + mask_ref[r0:r1, lo:r1] for r0, r1, lo in spans]
        dp = [dot_nt(go1[r0:r1], v1[lo:r1]) for r0, r1, lo in spans]
        peak = [jnp.max(one, axis=1, keepdims=True) for one in s]
        e = [jnp.exp(one - top) for one, top in zip(s, peak)]
        norm = [1.0 / jnp.sum(one, axis=1, keepdims=True) for one in e]
        p = [one * scale for one, scale in zip(e, norm)]
        p_low = [one.astype(BF16) for one in p]
        mix = [dot_nn(one, v1[lo:r1]) for one, (r0, r1, lo) in zip(p_low, spans)]
        delta = [
            jnp.sum(one * go1[r0:r1].astype(F32), axis=1, keepdims=True) for one, (r0, r1, lo) in zip(mix, spans)
        ]
        ds = [(one * (grad - centre)).astype(BF16) for one, grad, centre in zip(p, dp, delta)]
        dq = [dot_nn(one, k0[lo:r1]) for one, (r0, r1, lo) in zip(ds, spans)]
        dkT = [dot_nn(qT[:, r0:r1], one) for one, (r0, r1, lo) in zip(ds, spans)]
        dvT = [dot_nn(goT[:, r0:r1], one) for one, (r0, r1, lo) in zip(p_low, spans)]
        sums = []
        for parts in (dvT, dkT):
            total = [None] * len(spans)
            for part, (r0, r1, lo) in zip(parts, spans):
                for n in range(lo // NEAR, r1 // NEAR):
                    one = part[:, n * NEAR - lo : (n + 1) * NEAR - lo]
                    total[n] = one if total[n] is None else total[n] + one
            sums.append(jnp.concatenate(total, axis=1))
        dvk = jnp.concatenate(sums, axis=0).T
        dqk = jnp.where(low, jnp.concatenate(dq, axis=0) * (1.0 / math.sqrt(HD)), dvk)
        dqk = dqk * keep - pltpu.roll(dqk, 2 * HD - ROT // 2, 1) * ahead - pltpu.roll(dqk, ROT // 2, 1) * behind
        dqkv_ref[0, :, i * HEAD : i * HEAD + 2 * HD] = dqk.astype(BF16)
        dqkv_ref[0, :, i * HEAD + 2 * HD : (i + 1) * HEAD] = jnp.where(low, dvk, 0.0).astype(BF16)
        mix_ref[0, :, i * 2 * HD : (i + 1) * 2 * HD] = jnp.concatenate(mix, axis=0).astype(BF16)

    dbias_ref[0] = jnp.sum(dqkv_ref[0].astype(F32), axis=0, keepdims=True)

    @pl.loop(0, width // tile)
    def _(t):
        rows = pl.ds(pl.multiple_of(t * tile, tile), tile)
        g_in = dot_nn(naT_ref[rows, :], dqkv_ref[0])
        g_out = dot_nn(cotT_ref[rows, :], mix_ref[0])
        for i in range(heads):
            at = i * HEAD
            g_scr[rows, at : at + 2 * HD] = g_in[:, at : at + 2 * HD].astype(BF16)
            g_scr[rows, at + 2 * HD : at + HEAD] = (
                g_in[:, at + 2 * HD : at + HEAD] + g_out[:, i * 2 * HD : (i + 1) * 2 * HD]
            ).astype(BF16)

    hand_out(me_ref, g_scr, 0, gk_ref, gs_ref, 0, orders[0], core_bit)
    hand_out(me_ref, g_scr, block_cols // 2, gk_ref, gs_ref, kept, orders[1], core_bit)


def mlp_kernel(orders, core_bit, waits, me_ref, nm_ref, nmT_ref, cot_ref, cotT_ref, *rest):
    left, right, bias_ref, rest = rest[:4], rest[4:8], rest[8], rest[9 + waits :]
    act_ref, dh_ref, dbias_ref, gk_ref, gs_ref, wu_scr, wd_scr, g_scr = rest
    length, width = nm_ref.shape
    up_cols = wu_scr.shape[1]
    kept = gk_ref.shape[0] // 2
    tile = 256
    assemble(me_ref, left, gathered_order(orders[0], core_bit), wu_scr, 0)
    assemble(me_ref, right, gathered_order(orders[1], core_bit), wd_scr, 0)
    dbias_ref[0] = jnp.zeros_like(dbias_ref[0])

    @pl.loop(0, length // tile)
    def _(t):
        rows = pl.ds(pl.multiple_of(t * tile, tile), tile)
        for n in range(0, up_cols, tile):
            hidden = dot_nn(nm_ref[rows, :], wu_scr[:, n : n + tile]) + bias_ref[0, :, n : n + tile]
            d_act = dot_nn(cot_ref[rows, :], wd_scr[:, n : n + tile])
            gate = 0.5 * (1.0 + lax.erf(hidden * (1.0 / math.sqrt(2.0))))
            act_ref[0, rows, n : n + tile] = (hidden * gate).astype(BF16)
            slope = gate + hidden * jnp.exp(-0.5 * hidden * hidden) * (1.0 / math.sqrt(2.0 * math.pi))
            dh = (d_act * slope).astype(BF16)
            dh_ref[0, rows, n : n + tile] = dh
            dbias_ref[0, :, n : n + tile] += jnp.sum(dh.astype(F32), axis=0, keepdims=True)

    for side, lhs, rhs in ((0, nmT_ref, dh_ref), (1, cotT_ref, act_ref)):

        @pl.loop(0, width // tile)
        def _(t):
            rows = pl.ds(pl.multiple_of(t * tile, tile), tile)
            g_scr[rows, :] = dot_nn(lhs[rows, :], rhs[0]).astype(BF16)

        hand_out(me_ref, g_scr, 0, gk_ref, gs_ref, side * kept, orders[side], core_bit)


def weight_spec(array, block_of):
    count, _, rows, cols = array.shape
    return pl.BlockSpec((count, 1, rows, cols), lambda s: (0, block_of(s), 0, 0))


def block_part(kernel, k0, count, orders, core_bit, after, me, norm, norm_t, cot, cot_t, left, right, vectors, mid_cols,
               g_cols, scratch, us):
    length, width = norm.shape
    rows = left[0].shape[2]
    pieces = width // rows
    cols = vectors[0].shape[-1]
    g_spec = pl.BlockSpec((pieces, 1, rows, g_cols), lambda s: (0, s, 0, 0))
    return pl.pallas_call(
        functools.partial(kernel, orders, core_bit, len(after)),
        grid=(count,),
        in_specs=[SCALAR, full(length, width), full(width, length), full(length, width), full(width, length)]
        + [weight_spec(w, lambda s: k0 + s) for w in left + right]
        + [pl.BlockSpec((1, 1, cols), lambda s: (k0 + s, 0, 0))]
        + [full(*v.shape) for v in vectors[1:]]
        + [ANY] * len(after),
        out_specs=[pl.BlockSpec((1, length, m), lambda s: (s, 0, 0)) for m in mid_cols]
        + [pl.BlockSpec((1, 1, cols), lambda s: (s, 0, 0))] + [g_spec] * 2,
        out_shape=[shaped((count, length, m), BF16) for m in mid_cols]
        + [shaped((count, 1, cols), F32)] + [shaped((pieces, count, rows, g_cols), BF16)] * 2,
        scratch_shapes=scratch,
        compiler_params=pltpu.CompilerParams(vmem_limit_bytes=56 * 2**20),
        cost_estimate=cost(us * count),
    )(me, norm, norm_t, cot, cot_t, *left, *right, *vectors, *after)


def pick(refs, per_call, scr):
    for n, ref in enumerate(refs):

        @pl.when(pl.program_id(0) // per_call == n)
        def _():
            scr[...] = ref[0]


def attention_tail_kernel(orders, core_bit, calls, per_call, waits, me_ref, *rest):
    left, right, rest = rest[:4], rest[4:8], rest[8:]
    dqkv_refs, mix_refs, rest = rest[:calls], rest[calls : 2 * calls], rest[2 * calls + waits :]
    branch_ref, dna_ref, w_scr, wv_scr, dqkv_scr, mix_scr = rest
    block_cols = w_scr.shape[1]

    @pl.when(pl.program_id(0) == 0)
    def _():
        branch_ref[...] = jnp.zeros_like(branch_ref)
        dna_ref[...] = jnp.zeros_like(dna_ref)

    pick(dqkv_refs, per_call, dqkv_scr)
    pick(mix_refs, per_call, mix_scr)
    assemble(me_ref, left, gathered_order(orders[0], core_bit), w_scr, 0)
    assemble(me_ref, right, gathered_order(orders[1], core_bit), w_scr, block_cols // 2)
    for i in range(block_cols // HEAD):
        wv_scr[:, i * 2 * HD : (i + 1) * 2 * HD] = w_scr[:, i * HEAD + 2 * HD : (i + 1) * HEAD]
    tile = 256

    @pl.loop(0, branch_ref.shape[0] // tile)
    def _(t):
        rows = pl.ds(pl.multiple_of(t * tile, tile), tile)
        branch_ref[rows, :] += dot_nt(mix_scr[rows, :], wv_scr[...])
        dna_ref[rows, :] += dot_nt(dqkv_scr[rows, :], w_scr[...])


def mlp_tail_kernel(orders, core_bit, calls, per_call, waits, me_ref, *rest):
    left, right, rest = rest[:4], rest[4:8], rest[8:]
    dh_refs, act_refs, rest = rest[:calls], rest[calls : 2 * calls], rest[2 * calls :]
    branch_in, dna_ref, x_ref, cot_ref, ga_ref, gm_ref, bo_ref, bd_ref = rest[:8]
    block_ref, grad_ref, stats_ref, branch_ref, dnm_ref, wu_scr, wd_scr, dh_scr, act_scr = rest[8 + waits :]
    length = x_ref.shape[0]
    step = pl.program_id(0)

    @pl.when(step == 0)
    def _():
        branch_ref[...] = branch_in[...]
        dnm_ref[...] = jnp.zeros_like(dnm_ref)

    pick(dh_refs, per_call, dh_scr)
    pick(act_refs, per_call, act_scr)
    assemble(me_ref, left, gathered_order(orders[0], core_bit), wu_scr, 0)
    assemble(me_ref, right, gathered_order(orders[1], core_bit), wd_scr, 0)
    tile = 256

    @pl.loop(0, length // tile)
    def _(t):
        rows = pl.ds(pl.multiple_of(t * tile, tile), tile)
        branch_ref[rows, :] += dot_nt(act_scr[rows, :], wd_scr[...])
        dnm_ref[rows, :] += dot_nt(dh_scr[rows, :], wu_scr[...])

    @pl.when(step == pl.num_programs(0) - 1)
    def _():
        stats_ref[...] = jnp.zeros_like(stats_ref)
        small = 128

        @pl.loop(0, length // small)
        def _(t):
            rows = pl.ds(pl.multiple_of(t * small, small), small)
            x = x_ref[rows, :].astype(F32)
            cot = cot_ref[rows, :].astype(F32)
            normed, inv_std = normalize(x)
            block_ref[rows, :] = (x + branch_ref[rows, :] + bo_ref[...] + bd_ref[...]).astype(BF16)
            dna, dnm = dna_ref[rows, :], dnm_ref[rows, :]
            d_normed = dna * ga_ref[...] + dnm * gm_ref[...]
            pulled = (
                d_normed
                - jnp.mean(d_normed, axis=1, keepdims=True)
                - normed * jnp.mean(d_normed * normed, axis=1, keepdims=True)
            )
            grad_ref[rows, :] = (cot + inv_std * pulled).astype(BF16)
            for at, term in enumerate((cot, dna * normed, dna, dnm * normed, dnm)):
                stats_ref[at : at + 1, :] += jnp.sum(term, axis=0, keepdims=True)


def tail_part(kernel, block_of, per_call, orders, core_bit, after, me, left, right, mids, extra, outs, scratch, us):
    steps = left[0].shape[1]
    calls = steps // per_call

    def mid_spec(array, n):
        _, length, cols = array.shape
        return pl.BlockSpec((1, length, cols), lambda s: (jnp.clip(s - n * per_call, 0, per_call - 1), 0, 0))

    kept = [pltpu.VMEM(group[0].shape[1:], BF16) for group in mids]
    return pl.pallas_call(
        functools.partial(kernel, orders, core_bit, calls, per_call, len(after)),
        grid=(steps,),
        in_specs=[SCALAR] + [weight_spec(w, block_of) for w in left + right]
        + [mid_spec(array, n) for group in mids for n, array in enumerate(group)]
        + [full(*e.shape) for e in extra] + [ANY] * len(after),
        out_specs=[full(*o.shape) for o in outs],
        out_shape=outs,
        scratch_shapes=scratch + kept,
        compiler_params=pltpu.CompilerParams(vmem_limit_bytes=56 * 2**20),
        cost_estimate=cost(us),
    )(me, *left, *right, *[array for group in mids for array in group], *extra, *after)


def swap(value, bit):
    axis, flip = ("dp", 1) if bit == 1 else ("row", bit // 2)
    return flipped(value, axis, flip)


def flipped(value, axis, flip):
    return lax.ppermute(value, axis, [(i, i ^ flip) for i in range(lax.axis_size(axis))])


def shifted(value, by):
    size = lax.axis_size("col")
    return lax.ppermute(value, "col", [(i, (i + by) % size) for i in range(size)])


def gather_pieces(own, order, core_bit):
    held, steps = own[None], []
    for bit in order[:-1]:
        came = swap(held, bit)
        steps.append(came)
        held = jnp.concatenate([held, came], axis=0)
    came = swap(held, order[-1])
    steps.append(came)
    return [held, came, swap(held, core_bit), swap(came, core_bit)], steps


def add(a, b):
    return (a.astype(F32) + b.astype(F32)).astype(BF16)


def reduce_pieces(keep, send, orders, core_bit):
    came = swap(send, core_bit)
    steps = [[came]] + [[] for _ in orders[0]]
    size = keep.shape[0] // len(orders)
    totals = []
    for side, order in enumerate(orders):
        held, other = keep[side * size : (side + 1) * size], came[side * size : (side + 1) * size]
        for at, bit in enumerate(order):
            half = held.shape[0] // 2
            moved = swap(add(held[half:], other[half:]), bit)
            held, other = add(held[:half], other[:half]), moved
            steps[at + 1].append(moved)
        totals.append(add(held[0], other[0]))
    return jnp.concatenate(totals, axis=2), steps


def all_sum(value):
    for axis in ("row", "dp", "col"):
        flip = 1
        while flip < lax.axis_size(axis):
            value = value + flipped(value, axis, flip)
            flip *= 2
    return value


def on_device(
    tokens_in,
    segment_ids,
    attn_gain,
    attn_shift,
    mlp_gain,
    mlp_shift,
    qkv_weight,
    qkv_bias,
    out_weight,
    out_bias,
    up_weight,
    up_bias,
    down_weight,
    down_bias,
    out_cotangent,
):
    row_size = lax.axis_size("row")
    col_size = lax.axis_size("col")
    length, width = tokens_in.shape
    rows = qkv_weight.shape[0]
    half_rows = rows // 2
    local_heads = qkv_weight.shape[1] // QKV
    block_cols = local_heads * HEAD
    up_cols = up_weight.shape[1]
    row_id = lax.axis_index("row")
    col_id = lax.axis_index("col")
    half = lax.axis_index("dp") % 2
    me = (row_id * 2 + half).reshape(1).astype(jnp.int32)
    row_bits = [2 << i for i in range(row_size.bit_length() - 1)]
    core_bit, far_bits = row_bits[0], row_bits[1:][::-1]
    orders = (far_bits + [1], [1] + far_bits)

    head_weight = jnp.concatenate(
        [qkv_weight.reshape(rows, local_heads, QKV), out_weight.T.reshape(rows, local_heads, HD)], axis=2
    ).reshape(rows, block_cols)
    attn_own = lax.dynamic_slice_in_dim(head_weight, half * half_rows, half_rows, axis=0)
    mlp_own = jnp.concatenate(
        [
            lax.dynamic_slice_in_dim(up_weight, half * half_rows, half_rows, axis=0),
            lax.dynamic_slice_in_dim(down_weight, half * half_rows, half_rows, axis=1).T,
        ],
        axis=1,
    )
    def gather_col(own):
        return jnp.stack([own] + [shifted(own, k) for k in range(1, col_size)])

    attn_all = gather_col(attn_own)
    cut = block_cols // 2
    attn_left, _ = gather_pieces(attn_all[:, :, :cut], orders[0], core_bit)
    attn_right, _ = gather_pieces(attn_all[:, :, cut:], orders[1], core_bit)

    seg_row = lax.dynamic_index_in_dim(segment_ids, row_id * col_size + col_id, axis=0, keepdims=False)
    na, na_t, nm, nm_t, cot_t, keep, ahead, behind, mask, mlp_own = prep_part(
        tokens_in, out_cotangent, [v[None, :] for v in (attn_gain, attn_shift, mlp_gain, mlp_shift)], seg_row,
        mlp_own, attn_all,
    )
    mlp_all = gather_col(mlp_own)
    up, up_steps = gather_pieces(mlp_all[:, :, :up_cols], orders[0], core_bit)
    down, down_steps = gather_pieces(mlp_all[:, :, up_cols:], orders[1], core_bit)
    mlp_steps = [list(pair) for pair in zip(up_steps, down_steps)]

    blocks_here = (col_id - jnp.arange(col_size)) % col_size
    head_bias = jnp.pad(
        qkv_bias.reshape(col_size, local_heads, QKV), ((0, 0), (0, 0), (0, HEAD - QKV))
    ).reshape(col_size, 1, block_cols)
    head_bias = jnp.take(head_bias, blocks_here, axis=0)
    hidden_bias = jnp.take(up_bias.reshape(col_size, 1, up_cols), blocks_here, axis=0)

    per_call = 2
    calls = col_size // per_call
    starts = [k0 for k0 in range(0, col_size, per_call)][::-1]

    def block_of(s):
        return (calls - 1 - s // per_call) * per_call + s % per_call

    attn_calls, attn_sums, attn_steps = [], [], []
    last = []
    for n, k0 in enumerate(starts):
        after = last + ([mlp_all] if n == 0 else mlp_steps[0] if n == 1 else [])
        *mids, d_bias, g_keep, g_send = block_part(
            attention_kernel, k0, per_call, orders, core_bit, after, me, na, na_t, out_cotangent, cot_t,
            attn_left, attn_right, [head_bias, keep, ahead, behind, mask], [block_cols, cut], cut,
            [
                pltpu.VMEM((width, block_cols), BF16), pltpu.VMEM((width, cut), BF16),
                pltpu.VMEM((length, block_cols), F32), pltpu.VMEM((length, cut), BF16),
                pltpu.VMEM((width, block_cols), BF16),
            ],
            11,
        )
        last = [d_bias]
        attn_calls.append(mids + [d_bias])
        total, steps = reduce_pieces(g_keep, g_send, orders, core_bit)
        attn_sums.append(total)
        attn_steps.append(steps)
    branch, d_norm_attn = tail_part(
        attention_tail_kernel, block_of, per_call, orders, core_bit, last + mlp_steps[-1], me, attn_left, attn_right,
        [[c[0] for c in attn_calls], [c[1] for c in attn_calls]], [], [shaped((length, width), F32)] * 2,
        [pltpu.VMEM((width, block_cols), BF16), pltpu.VMEM((width, cut), BF16)], 9,
    )
    mlp_calls, mlp_sums, mlp_moves = [], [], []
    last = [branch]
    for n, k0 in enumerate(starts):
        after = last + attn_steps[0][min(n, len(orders[0]))]
        *mids, d_bias, g_keep, g_send = block_part(
            mlp_kernel, k0, per_call, orders, core_bit, after, me, nm, nm_t, out_cotangent, cot_t,
            up, down, [hidden_bias], [up_cols, up_cols], up_cols,
            [pltpu.VMEM((width, up_cols), BF16)] * 3,
            6,
        )
        last = [d_bias]
        mlp_calls.append(mids + [d_bias])
        total, steps = reduce_pieces(g_keep, g_send, orders, core_bit)
        mlp_sums.append(total)
        mlp_moves.append(steps)
    block_out, in_grad, stats = tail_part(
        mlp_tail_kernel, block_of, per_call, orders, core_bit, last + mlp_moves[0][0], me, up, down,
        [[c[1] for c in mlp_calls], [c[0] for c in mlp_calls]],
        [
            branch, d_norm_attn, tokens_in, out_cotangent, attn_gain[None, :], mlp_gain[None, :], out_bias[None, :],
            down_bias[None, :],
        ],
        [shaped((length, width), BF16)] * 2 + [shaped((8, width), F32)],
        [pltpu.VMEM((length, width), F32)] * 2 + [pltpu.VMEM((width, up_cols), BF16)] * 2, 13,
    )

    def settle(parts):
        total = None
        for both, k0 in zip(parts, starts):
            for i in range(per_call):
                k = k0 + i
                term = (both[i] if k == 0 else shifted(both[i], -k)).astype(F32)
                total = term if total is None else total + term
        flip = 2
        while flip < lax.axis_size("dp"):
            total = total + flipped(total, "dp", flip)
            flip *= 2
        mine = total.astype(BF16)
        other = swap(mine, 1)
        first = half == 0
        return jnp.concatenate([jnp.where(first, mine, other), jnp.where(first, other, mine)], axis=0).astype(F32)

    g_heads = settle(attn_sums).reshape(rows, local_heads, HEAD)
    g_mlp = settle(mlp_sums)

    d_bias_up = jnp.take(jnp.concatenate([c[2] for c in mlp_calls[::-1]]), blocks_here, axis=0)
    d_bias_attn = jnp.take(jnp.concatenate([c[2] for c in attn_calls[::-1]]), blocks_here, axis=0)
    smalls = jnp.concatenate(
        [
            stats[:5].reshape(-1),
            d_bias_up.reshape(-1),
            d_bias_attn.reshape(col_size * local_heads, HEAD)[:, :QKV].reshape(-1),
        ]
    )
    smalls = all_sum(smalls.reshape(-1, 128)).reshape(-1)
    stats = smalls[: 5 * width].reshape(5, width)
    grad_up_bias = smalls[5 * width : 5 * width + up_bias.shape[0]]
    grad_qkv_bias = smalls[5 * width + up_bias.shape[0] :]
    return (
        block_out,
        in_grad,
        stats[1],
        stats[2],
        stats[3],
        stats[4],
        g_heads[:, :, :QKV].reshape(rows, local_heads * QKV),
        grad_qkv_bias,
        g_heads[:, :, QKV:].reshape(rows, local_heads * HD).T,
        stats[0],
        g_mlp[:, :up_cols],
        grad_up_bias,
        g_mlp[:, up_cols:].T,
        stats[0],
    )


def solution(mesh):
    return jax.shard_map(
        on_device,
        mesh=mesh,
        in_specs=(
            P(("dp", "row", "col"), None),
            P("dp", None),
            P(),
            P(),
            P(),
            P(),
            P("row", "col"),
            P(),
            P("col", "row"),
            P(),
            P("row", "col"),
            P(),
            P("col", "row"),
            P(),
            P(("dp", "row", "col"), None),
        ),
        out_specs=(
            P(("dp", "row", "col"), None),
            P(("dp", "row", "col"), None),
            P(),
            P(),
            P(),
            P(),
            P("row", "col"),
            P(),
            P("col", "row"),
            P(),
            P("row", "col"),
            P(),
            P("col", "row"),
            P(),
        ),
        check_vma=False,
    )
```

time: 359 us -> 314 us (0.87)
  waiting for transfers between devices: 125 us -> 98.1 us
  Pallas kernels: 119 us -> 99.9 us
  starting transfers between devices: 70.6 us -> 57.2 us
  other arithmetic: 14.1 us -> 27.1 us
    ppermute x59 -> x43, waiting for transfers between devices: 89.5 us -> 58.8 us  [flipped(): lax.ppermute(value, axis, [(i, i ^ flip) for i in range(lax.axis_size(axi...]
    pallas_call x4, Pallas kernels: 88.8 us -> 68.8 us  [block_part(): pl.pallas_call(functools.partial(kernel, orders, core_bit, len(after)), g...]
    ppermute x59 -> x43, starting transfers between devices: 46.3 us -> 38.6 us  [flipped(): lax.ppermute(value, axis, [(i, i ^ flip) for i in range(lax.axis_size(axi...]
    convert_element_type x24 -> x20, other arithmetic: 8.08 us -> 14 us  [add(): return (a.astype(F32) + b.astype(F32)).astype(BF16)]
    ppermute x12, starting transfers between devices: 24.3 us -> 18.6 us  [shifted(): lax.ppermute(value, 'col', [(i, (i + by) % size) for i in range(size)])]
    concatenate x2 -> x7, other arithmetic: 0.72 us -> 4.87 us  [the longest x4 3.44 us: gather_pieces(): held = jnp.concatenate([held, came], axis=0)]
    unnamed x152 -> x110, local copies, waits for them, and re-layouts: 13.5 us -> 14.4 us
  transfers between devices with their start and end apart: 71 -> 55, of which waited for: 22 -> 16; matrix products, arithmetic and copies ran while one was open for 6% -> 12% of each run, Pallas kernels for 33% -> 25%
where the time goes in v3:
time: 314 us; the launch traced here: 311 us
  Pallas kernels  99.9 us (32%)
  waiting for transfers between devices  98.1 us (31%)
  starting transfers between devices  57.2 us (18%)
  local copies, waits for them, and re-layouts  27.6 us (9%)
  other arithmetic  27.1 us (9%)
    pallas_call x4, Pallas kernels, block_part(): pl.pallas_call(functools.partial(kernel, orders, core_bit, len(after)), g...  68.8 us
    ppermute x43, waiting for transfers between devices, flipped(): lax.ppermute(value, axis, [(i, i ^ flip) for i in range(lax.axis_size(axi...  58.8 us
    ppermute x12, waiting for transfers between devices, shifted(): lax.ppermute(value, 'col', [(i, (i + by) % size) for i in range(size)])  39.3 us
    ppermute x43, starting transfers between devices, flipped(): lax.ppermute(value, axis, [(i, i ^ flip) for i in range(lax.axis_size(axi...  38.6 us
    pallas_call x2, Pallas kernels, tail_part(): pl.pallas_call(functools.partial(kernel, orders, core_bit, calls, per_cal...  26.7 us
    ppermute x12, starting transfers between devices, shifted(): lax.ppermute(value, 'col', [(i, (i + by) % size) for i in range(size)])  18.6 us
    unnamed x110, local copies, waits for them, and re-layouts  14.4 us
    convert_element_type x20, other arithmetic, add(): return (a.astype(F32) + b.astype(F32)).astype(BF16)  14 us
  transfers between devices with their start and end apart: 55, of which 16 were waited for; matrix products, arithmetic and copies ran while one was open for 12% of the time, Pallas kernels for 25%

profile of v3, /device:TPU:0, one launch (start us, length us, event | category | flops | bytes accessed | tf_op | source)
XLA Modules:
  0.0 311.5 jit_solution(11867617618207136681)
XLA Ops:
  3.1 5.1 %collective-permute-start.2 = (bf16[96,768]{1,0:T(8,128)(2,1)S(1)}, bf16[96,768]{1,0:T(8,128)(2,1)S(1)}, u32[]{:S(2)}, u32[]{:S(2)}) collective-permute-start(bf16[96,768]{1,0:T(8,128)(2,1)S(1)} %copy.47), channel_id=1, source_target_pairs={{0,3},{1,0},{2,1},{3,2},{4,7},{5,4},{6,5},{7,6},{8,11},{9,8},{10,9... | collective-permute-start | bytes 442376 | tf_op jit(solution)/shard_map/ppermute | solution.py:400
  9.4 3.1 collective-permute-done.2
  12.5 8.2 %collective-permute-done.1 = bf16[96,768]{1,0:T(8,128)(2,1)S(1)} collective-permute-done((bf16[96,768]{1,0:T(8,128)(2,1)S(1)}, bf16[96,768]{1,0:T(8,128)(2,1)S(1)}, u32[]{:S(2)}, u32[]{:S(2)}) %collective-permute-start.1) | collective-permute-done | bytes 147488 | tf_op jit(solution)/shard_map/ppermute | solution.py:400
  20.9 1.6 collective-permute-start.14
  23.2 1.5 collective-permute-start.18
  25.7 3.5 %collective-permute-done.14 = bf16[1,4,96,384]{3,2,1,0:T(8,128)(2,1)S(1)} collective-permute-done((bf16[1,4,96,384]{3,2,1,0:T(8,128)(2,1)S(1)}, bf16[1,4,96,384]{3,2,1,0:T(8,128)(2,1)S(1)}, u32[]{:S(2)}, u32[]{:S(2)}) %collective-permute-start.14) | collective-permute-done | bytes 294944 | tf_op jit(solution)/shard_map/ppermute | solution.py:395
  29.3 1.6 collective-permute-start.15
  32.6 4.5 %shard_map.254 = (bf16[512,768]{1,0:T(8,128)(2,1)S(1)}, bf16[768,512]{1,0:T(8,128)(2,1)S(1)}, bf16[512,768]{1,0:T(8,128)(2,1)S(1)}, bf16[768,512]{1,0:T(8,128)(2...) custom-call(bf16[512,768]{1,0:T(8,128)(2,1)} %rest_14_.1, ...), custom_call_target="tpu_custom_call", output_to_operand_aliasing={{9}: (9, {})} | custom-call | flops 6899999744 | bytes 1048576 | tf_op jit(solution)/shard_map/pallas_call | solution.py:121
  44.6 1.6 collective-permute-start.4
  47.4 2.3 collective-permute-start.3
  49.6 2.4 collective-permute-done.5
  52.1 18.0 %collective-permute-done.4 = bf16[96,1536]{1,0:T(8,128)(2,1)S(1)} collective-permute-done((bf16[96,1536]{1,0:T(8,128)(2,1)S(1)}, bf16[96,1536]{1,0:T(8,128)(2,1)S(1)}, u32[]{:S(2)}, u32[]{:S(2)}) %collective-permute-start.4) | collective-permute-done | bytes 294944 | tf_op jit(solution)/shard_map/ppermute | solution.py:400
  73.4 1.5 collective-permute-start.6
  74.9 21.1 %shard_map.255 = (bf16[2,512,768]{2,1,0:T(8,128)(2,1)}, bf16[2,512,384]{2,1,0:T(8,128)(2,1)}, f32[2,1,768]{2,1,0:T(1,128)}, bf16[8,2,96,384]{3,2,1,0:T(8,128)(2,1)}, bf16[8,2,96,384]{3,2,1,0:T(8,128)(2,1)}) custom-call(s32[1]{0:T(128)} %bitcast.me_ref, bf16[512,768]{1,0:T(8,128)(2,1)} %copy-done.7, bf16[768,512]{1,0:T(8,128)(2,1)} %copy-done.8, ...), custom_call_target="tpu_custom_call" | custom-call | flops 25300000768 | bytes 1048576 | tf_op jit(solution)/shard_map/pallas_call | solution.py:265
  97.0 21.0 %shard_map.256 = (bf16[2,512,768]{2,1,0:T(8,128)(2,1)}, bf16[2,512,384]{2,1,0:T(8,128)(2,1)}, f32[2,1,768]{2,1,0:T(1,128)}, bf16[8,2,96,384]{3,2,1,0:T(8,128)(2,1)}, bf16[8,2,96,384]{3,2,1,0:T(8,128)(2,1)}) custom-call(s32[1]{0:T(128)} %bitcast.me_ref, bf16[512,768]{1,0:T(8,128)(2,1)} %copy-done.7, bf16[768,512]{1,0:T(8,128)(2,1)} %copy-done.8, ...), custom_call_target="tpu_custom_call" | custom-call | flops 25300000768 | bytes 1048576 | tf_op jit(solution)/shard_map/pallas_call | solution.py:265
  118.6 2.2 pad_maximum_fusion.1.rest_0_
  124.2 1.3 broadcast_in_dim.56.rest_19_
  129.7 20.3 %collective-permute-done.7.rest_13_.rest_1_ = bf16[2,4,96,768]{3,2,1,0:T(8,128)(2,1)} collective-permute-done((bf16[2,4,96,768]{3,2,1,0:T(8,128)(2,1)}, bf16[2,4,96,768]{3,2,1,0:T(8,128)(2,1)}, u32[]{:S(2)}, u32[]{:S(2)}) %collective-permute-start.7) | collective-permute-done | bytes 1179680 | tf_op jit(solution)/shard_map/ppermute | solution.py:395
  150.7 1.5 collective-permute-start.24
  152.2 11.2 %shard_map.257 = (f32[512,768]{1,0:T(8,128)}, f32[512,768]{1,0:T(8,128)}) custom-call(s32[1]{0:T(128)} %bitcast.me_ref, bf16[2,4,96,384]{3,2,1,0:T(8,128)(2,1)} %copy-done.23, bf16[2,4,96,384]{3,2,1,0:T(8,128)(2,1)} %collective-permute-done.15.rest_1_, bf16[2,4,96,384]{3,2,1,0:T(8,128)(2,1)} %copy-done.50, ...), custom_call_target="tpu_custom_call" | custom-call | flops 10350000128 | bytes 1048576 | tf_op jit(solution)/shard_map/pallas_call | solution.py:375
  164.8 8.3 %collective-permute-done.23.rest_10_ = bf16[2,2,96,384]{3,2,1,0:T(8,128)(2,1)S(1)} collective-permute-done((bf16[2,2,96,384]{3,2,1,0:T(8,128)(2,1)S(1)}, bf16[2,2,96,384]{3,2,1,0:T(8,128)(2,1)S(1)}, u32[]{:S(2)}, u32[]{:S(2)}) %collective-permute-start.23) | collective-permute-done | bytes 294944 | tf_op jit(solution)/shard_map/ppermute | solution.py:395
  173.7 4.5 %collective-permute-done.39 = bf16[1,2,96,384]{3,2,1,0:T(8,128)(2,1)S(1)} collective-permute-done((bf16[1,2,96,384]{3,2,1,0:T(8,128)(2,1)S(1)}, bf16[1,2,96,384]{3,2,1,0:T(8,128)(2,1)S(1)}, u32[]{:S(2)}, u32[]{:S(2)}) %collective-permute-start.39) | collective-permute-done | bytes 147488 | tf_op jit(solution)/shard_map/ppermute | solution.py:395
  178.8 1.4 collective-permute-start.32
  182.4 13.3 %shard_map.258 = (bf16[2,512,768]{2,1,0:T(8,128)(2,1)}, bf16[2,512,768]{2,1,0:T(8,128)(2,1)}, f32[2,1,768]{2,1,0:T(1,128)}, bf16[8,2,96,768]{3,2,1,0:T(8,128)(2,1)}, bf16[8,2,96,768]{3,2,1,0:T(8,128)(2,1)}) custom-call(s32[1]{0:T(128)} %bitcast.me_ref, bf16[512,768]{1,0:T(8,128)(2,1)} %copy-done.4, bf16[768,512]{1,0:T(8,128)(2,1)} %copy-done.5, ...), custom_call_target="tpu_custom_call" | custom-call | flops 13799999488 | bytes 1048576 | tf_op jit(solution)/shard_map/pallas_call | solution.py:265
  197.5 2.0 collective-permute-start.34
  199.5 13.4 %shard_map.259 = (bf16[2,512,768]{2,1,0:T(8,128)(2,1)}, bf16[2,512,768]{2,1,0:T(8,128)(2,1)}, f32[2,1,768]{2,1,0:T(1,128)}, bf16[8,2,96,768]{3,2,1,0:T(8,128)(2,1)}, bf16[8,2,96,768]{3,2,1,0:T(8,128)(2,1)}) custom-call(s32[1]{0:T(128)} %bitcast.me_ref, bf16[512,768]{1,0:T(8,128)(2,1)} %copy-done.4, bf16[768,512]{1,0:T(8,128)(2,1)} %copy-done.5, ...), custom_call_target="tpu_custom_call" | custom-call | flops 13799999488 | bytes 1048576 | tf_op jit(solution)/shard_map/pallas_call | solution.py:265
  215.6 1.5 copy-done.14
  217.1 15.5 %shard_map.260 = (bf16[512,768]{1,0:T(8,128)(2,1)}, bf16[512,768]{1,0:T(8,128)(2,1)}, f32[8,768]{1,0:T(8,128)}) custom-call(s32[1]{0:T(128)} %bitcast.me_ref, bf16[2,4,96,768]{3,2,1,0:T(8,128)(2,1)} %pad_maximum_fusion.1.rest_0_, bf16[2,4,96,768]{3,2,1,0:T(8,128)(2,1)} %collective-permute-done.7.rest_13_.rest_1_, ...), custom_call_target="tpu_custom_call" | custom-call | flops 14949999616 | bytes 1048576 | tf_op jit(solution)/shard_map/pallas_call | solution.py:375
  235.1 1.3 collective-permute-start.41
  237.2 3.4 %add_convert_fusion.7 = (bf16[2,2,96,768]{3,2,1,0:T(8,128)(2,1)S(1)}, bf16[2,2,96,768]{3,2,1,0:T(8,128)(2,1)}, bf16[2,2,96,768]{3,2,1,0:T(8,128)(2,1)S(1)}, bf16[2,2,96,768]{3,2,1,0:T(8,128)(2,1)}) fusion(bf16[8,2,96,768]{3,2,1,0:T(8,128)(2,1)} %copy-done.14, bf16[8,2,96,768]{3,2,1,0:T(8,128)(2,1)S(1)} %copy-done.13), kind=kLoop, calls=%fused_computation.14 | loop fusion | flops 4718592 | bytes 7077888 | tf_op jit(solution)/shard_map/convert_element_type | solution.py:415
  240.6 1.5 collective-permute-start.44
  244.0 3.1 add_convert_fusion.3
  248.0 9.9 %collective-permute-done.28 = f32[72,128]{1,0:T(8,128)S(1)} collective-permute-done((f32[72,128]{1,0:T(8,128)S(1)}, f32[72,128]{1,0:T(8,128)S(1)}, u32[]{:S(2)}, u32[]{:S(2)}) %collective-permute-start.28) | collective-permute-done | bytes 36896 | tf_op jit(solution)/shard_map/ppermute | solution.py:395
  257.9 1.5 collective-permute-start.29
  259.5 1.4 collective-permute-start.49
  261.9 1.4 add.228
  263.3 3.0 collective-permute-start.30
  267.4 1.4 collective-permute-start.45
  271.7 1.5 collective-permute-start.52
  273.2 2.7 collective-permute-done.49
  275.9 1.6 collective-permute-start.50
  277.5 3.6 %collective-permute-done.45 = bf16[1,2,96,768]{3,2,1,0:T(8,128)(2,1)S(1)} collective-permute-done((bf16[1,2,96,768]{3,2,1,0:T(8,128)(2,1)S(1)}, bf16[1,2,96,768]{3,2,1,0:T(8,128)(2,1)S(1)}, u32[]{:S(2)}, u32[]{:S(2)}) %collective-permute-start.45) | collective-permute-done | bytes 294944 | tf_op jit(solution)/shard_map/ppermute | solution.py:395
  284.2 1.8 collective-permute-start.46
  285.9 1.7 collective-permute-start.47
  288.9 2.2 collective-permute-start.53
  295.1 6.5 %collective-permute-done.46 = bf16[96,1536]{1,0:T(8,128)(2,1)S(1)} collective-permute-done((bf16[96,1536]{1,0:T(8,128)(2,1)}, bf16[96,1536]{1,0:T(8,128)(2,1)S(1)}, u32[]{:S(2)}, u32[]{:S(2)}) %collective-permute-start.46) | collective-permute-done | bytes 294944 | tf_op jit(solution)/shard_map/ppermute | solution.py:400
  302.8 1.6 collective-permute-start.54
  305.6 4.0 %collective-permute-done.54 = bf16[96,1536]{1,0:T(8,128)(2,1)S(1)} collective-permute-done((bf16[96,1536]{1,0:T(8,128)(2,1)S(1)}, bf16[96,1536]{1,0:T(8,128)(2,1)S(1)}, u32[]{:S(2)}, u32[]{:S(2)}) %collective-permute-start.54) | collective-permute-done | bytes 294944 | tf_op jit(solution)/shard_map/ppermute | solution.py:395
  (264 shorter events, 61.9 us)
Async XLA Ops:
  3.1 9.4 %collective-permute-start.2 = (bf16[96,768]{1,0:T(8,128)(2,1)S(1)}, bf16[96,768]{1,0:T(8,128)(2,1)S(1)}, u32[]{:S(2)}, u32[]{:S(2)}) collective-permute-start(bf16[96,768]{1,0:T(8,128)(2,1)S(1)} %copy.47), channel_id=1, source_target_pairs={{0,3},{1,0},{2,1},{3,2},{4,7},{5,4},{6,5},{7,6},{8,11},{9,8},{10,9... | collective-permute-start | bytes 442376 | tf_op jit(solution)/shard_map/ppermute | solution.py:400
  8.2 12.5 %collective-permute-start.1 = (bf16[96,768]{1,0:T(8,128)(2,1)S(1)}, bf16[96,768]{1,0:T(8,128)(2,1)S(1)}, u32[]{:S(2)}, u32[]{:S(2)}) collective-permute-start(bf16[96,768]{1,0:T(8,128)(2,1)S(1)} %copy.47), channel_id=1, source_target_pairs={{0,2},{1,3},{2,0},{3,1},{4,6},{5,7},{6,4},{7,5},{8,10},{9,11},{10,... | collective-permute-start | bytes 442376 | tf_op jit(solution)/shard_map/ppermute | solution.py:400
  8.2 12.5 %collective-permute-start = (bf16[96,768]{1,0:T(8,128)(2,1)S(1)}, bf16[96,768]{1,0:T(8,128)(2,1)S(1)}, u32[]{:S(2)}, u32[]{:S(2)}) collective-permute-start(bf16[96,768]{1,0:T(8,128)(2,1)S(1)} %copy.47), channel_id=1, source_target_pairs={{0,1},{1,2},{2,3},{3,0},{4,5},{5,6},{6,7},{7,4},{8,9},{9,10},{10,1... | collective-permute-start | bytes 442376 | tf_op jit(solution)/shard_map/ppermute | solution.py:400
  20.9 8.4 %collective-permute-start.14 = (bf16[1,4,96,384]{3,2,1,0:T(8,128)(2,1)S(1)}, bf16[1,4,96,384]{3,2,1,0:T(8,128)(2,1)S(1)}, u32[]{:S(2)}, u32[]{:S(2)}) collective-permute-start(bf16[1,4,96,384]{3,2,1,0:T(8,128)(2,1)S(1)} %get-tuple-element.138), channel_id=1, source_target_pairs={{0,8},{4,12},{8,0},{12,4},{1,9},{5,13},{9,1},{13,5},{2,10},{6,14},... | collective-permute-start | bytes 884744 | tf_op jit(solution)/shard_map/ppermute | solution.py:395
  23.2 8.7 %collective-permute-start.18 = (bf16[1,4,96,384]{3,2,1,0:T(8,128)(2,1)S(1)}, bf16[1,4,96,384]{3,2,1,0:T(8,128)(2,1)S(1)}, u32[]{:S(2)}, u32[]{:S(2)}) collective-permute-start(bf16[1,4,96,384]{3,2,1,0:T(8,128)(2,1)S(1)} %get-tuple-element.137), channel_id=1, source_target_pairs={{0,16},{16,0},{1,17},{17,1},{2,18},{18,2},{3,19},{19,3},{4,20},{20... | collective-permute-start | bytes 884744 | tf_op jit(solution)/shard_map/ppermute | solution.py:395
  29.3 40.8 %collective-permute-start.15 = (bf16[2,4,96,384]{3,2,1,0:T(8,128)(2,1)S(1)}, bf16[2,4,96,384]{3,2,1,0:T(8,128)(2,1)}, u32[]{:S(2)}, u32[]{:S(2)}) collective-permute-start(bf16[2,4,96,384]{3,2,1,0:T(8,128)(2,1)S(1)} %pad_maximum_fusion.4.rest_0_), channel_id=1, source_target_pairs={{0,16},{16,0},{1,17},{17,1},{2,18},{18,2},{3,19},{19,3},{4,20},{20... | collective-permute-start | bytes 1769480 | tf_op jit(solution)/shard_map/ppermute | solution.py:395
  31.9 38.7 %collective-permute-start.19 = (bf16[2,4,96,384]{3,2,1,0:T(8,128)(2,1)S(1)}, bf16[2,4,96,384]{3,2,1,0:T(8,128)(2,1)}, u32[]{:S(2)}, u32[]{:S(2)}) collective-permute-start(bf16[2,4,96,384]{3,2,1,0:T(8,128)(2,1)S(1)} %pad_maximum_fusion.5.rest_4_), channel_id=1, source_target_pairs={{0,8},{4,12},{8,0},{12,4},{1,9},{5,13},{9,1},{13,5},{2,10},{6,14},... | collective-permute-start | bytes 1769480 | tf_op jit(solution)/shard_map/ppermute | solution.py:395
  43.6 8.5 %collective-permute-start.5 = (bf16[96,1536]{1,0:T(8,128)(2,1)S(1)}, bf16[96,1536]{1,0:T(8,128)(2,1)S(1)}, u32[]{:S(2)}, u32[]{:S(2)}) collective-permute-start(bf16[96,1536]{1,0:T(8,128)(2,1)S(1)} %get-tuple-element.50), channel_id=1, source_target_pairs={{0,3},{1,0},{2,1},{3,2},{4,7},{5,4},{6,5},{7,6},{8,11},{9,8},{10,9... | collective-permute-start | bytes 884744 | tf_op jit(solution)/shard_map/ppermute | solution.py:400
  44.6 25.5 %collective-permute-start.4 = (bf16[96,1536]{1,0:T(8,128)(2,1)S(1)}, bf16[96,1536]{1,0:T(8,128)(2,1)S(1)}, u32[]{:S(2)}, u32[]{:S(2)}) collective-permute-start(bf16[96,1536]{1,0:T(8,128)(2,1)S(1)} %get-tuple-element.50), channel_id=1, source_target_pairs={{0,2},{1,3},{2,0},{3,1},{4,6},{5,7},{6,4},{7,5},{8,10},{9,11},{10,... | collective-permute-start | bytes 884744 | tf_op jit(solution)/shard_map/ppermute | solution.py:400
  47.4 24.0 %collective-permute-start.3 = (bf16[96,1536]{1,0:T(8,128)(2,1)S(1)}, bf16[96,1536]{1,0:T(8,128)(2,1)S(1)}, u32[]{:S(2)}, u32[]{:S(2)}) collective-permute-start(bf16[96,1536]{1,0:T(8,128)(2,1)S(1)} %get-tuple-element.50), channel_id=1, source_target_pairs={{0,1},{1,2},{2,3},{3,0},{4,5},{5,6},{6,7},{7,4},{8,9},{9,10},{10,1... | collective-permute-start | bytes 884744 | tf_op jit(solution)/shard_map/ppermute | solution.py:400
  52.1 21.3 %collective-permute-start.16 = (bf16[2,4,96,384]{3,2,1,0:T(8,128)(2,1)S(1)}, bf16[2,4,96,384]{3,2,1,0:T(8,128)(2,1)S(1)}, u32[]{:S(2)}, u32[]{:S(2)}) collective-permute-start(bf16[2,4,96,384]{3,2,1,0:T(8,128)(2,1)S(1)} %pad_maximum_fusion.4.rest_0_), channel_id=1, source_target_pairs={{0,4},{4,0},{8,12},{12,8},{1,5},{5,1},{9,13},{13,9},{2,6},{6,2},{1... | collective-permute-start | bytes 1769480 | tf_op jit(solution)/shard_map/ppermute | solution.py:395
  72.6 23.4 %collective-permute-start.10 = (bf16[1,4,96,768]{3,2,1,0:T(8,128)(2,1)S(1)}, bf16[1,4,96,768]{3,2,1,0:T(8,128)(2,1)S(1)}, u32[]{:S(2)}, u32[]{:S(2)}) collective-permute-start(bf16[1,4,96,768]{3,2,1,0:T(8,128)(2,1)S(1)} %get-tuple-element.131), channel_id=1, source_target_pairs={{0,16},{16,0},{1,17},{17,1},{2,18},{18,2},{3,19},{19,3},{4,20},{20... | collective-permute-start | bytes 1769480 | tf_op jit(solution)/shard_map/ppermute | solution.py:395
  73.4 22.6 %collective-permute-start.6 = (bf16[1,4,96,768]{3,2,1,0:T(8,128)(2,1)S(1)}, bf16[1,4,96,768]{3,2,1,0:T(8,128)(2,1)S(1)}, u32[]{:S(2)}, u32[]{:S(2)}) collective-permute-start(bf16[1,4,96,768]{3,2,1,0:T(8,128)(2,1)S(1)} %get-tuple-element.132), channel_id=1, source_target_pairs={{0,8},{4,12},{8,0},{12,4},{1,9},{5,13},{9,1},{13,5},{2,10},{6,14},... | collective-permute-start | bytes 1769480 | tf_op jit(solution)/shard_map/ppermute | solution.py:395
  118.0 9.4 %collective-permute-start.35 = (bf16[8,2,96,384]{3,2,1,0:T(8,128)(2,1)}, bf16[8,2,96,384]{3,2,1,0:T(8,128)(2,1)S(1)}, u32[]{:S(2)}, u32[]{:S(2)}) collective-permute-start(bf16[8,2,96,384]{3,2,1,0:T(8,128)(2,1)} %get-tuple-element.81), channel_id=1, source_target_pairs={{0,4},{4,0},{8,12},{12,8},{1,5},{5,1},{9,13},{13,9},{2,6},{6,2},{1... | collective-permute-start | bytes 3538952 | tf_op jit(solution)/shard_map/ppermute | solution.py:395
  118.1 10.1 %collective-permute-start.22 = (bf16[8,2,96,384]{3,2,1,0:T(8,128)(2,1)}, bf16[8,2,96,384]{3,2,1,0:T(8,128)(2,1)S(1)}, u32[]{:S(2)}, u32[]{:S(2)}) collective-permute-start(bf16[8,2,96,384]{3,2,1,0:T(8,128)(2,1)} %get-tuple-element.67), channel_id=1, source_target_pairs={{0,4},{4,0},{8,12},{12,8},{1,5},{5,1},{9,13},{13,9},{2,6},{6,2},{1... | collective-permute-start | bytes 3538952 | tf_op jit(solution)/shard_map/ppermute | solution.py:395
  120.8 29.1 %collective-permute-start.7 = (bf16[2,4,96,768]{3,2,1,0:T(8,128)(2,1)}, bf16[2,4,96,768]{3,2,1,0:T(8,128)(2,1)}, u32[]{:S(2)}, u32[]{:S(2)}) collective-permute-start(bf16[2,4,96,768]{3,2,1,0:T(8,128)(2,1)} %pad_maximum_fusion.1.rest_0_), channel_id=1, source_target_pairs={{0,16},{16,0},{1,17},{17,1},{2,18},{18,2},{3,19},{19,3},{4,20},{20... | collective-permute-start | bytes 3538952 | tf_op jit(solution)/shard_map/ppermute | solution.py:395
  122.4 28.3 %collective-permute-start.11 = (bf16[2,4,96,768]{3,2,1,0:T(8,128)(2,1)}, bf16[2,4,96,768]{3,2,1,0:T(8,128)(2,1)}, u32[]{:S(2)}, u32[]{:S(2)}) collective-permute-start(bf16[2,4,96,768]{3,2,1,0:T(8,128)(2,1)} %pad_maximum_fusion.2.rest_4_), channel_id=1, source_target_pairs={{0,8},{4,12},{8,0},{12,4},{1,9},{5,13},{9,1},{13,5},{2,10},{6,14},... | collective-permute-start | bytes 3538952 | tf_op jit(solution)/shard_map/ppermute | solution.py:395
  125.5 53.3 %collective-permute-start.8 = (bf16[2,4,96,768]{3,2,1,0:T(8,128)(2,1)}, bf16[2,4,96,768]{3,2,1,0:T(8,128)(2,1)}, u32[]{:S(2)}, u32[]{:S(2)}) collective-permute-start(bf16[2,4,96,768]{3,2,1,0:T(8,128)(2,1)} %pad_maximum_fusion.1.rest_0_), channel_id=1, source_target_pairs={{0,4},{4,0},{8,12},{12,8},{1,5},{5,1},{9,13},{13,9},{2,6},{6,2},{1... | collective-permute-start | bytes 3538952 | tf_op jit(solution)/shard_map/ppermute | solution.py:395
  127.4 52.8 %collective-permute-start.12 = (bf16[2,4,96,768]{3,2,1,0:T(8,128)(2,1)}, bf16[2,4,96,768]{3,2,1,0:T(8,128)(2,1)}, u32[]{:S(2)}, u32[]{:S(2)}) collective-permute-start(bf16[2,4,96,768]{3,2,1,0:T(8,128)(2,1)} %pad_maximum_fusion.2.rest_4_), channel_id=1, source_target_pairs={{0,4},{4,0},{8,12},{12,8},{1,5},{5,1},{9,13},{13,9},{2,6},{6,2},{1... | collective-permute-start | bytes 3538952 | tf_op jit(solution)/shard_map/ppermute | solution.py:395
  128.2 35.2 %collective-permute-start.38 = (bf16[2,2,96,384]{3,2,1,0:T(8,128)(2,1)S(1)}, bf16[2,2,96,384]{3,2,1,0:T(8,128)(2,1)S(1)}, u32[]{:S(2)}, u32[]{:S(2)}) collective-permute-start(bf16[2,2,96,384]{3,2,1,0:T(8,128)(2,1)S(1)} %get-tuple-element.126), channel_id=1, source_target_pairs={{0,16},{16,0},{1,17},{17,1},{2,18},{18,2},{3,19},{19,3},{4,20},{20... | collective-permute-start | bytes 884744 | tf_op jit(solution)/shard_map/ppermute | solution.py:395
  149.9 13.5 %collective-permute-start.36 = (bf16[2,2,96,384]{3,2,1,0:T(8,128)(2,1)S(1)}, bf16[2,2,96,384]{3,2,1,0:T(8,128)(2,1)S(1)}, u32[]{:S(2)}, u32[]{:S(2)}) collective-permute-start(bf16[2,2,96,384]{3,2,1,0:T(8,128)(2,1)S(1)} %get-tuple-element.128), channel_id=1, source_target_pairs={{0,8},{4,12},{8,0},{12,4},{1,9},{5,13},{9,1},{13,5},{2,10},{6,14},... | collective-permute-start | bytes 884744 | tf_op jit(solution)/shard_map/ppermute | solution.py:395
  150.7 13.3 %collective-permute-start.24 = (bf16[2,2,96,384]{3,2,1,0:T(8,128)(2,1)S(1)}, bf16[2,2,96,384]{3,2,1,0:T(8,128)(2,1)S(1)}, u32[]{:S(2)}, u32[]{:S(2)}) collective-permute-start(bf16[2,2,96,384]{3,2,1,0:T(8,128)(2,1)S(1)} %get-tuple-element.123), channel_id=1, source_target_pairs={{0,16},{16,0},{1,17},{17,1},{2,18},{18,2},{3,19},{19,3},{4,20},{20... | collective-permute-start | bytes 884744 | tf_op jit(solution)/shard_map/ppermute | solution.py:395
  163.4 17.6 %collective-permute-start.9 = (bf16[2,4,96,768]{3,2,1,0:T(8,128)(2,1)}, bf16[2,4,96,768]{3,2,1,0:T(8,128)(2,1)S(1)}, u32[]{:S(2)}, u32[]{:S(2)}) collective-permute-start(bf16[2,4,96,768]{3,2,1,0:T(8,128)(2,1)} %collective-permute-done.7.rest_13_.rest_1_), channel_id=1, source_target_pairs={{0,4},{4,0},{8,12},{12,8},{1,5},{5,1},{9,13},{13,9},{2,6},{6,2},{1... | collective-permute-start | bytes 3538952 | tf_op jit(solution)/shard_map/ppermute | solution.py:395
  163.5 17.6 %collective-permute-start.13 = (bf16[2,4,96,768]{3,2,1,0:T(8,128)(2,1)}, bf16[2,4,96,768]{3,2,1,0:T(8,128)(2,1)S(1)}, u32[]{:S(2)}, u32[]{:S(2)}) collective-permute-start(bf16[2,4,96,768]{3,2,1,0:T(8,128)(2,1)} %collective-permute-done.11.rest_14_.rest_5_), channel_id=1, source_target_pairs={{0,4},{4,0},{8,12},{12,8},{1,5},{5,1},{9,13},{13,9},{2,6},{6,2},{1... | collective-permute-start | bytes 3538952 | tf_op jit(solution)/shard_map/ppermute | solution.py:395
  164.0 9.1 %collective-permute-start.23 = (bf16[2,2,96,384]{3,2,1,0:T(8,128)(2,1)S(1)}, bf16[2,2,96,384]{3,2,1,0:T(8,128)(2,1)S(1)}, u32[]{:S(2)}, u32[]{:S(2)}) collective-permute-start(bf16[2,2,96,384]{3,2,1,0:T(8,128)(2,1)S(1)} %get-tuple-element.124), channel_id=1, source_target_pairs={{0,8},{4,12},{8,0},{12,4},{1,9},{5,13},{9,1},{13,5},{2,10},{6,14},... | collective-permute-start | bytes 884744 | tf_op jit(solution)/shard_map/ppermute | solution.py:395
  178.2 17.6 %collective-permute-start.37 = (bf16[1,2,96,384]{3,2,1,0:T(8,128)(2,1)S(1)}, bf16[1,2,96,384]{3,2,1,0:T(8,128)(2,1)S(1)}, u32[]{:S(2)}, u32[]{:S(2)}) collective-permute-start(bf16[1,2,96,384]{3,2,1,0:T(8,128)(2,1)S(1)} %add_convert_fusion.32), channel_id=1, source_target_pairs={{0,16},{16,0},{1,17},{17,1},{2,18},{18,2},{3,19},{19,3},{4,20},{20... | collective-permute-start | bytes 442376 | tf_op jit(solution)/shard_map/ppermute | solution.py:395
  178.8 17.8 %collective-permute-start.32 = (bf16[1,2,96,384]{3,2,1,0:T(8,128)(2,1)S(1)}, bf16[1,2,96,384]{3,2,1,0:T(8,128)(2,1)S(1)}, u32[]{:S(2)}, u32[]{:S(2)}) collective-permute-start(bf16[1,2,96,384]{3,2,1,0:T(8,128)(2,1)S(1)} %add_convert_fusion.35), channel_id=1, source_target_pairs={{0,8},{4,12},{8,0},{12,4},{1,9},{5,13},{9,1},{13,5},{2,10},{6,14},... | collective-permute-start | bytes 442376 | tf_op jit(solution)/shard_map/ppermute | solution.py:395
  180.2 16.5 %collective-permute-start.31 = (bf16[1,2,96,384]{3,2,1,0:T(8,128)(2,1)S(1)}, bf16[1,2,96,384]{3,2,1,0:T(8,128)(2,1)S(1)}, u32[]{:S(2)}, u32[]{:S(2)}) collective-permute-start(bf16[1,2,96,384]{3,2,1,0:T(8,128)(2,1)S(1)} %add_convert_fusion.38), channel_id=1, source_target_pairs={{0,16},{16,0},{1,17},{17,1},{2,18},{18,2},{3,19},{19,3},{4,20},{20... | collective-permute-start | bytes 442376 | tf_op jit(solution)/shard_map/ppermute | solution.py:395
  195.7 19.9 %collective-permute-start.25 = (bf16[8,2,96,768]{3,2,1,0:T(8,128)(2,1)}, bf16[8,2,96,768]{3,2,1,0:T(8,128)(2,1)S(1)}, u32[]{:S(2)}, u32[]{:S(2)}) collective-permute-start(bf16[8,2,96,768]{3,2,1,0:T(8,128)(2,1)} %get-tuple-element.76), channel_id=1, source_target_pairs={{0,4},{4,0},{8,12},{12,8},{1,5},{5,1},{9,13},{13,9},{2,6},{6,2},{1... | collective-permute-start | bytes 7077896 | tf_op jit(solution)/shard_map/ppermute | solution.py:395
  196.6 37.4 %collective-permute-start.40 = (bf16[96,768]{1,0:T(8,128)(2,1)}, bf16[96,768]{1,0:T(8,128)(2,1)}, u32[]{:S(2)}, u32[]{:S(2)}) collective-permute-start(bf16[96,768]{1,0:T(8,128)(2,1)} %fusion.22), channel_id=1, source_target_pairs={{0,3},{1,0},{2,1},{3,2},{4,7},{5,4},{6,5},{7,6},{8,11},{9,8},{10,9... | collective-permute-start | bytes 442376 | tf_op jit(solution)/shard_map/ppermute | solution.py:400
  197.5 36.5 %collective-permute-start.33 = (bf16[96,768]{1,0:T(8,128)(2,1)}, bf16[96,768]{1,0:T(8,128)(2,1)}, u32[]{:S(2)}, u32[]{:S(2)}) collective-permute-start(bf16[96,768]{1,0:T(8,128)(2,1)} %get-tuple-element.141), channel_id=1, source_target_pairs={{0,2},{1,3},{2,0},{3,1},{4,6},{5,7},{6,4},{7,5},{8,10},{9,11},{10,... | collective-permute-start | bytes 442376 | tf_op jit(solution)/shard_map/ppermute | solution.py:400
  197.5 36.5 %collective-permute-start.34 = (bf16[96,768]{1,0:T(8,128)(2,1)}, bf16[96,768]{1,0:T(8,128)(2,1)}, u32[]{:S(2)}, u32[]{:S(2)}) collective-permute-start(bf16[96,768]{1,0:T(8,128)(2,1)} %get-tuple-element.142), channel_id=1, source_target_pairs={{0,1},{1,2},{2,3},{3,0},{4,5},{5,6},{6,7},{7,4},{8,9},{9,10},{10,1... | collective-permute-start | bytes 442376 | tf_op jit(solution)/shard_map/ppermute | solution.py:400
  215.6 28.4 %collective-permute-start.48 = (bf16[8,2,96,768]{3,2,1,0:T(8,128)(2,1)}, bf16[8,2,96,768]{3,2,1,0:T(8,128)(2,1)}, u32[]{:S(2)}, u32[]{:S(2)}) collective-permute-start(bf16[8,2,96,768]{3,2,1,0:T(8,128)(2,1)} %get-tuple-element.84), channel_id=1, source_target_pairs={{0,4},{4,0},{8,12},{12,8},{1,5},{5,1},{9,13},{13,9},{2,6},{6,2},{1... | collective-permute-start | bytes 7077896 | tf_op jit(solution)/shard_map/ppermute | solution.py:395
  235.1 24.3 %collective-permute-start.41 = (bf16[96,768]{1,0:T(8,128)(2,1)S(1)}, bf16[96,768]{1,0:T(8,128)(2,1)S(1)}, u32[]{:S(2)}, u32[]{:S(2)}) collective-permute-start(bf16[96,768]{1,0:T(8,128)(2,1)S(1)} %fusion.13), channel_id=1, source_target_pairs={{0,16},{16,0},{1,17},{17,1},{2,18},{18,2},{3,19},{19,3},{4,20},{20... | collective-permute-start | bytes 442376 | tf_op jit(solution)/shard_map/ppermute | solution.py:395
  240.6 25.8 %collective-permute-start.44 = (bf16[2,2,96,768]{3,2,1,0:T(8,128)(2,1)}, bf16[2,2,96,768]{3,2,1,0:T(8,128)(2,1)}, u32[]{:S(2)}, u32[]{:S(2)}) collective-permute-start(bf16[2,2,96,768]{3,2,1,0:T(8,128)(2,1)} %get-tuple-element.114), channel_id=1, source_target_pairs={{0,16},{16,0},{1,17},{17,1},{2,18},{18,2},{3,19},{19,3},{4,20},{20... | collective-permute-start | bytes 1769480 | tf_op jit(solution)/shard_map/ppermute | solution.py:395
  242.1 26.6 %collective-permute-start.42 = (bf16[2,2,96,768]{3,2,1,0:T(8,128)(2,1)}, bf16[2,2,96,768]{3,2,1,0:T(8,128)(2,1)}, u32[]{:S(2)}, u32[]{:S(2)}) collective-permute-start(bf16[2,2,96,768]{3,2,1,0:T(8,128)(2,1)} %get-tuple-element.116), channel_id=1, source_target_pairs={{0,8},{4,12},{8,0},{12,4},{1,9},{5,13},{9,1},{13,5},{2,10},{6,14},... | collective-permute-start | bytes 1769480 | tf_op jit(solution)/shard_map/ppermute | solution.py:395
  242.8 15.1 %collective-permute-start.28 = (f32[72,128]{1,0:T(8,128)S(1)}, f32[72,128]{1,0:T(8,128)S(1)}, u32[]{:S(2)}, u32[]{:S(2)}) collective-permute-start(f32[72,128]{1,0:T(8,128)S(1)} %fusion.32), channel_id=1, source_target_pairs={{0,16},{16,0},{1,17},{17,1},{2,18},{18,2},{3,19},{19,3},{4,20},{20... | collective-permute-start | bytes 110600 | tf_op jit(solution)/shard_map/ppermute | solution.py:395
  247.1 23.6 %collective-permute-start.51 = (bf16[2,2,96,768]{3,2,1,0:T(8,128)(2,1)}, bf16[2,2,96,768]{3,2,1,0:T(8,128)(2,1)}, u32[]{:S(2)}, u32[]{:S(2)}) collective-permute-start(bf16[2,2,96,768]{3,2,1,0:T(8,128)(2,1)} %get-tuple-element.118), channel_id=1, source_target_pairs={{0,16},{16,0},{1,17},{17,1},{2,18},{18,2},{3,19},{19,3},{4,20},{20... | collective-permute-start | bytes 1769480 | tf_op jit(solution)/shard_map/ppermute | solution.py:395
  259.5 16.3 %collective-permute-start.49 = (bf16[2,2,96,768]{3,2,1,0:T(8,128)(2,1)S(1)}, bf16[2,2,96,768]{3,2,1,0:T(8,128)(2,1)S(1)}, u32[]{:S(2)}, u32[]{:S(2)}) collective-permute-start(bf16[2,2,96,768]{3,2,1,0:T(8,128)(2,1)S(1)} %get-tuple-element.120), channel_id=1, source_target_pairs={{0,8},{4,12},{8,0},{12,4},{1,9},{5,13},{9,1},{13,5},{2,10},{6,14},... | collective-permute-start | bytes 1769480 | tf_op jit(solution)/shard_map/ppermute | solution.py:395
  263.3 30.3 %collective-permute-start.30 = (f32[72,128]{1,0:T(8,128)}, f32[72,128]{1,0:T(8,128)}, u32[]{:S(2)}, u32[]{:S(2)}) collective-permute-start(f32[72,128]{1,0:T(8,128)} %add.228), channel_id=1, source_target_pairs={{0,2},{1,3},{2,0},{3,1},{4,6},{5,7},{6,4},{7,5},{8,10},{9,11},{10,... | collective-permute-start | bytes 110600 | tf_op jit(solution)/shard_map/ppermute | solution.py:395
  267.4 13.7 %collective-permute-start.45 = (bf16[1,2,96,768]{3,2,1,0:T(8,128)(2,1)S(1)}, bf16[1,2,96,768]{3,2,1,0:T(8,128)(2,1)S(1)}, u32[]{:S(2)}, u32[]{:S(2)}) collective-permute-start(bf16[1,2,96,768]{3,2,1,0:T(8,128)(2,1)S(1)} %add_convert_fusion.15), channel_id=1, source_target_pairs={{0,8},{4,12},{8,0},{12,4},{1,9},{5,13},{9,1},{13,5},{2,10},{6,14},... | collective-permute-start | bytes 884744 | tf_op jit(solution)/shard_map/ppermute | solution.py:395
  269.8 12.4 %collective-permute-start.43 = (bf16[1,2,96,768]{3,2,1,0:T(8,128)(2,1)S(1)}, bf16[1,2,96,768]{3,2,1,0:T(8,128)(2,1)S(1)}, u32[]{:S(2)}, u32[]{:S(2)}) collective-permute-start(bf16[1,2,96,768]{3,2,1,0:T(8,128)(2,1)S(1)} %add_convert_fusion.18), channel_id=1, source_target_pairs={{0,16},{16,0},{1,17},{17,1},{2,18},{18,2},{3,19},{19,3},{4,20},{20... | collective-permute-start | bytes 884744 | tf_op jit(solution)/shard_map/ppermute | solution.py:395
  271.7 15.9 %collective-permute-start.52 = (bf16[1,2,96,768]{3,2,1,0:T(8,128)(2,1)S(1)}, bf16[1,2,96,768]{3,2,1,0:T(8,128)(2,1)S(1)}, u32[]{:S(2)}, u32[]{:S(2)}) collective-permute-start(bf16[1,2,96,768]{3,2,1,0:T(8,128)(2,1)S(1)} %add_convert_fusion.9), channel_id=1, source_target_pairs={{0,8},{4,12},{8,0},{12,4},{1,9},{5,13},{9,1},{13,5},{2,10},{6,14},... | collective-permute-start | bytes 884744 | tf_op jit(solution)/shard_map/ppermute | solution.py:395
  275.9 12.8 %collective-permute-start.50 = (bf16[1,2,96,768]{3,2,1,0:T(8,128)(2,1)S(1)}, bf16[1,2,96,768]{3,2,1,0:T(8,128)(2,1)S(1)}, u32[]{:S(2)}, u32[]{:S(2)}) collective-permute-start(bf16[1,2,96,768]{3,2,1,0:T(8,128)(2,1)S(1)} %add_convert_fusion.12), channel_id=1, source_target_pairs={{0,16},{16,0},{1,17},{17,1},{2,18},{18,2},{3,19},{19,3},{4,20},{20... | collective-permute-start | bytes 884744 | tf_op jit(solution)/shard_map/ppermute | solution.py:395
  284.2 17.4 %collective-permute-start.46 = (bf16[96,1536]{1,0:T(8,128)(2,1)}, bf16[96,1536]{1,0:T(8,128)(2,1)S(1)}, u32[]{:S(2)}, u32[]{:S(2)}) collective-permute-start(bf16[96,1536]{1,0:T(8,128)(2,1)} %get-tuple-element.135), channel_id=1, source_target_pairs={{0,2},{1,3},{2,0},{3,1},{4,6},{5,7},{6,4},{7,5},{8,10},{9,11},{10,... | collective-permute-start | bytes 884744 | tf_op jit(solution)/shard_map/ppermute | solution.py:400
  285.9 15.7 %collective-permute-start.47 = (bf16[96,1536]{1,0:T(8,128)(2,1)}, bf16[96,1536]{1,0:T(8,128)(2,1)S(1)}, u32[]{:S(2)}, u32[]{:S(2)}) collective-permute-start(bf16[96,1536]{1,0:T(8,128)(2,1)} %get-tuple-element.136), channel_id=1, source_target_pairs={{0,1},{1,2},{2,3},{3,0},{4,5},{5,6},{6,7},{7,4},{8,9},{9,10},{10,1... | collective-permute-start | bytes 884744 | tf_op jit(solution)/shard_map/ppermute | solution.py:400
  288.9 13.8 %collective-permute-start.53 = (bf16[96,1536]{1,0:T(8,128)(2,1)S(1)}, bf16[96,1536]{1,0:T(8,128)(2,1)S(1)}, u32[]{:S(2)}, u32[]{:S(2)}) collective-permute-start(bf16[96,1536]{1,0:T(8,128)(2,1)S(1)} %fusion.10), channel_id=1, source_target_pairs={{0,3},{1,0},{2,1},{3,2},{4,7},{5,4},{6,5},{7,6},{8,11},{9,8},{10,9... | collective-permute-start | bytes 884744 | tf_op jit(solution)/shard_map/ppermute | solution.py:400
  302.8 6.8 %collective-permute-start.54 = (bf16[96,1536]{1,0:T(8,128)(2,1)S(1)}, bf16[96,1536]{1,0:T(8,128)(2,1)S(1)}, u32[]{:S(2)}, u32[]{:S(2)}) collective-permute-start(bf16[96,1536]{1,0:T(8,128)(2,1)S(1)} %fusion.1), channel_id=1, source_target_pairs={{0,16},{16,0},{1,17},{17,1},{2,18},{18,2},{3,19},{19,3},{4,20},{20... | collective-permute-start | bytes 884744 | tf_op jit(solution)/shard_map/ppermute | solution.py:395
  (58 other events, 456.2 us)

commit v4 on v3

--- a/solution.py
+++ b/solution.py
@@ -66,8 +66,8 @@
 
 
 def prep_kernel(
-    x_ref, cot_ref, ga_ref, sa_ref, gm_ref, sm_ref, segc_ref, segr_ref, freq_ref, _mlp_in, _after,
-    na_ref, naT_ref, nm_ref, nmT_ref, cotT_ref, keep_ref, ahead_ref, behind_ref, mask_ref, _mlp_out,
+    x_ref, cot_ref, ga_ref, sa_ref, gm_ref, sm_ref, segc_ref, segr_ref, freq_ref,
+    na_ref, naT_ref, nm_ref, nmT_ref, cotT_ref, keep_ref, ahead_ref, behind_ref, mask_ref,
 ):
     length = x_ref.shape[0]
     tile = 128
@@ -97,7 +97,7 @@
 
 
 def full(*shape):
-    return pl.BlockSpec(shape, lambda *_: (0,) * len(shape))
+    return pl.BlockSpec(shape, lambda *_: (0,) * len(shape), pipeline_mode=pl.Buffered(1))
 
 
 ANY = pl.BlockSpec(memory_space=pl.ANY)
@@ -112,7 +112,7 @@
     return jax.ShapeDtypeStruct(shape, dtype)
 
 
-def prep_part(tokens, cot, gains, seg_row, mlp_own, after):
+def prep_part(tokens, cot, gains, seg_row):
     length, width = tokens.shape
     halves = ROT // 2
     step = (lax.iota(jnp.int32, 2 * HD) % HD % halves).astype(F32)
@@ -122,16 +122,14 @@
         prep_kernel,
         grid=(1,),
         in_specs=[full(length, width)] * 2 + [full(1, width)] * 4
-        + [full(length, 1), full(1, length), full(1, 2 * HD), ANY, ANY],
+        + [full(length, 1), full(1, length), full(1, 2 * HD)],
         out_specs=[full(length, width), full(width, length)] * 2 + [full(width, length)]
-        + [full(length, 2 * HD)] * 3 + [full(length, length), ANY],
+        + [full(length, 2 * HD)] * 3 + [full(length, length)],
         out_shape=[shaped((length, width), BF16), shaped((width, length), BF16)] * 2
-        + [shaped((width, length), BF16)] + [table] * 3 + [shaped((length, length), F32)]
-        + [shaped(mlp_own.shape, BF16)],
-        input_output_aliases={9: 9},
-        compiler_params=pltpu.CompilerParams(vmem_limit_bytes=48 * 2**20),
+        + [shaped((width, length), BF16)] + [table] * 3 + [shaped((length, length), F32)],
+        compiler_params=pltpu.CompilerParams(vmem_limit_bytes=24 * 2**20),
         cost_estimate=cost(6),
-    )(tokens, cot, *gains, seg_row[:, None], seg_row[None, :], freq, mlp_own, after)
+    )(tokens, cot, *gains, seg_row[:, None], seg_row[None, :], freq)
 
 
 def attention_kernel(orders, core_bit, waits, me_ref, na_ref, naT_ref, cot_ref, cotT_ref, *rest):
@@ -256,12 +254,16 @@
 
 
 def block_part(kernel, k0, count, orders, core_bit, after, me, norm, norm_t, cot, cot_t, left, right, vectors, mid_cols,
-               g_cols, scratch, us):
+               g_cols, scratch, us, into=None):
     length, width = norm.shape
     rows = left[0].shape[2]
     pieces = width // rows
     cols = vectors[0].shape[-1]
-    g_spec = pl.BlockSpec((pieces, 1, rows, g_cols), lambda s: (0, s, 0, 0))
+    shared = into is not None
+    g_blocks = left[0].shape[1] if shared else count
+    g_spec = pl.BlockSpec((pieces, 1, rows, g_cols), lambda s: (0, k0 + s if shared else s, 0, 0))
+    after = list(after) + list(into or [])
+    fixed = 5 + len(left + right) + len(vectors) + len(after)
     return pl.pallas_call(
         functools.partial(kernel, orders, core_bit, len(after)),
         grid=(count,),
@@ -273,9 +275,10 @@
         out_specs=[pl.BlockSpec((1, length, m), lambda s: (s, 0, 0)) for m in mid_cols]
         + [pl.BlockSpec((1, 1, cols), lambda s: (s, 0, 0))] + [g_spec] * 2,
         out_shape=[shaped((count, length, m), BF16) for m in mid_cols]
-        + [shaped((count, 1, cols), F32)] + [shaped((pieces, count, rows, g_cols), BF16)] * 2,
+        + [shaped((count, 1, cols), F32)] + [shaped((pieces, g_blocks, rows, g_cols), BF16)] * 2,
+        input_output_aliases={fixed - 2: len(mid_cols) + 1, fixed - 1: len(mid_cols) + 2} if into else {},
         scratch_shapes=scratch,
-        compiler_params=pltpu.CompilerParams(vmem_limit_bytes=56 * 2**20),
+        compiler_params=pltpu.CompilerParams(vmem_limit_bytes=30 * 2**20),
         cost_estimate=cost(us * count),
     )(me, norm, norm_t, cot, cot_t, *left, *right, *vectors, *after)
 
@@ -381,9 +384,25 @@
         out_specs=[full(*o.shape) for o in outs],
         out_shape=outs,
         scratch_shapes=scratch + kept,
-        compiler_params=pltpu.CompilerParams(vmem_limit_bytes=56 * 2**20),
+        compiler_params=pltpu.CompilerParams(vmem_limit_bytes=40 * 2**20),
         cost_estimate=cost(us),
     )(me, *left, *right, *[array for group in mids for array in group], *extra, *after)
+
+
+def fence_kernel(*_):
+    pass
+
+
+def fence(values, after=()):
+    count = len(values)
+    return pl.pallas_call(
+        fence_kernel,
+        in_specs=[ANY] * (count + len(after)),
+        out_specs=[ANY] * count,
+        out_shape=[shaped(value.shape, value.dtype) for value in values],
+        input_output_aliases={n: n for n in range(count)},
+        cost_estimate=cost(1),
+    )(*values, *after)
 
 
 def swap(value, bit):
@@ -401,34 +420,54 @@
 
 
 def gather_pieces(own, order, core_bit):
-    held, steps = own[None], []
+    held = own[None]
     for bit in order[:-1]:
-        came = swap(held, bit)
-        steps.append(came)
-        held = jnp.concatenate([held, came], axis=0)
+        held = jnp.concatenate([held, swap(held, bit)], axis=0)
     came = swap(held, order[-1])
-    steps.append(came)
-    return [held, came, swap(held, core_bit), swap(came, core_bit)], steps
+    return [held, came, swap(held, core_bit), swap(came, core_bit)]
 
 
 def add(a, b):
     return (a.astype(F32) + b.astype(F32)).astype(BF16)
 
 
-def reduce_pieces(keep, send, orders, core_bit):
-    came = swap(send, core_bit)
-    steps = [[came]] + [[] for _ in orders[0]]
-    size = keep.shape[0] // len(orders)
-    totals = []
-    for side, order in enumerate(orders):
-        held, other = keep[side * size : (side + 1) * size], came[side * size : (side + 1) * size]
-        for at, bit in enumerate(order):
-            half = held.shape[0] // 2
-            moved = swap(add(held[half:], other[half:]), bit)
-            held, other = add(held[:half], other[:half]), moved
-            steps[at + 1].append(moved)
-        totals.append(add(held[0], other[0]))
-    return jnp.concatenate(totals, axis=2), steps
+class Reduction:
+    def __init__(self, keep, send, orders, core_bit):
+        self.keep, self.orders, self.core_bit = keep, orders, core_bit
+        self.moving, self.held, self.done, self.closed = [send], None, -1, False
+
+    def advance(self):
+        if self.done < 0:
+            self.moving = [swap(self.moving[0], self.core_bit)]
+        else:
+            if self.done == 0:
+                size = self.keep.shape[0] // len(self.orders)
+                cuts = [slice(side * size, (side + 1) * size) for side in range(len(self.orders))]
+                self.held, self.moving = [self.keep[c] for c in cuts], [self.moving[0][c] for c in cuts]
+            half = self.held[0].shape[0] // 2
+            sent = [add(a[half:], b[half:]) for a, b in zip(self.held, self.moving)]
+            self.held = [add(a[:half], b[:half]) for a, b in zip(self.held, self.moving)]
+            self.moving = [swap(one, order[self.done]) for one, order in zip(sent, self.orders)]
+        self.done += 1
+
+    def total(self):
+        assert self.done == len(self.orders[0])
+        return jnp.concatenate([add(a[0], b[0]) for a, b in zip(self.held, self.moving)], axis=2)
+
+
+def phase(reductions, values=(), after=()):
+    values = list(values)
+    reductions = [r for r in reductions if not r.closed]
+    out = list(fence(values + [one for r in reductions for one in r.moving], after))
+    at = len(values)
+    for r in reductions:
+        r.moving = out[at : at + len(r.moving)]
+        at += len(r.moving)
+        if r.done < len(r.orders[0]):
+            r.advance()
+        else:
+            r.closed = True
+    return out
 
 
 def all_sum(value):
@@ -489,19 +528,14 @@
 
     attn_all = gather_col(attn_own)
     cut = block_cols // 2
-    attn_left, _ = gather_pieces(attn_all[:, :, :cut], orders[0], core_bit)
-    attn_right, _ = gather_pieces(attn_all[:, :, cut:], orders[1], core_bit)
+    attn_left = gather_pieces(attn_all[:, :, :cut], orders[0], core_bit)
+    attn_right = gather_pieces(attn_all[:, :, cut:], orders[1], core_bit)
 
     seg_row = lax.dynamic_index_in_dim(segment_ids, row_id * col_size + col_id, axis=0, keepdims=False)
-    na, na_t, nm, nm_t, cot_t, keep, ahead, behind, mask, mlp_own = prep_part(
+    na, na_t, nm, nm_t, cot_t, keep, ahead, behind, mask = prep_part(
         tokens_in, out_cotangent, [v[None, :] for v in (attn_gain, attn_shift, mlp_gain, mlp_shift)], seg_row,
-        mlp_own, attn_all,
     )
-    mlp_all = gather_col(mlp_own)
-    up, up_steps = gather_pieces(mlp_all[:, :, :up_cols], orders[0], core_bit)
-    down, down_steps = gather_pieces(mlp_all[:, :, up_cols:], orders[1], core_bit)
-    mlp_steps = [list(pair) for pair in zip(up_steps, down_steps)]
-
+    mlp_all = gather_col(fence([mlp_own], [attn_all])[0])
     blocks_here = (col_id - jnp.arange(col_size)) % col_size
     head_bias = jnp.pad(
         qkv_bias.reshape(col_size, local_heads, QKV), ((0, 0), (0, 0), (0, HEAD - QKV))
@@ -516,11 +550,14 @@
     def block_of(s):
         return (calls - 1 - s // per_call) * per_call + s % per_call
 
-    attn_calls, attn_sums, attn_steps = [], [], []
-    last = []
-    for n, k0 in enumerate(starts):
-        after = last + ([mlp_all] if n == 0 else mlp_steps[0] if n == 1 else [])
-        *mids, d_bias, g_keep, g_send = block_part(
+    def held_until_last(own, order):
+        held = own[None]
+        for bit in order[:-1]:
+            held = jnp.concatenate([held, swap(held, bit)], axis=0)
+        return held
+
+    def attention_call(k0, after, into):
+        return block_part(
             attention_kernel, k0, per_call, orders, core_bit, after, me, na, na_t, out_cotangent, cot_t,
             attn_left, attn_right, [head_bias, keep, ahead, behind, mask], [block_cols, cut], cut,
             [
@@ -528,35 +565,47 @@
                 pltpu.VMEM((length, block_cols), F32), pltpu.VMEM((length, cut), BF16),
                 pltpu.VMEM((width, block_cols), BF16),
             ],
-            11,
+            11, into,
         )
-        last = [d_bias]
-        attn_calls.append(mids + [d_bias])
-        total, steps = reduce_pieces(g_keep, g_send, orders, core_bit)
-        attn_sums.append(total)
-        attn_steps.append(steps)
+
+    def mlp_call(k0, after):
+        return block_part(
+            mlp_kernel, k0, per_call, orders, core_bit, after, me, nm, nm_t, out_cotangent, cot_t,
+            up, down, [hidden_bias], [up_cols, up_cols], up_cols, [pltpu.VMEM((width, up_cols), BF16)] * 3, 6,
+        )
+
+    held = [held_until_last(mlp_all[:, :, :up_cols], orders[0]), held_until_last(mlp_all[:, :, up_cols:], orders[1])]
+    held = list(fence(held, [w for w in attn_left + attn_right]))
+    came = [swap(one, order[-1]) for one, order in zip(held, orders)]
+    held_over = [swap(one, core_bit) for one in held]
+
+    attn_calls, into = [], []
+    for n, k0 in enumerate(starts):
+        outs = attention_call(k0, [held[0]] if n == 0 else [came[0]], into)
+        attn_calls.append(outs[:3])
+        into = list(outs[3:])
+        if n == 0:
+            came = list(fence(came, [outs[2]] + held_over))
+            came_over = [swap(one, core_bit) for one in came]
+    attn_sum = Reduction(into[0], into[1], orders, core_bit)
+    up, down = ([held[i], came[i], held_over[i], came_over[i]] for i in range(2))
+
+    token = phase([attn_sum], [], came_over)
+    mlp_calls, mlp_sums = [], []
+    for k0 in starts:
+        *mids, g_keep, g_send = mlp_call(k0, token[:1])
+        mlp_calls.append(mids)
+        mlp_sums.append(Reduction(g_keep, g_send, orders, core_bit))
+        token = phase([attn_sum] + mlp_sums, [], [mids[2]])
+
     branch, d_norm_attn = tail_part(
-        attention_tail_kernel, block_of, per_call, orders, core_bit, last + mlp_steps[-1], me, attn_left, attn_right,
+        attention_tail_kernel, block_of, per_call, orders, core_bit, token[:1], me, attn_left, attn_right,
         [[c[0] for c in attn_calls], [c[1] for c in attn_calls]], [], [shaped((length, width), F32)] * 2,
         [pltpu.VMEM((width, block_cols), BF16), pltpu.VMEM((width, cut), BF16)], 9,
     )
-    mlp_calls, mlp_sums, mlp_moves = [], [], []
-    last = [branch]
-    for n, k0 in enumerate(starts):
-        after = last + attn_steps[0][min(n, len(orders[0]))]
-        *mids, d_bias, g_keep, g_send = block_part(
-            mlp_kernel, k0, per_call, orders, core_bit, after, me, nm, nm_t, out_cotangent, cot_t,
-            up, down, [hidden_bias], [up_cols, up_cols], up_cols,
-            [pltpu.VMEM((width, up_cols), BF16)] * 3,
-            6,
-        )
-        last = [d_bias]
-        mlp_calls.append(mids + [d_bias])
-        total, steps = reduce_pieces(g_keep, g_send, orders, core_bit)
-        mlp_sums.append(total)
-        mlp_moves.append(steps)
+    token = phase([attn_sum] + mlp_sums, [], [branch])
     block_out, in_grad, stats = tail_part(
-        mlp_tail_kernel, block_of, per_call, orders, core_bit, last + mlp_moves[0][0], me, up, down,
+        mlp_tail_kernel, block_of, per_call, orders, core_bit, token[:1], me, up, down,
         [[c[1] for c in mlp_calls], [c[0] for c in mlp_calls]],
         [
             branch, d_norm_attn, tokens_in, out_cotangent, attn_gain[None, :], mlp_gain[None, :], out_bias[None, :],
@@ -565,14 +614,17 @@
         [shaped((length, width), BF16)] * 2 + [shaped((8, width), F32)],
         [pltpu.VMEM((length, width), F32)] * 2 + [pltpu.VMEM((width, up_cols), BF16)] * 2, 13,
     )
+    stats = phase([attn_sum] + mlp_sums, [stats])[0]
+    while any(r.done < len(orders[0]) for r in mlp_sums):
+        for r in mlp_sums:
+            if r.done < len(orders[0]):
+                r.advance()
 
     def settle(parts):
         total = None
-        for both, k0 in zip(parts, starts):
-            for i in range(per_call):
-                k = k0 + i
-                term = (both[i] if k == 0 else shifted(both[i], -k)).astype(F32)
-                total = term if total is None else total + term
+        for k, part in parts:
+            term = (part if k == 0 else shifted(part, -k)).astype(F32)
+            total = term if total is None else total + term
         flip = 2
         while flip < lax.axis_size("dp"):
             total = total + flipped(total, "dp", flip)
@@ -582,8 +634,10 @@
         first = half == 0
         return jnp.concatenate([jnp.where(first, mine, other), jnp.where(first, other, mine)], axis=0).astype(F32)
 
-    g_heads = settle(attn_sums).reshape(rows, local_heads, HEAD)
-    g_mlp = settle(mlp_sums)
+    attn_sum = attn_sum.total()
+    g_heads = settle([(k, attn_sum[k]) for k in range(col_size)]).reshape(rows, local_heads, HEAD)
+    mlp_totals = [r.total() for r in mlp_sums]
+    g_mlp = settle([(k0 + i, one[i]) for k0, one in zip(starts, mlp_totals) for i in range(per_call)])
 
     d_bias_up = jnp.take(jnp.concatenate([c[2] for c in mlp_calls[::-1]]), blocks_here, axis=0)
     d_bias_attn = jnp.take(jnp.concatenate([c[2] for c in attn_calls[::-1]]), blocks_here, axis=0)

time: 314 us -> 365 us (1.16); the launches traced: 311 us -> 359 us
  local copies, waits for them, and re-layouts: 27.6 us -> 114 us
  waiting for transfers between devices: 98.1 us -> 66.7 us
  Pallas kernels: 99.9 us -> 81.9 us
  other arithmetic: 27.1 us -> 40.4 us
  starting transfers between devices: 57.2 us -> 53.3 us
    unnamed x110 -> x328, local copies, waits for them, and re-layouts: 14.4 us -> 101 us
    ppermute x43 -> x38, waiting for transfers between devices: 58.8 us -> 33.9 us  [flipped(): lax.ppermute(value, axis, [(i, i ^ flip) for i in range(lax.axis_size(axi...]
    pallas_call x4, Pallas kernels: 68.8 us -> 56.6 us  [block_part(): pl.pallas_call(functools.partial(kernel, orders, core_bit, len(after)), g...]
    convert_element_type x20 -> x13, other arithmetic: 14 us -> 25.2 us  [add(): return (a.astype(F32) + b.astype(F32)).astype(BF16)]
    ppermute x43 -> x38, starting transfers between devices: 38.6 us -> 32 us  [flipped(): lax.ppermute(value, axis, [(i, i ^ flip) for i in range(lax.axis_size(axi...]
    ppermute x12, waiting for transfers between devices: 39.3 us -> 32.8 us  [shifted(): lax.ppermute(value, 'col', [(i, (i + by) % size) for i in range(size)])]
    pallas_call x2, Pallas kernels: 26.7 us -> 22.6 us  [tail_part(): pl.pallas_call(functools.partial(kernel, orders, core_bit, calls, per_cal...]
  transfers between devices with their start and end apart: 55 -> 50, of which waited for: 16 -> 12; matrix products, arithmetic and copies ran while one was open for 12% -> 13% of each run, Pallas kernels for 25% -> 23%
where the time goes in v4:
time: 365 us; the launch traced here: 359 us
  local copies, waits for them, and re-layouts  114 us (31%)
  Pallas kernels  81.9 us (22%)
  waiting for transfers between devices  66.7 us (18%)
  starting transfers between devices  53.3 us (15%)
  other arithmetic  40.4 us (11%)
    unnamed x328, local copies, waits for them, and re-layouts  101 us
    pallas_call x4, Pallas kernels, block_part(): pl.pallas_call(functools.partial(kernel, orders, core_bit, len(after)), g...  56.6 us
    ppermute x38, waiting for transfers between devices, flipped(): lax.ppermute(value, axis, [(i, i ^ flip) for i in range(lax.axis_size(axi...  33.9 us
    ppermute x12, waiting for transfers between devices, shifted(): lax.ppermute(value, 'col', [(i, (i + by) % size) for i in range(size)])  32.8 us
    ppermute x38, starting transfers between devices, flipped(): lax.ppermute(value, axis, [(i, i ^ flip) for i in range(lax.axis_size(axi...  32 us
    convert_element_type x13, other arithmetic, add(): return (a.astype(F32) + b.astype(F32)).astype(BF16)  25.2 us
    pallas_call x2, Pallas kernels, tail_part(): pl.pallas_call(functools.partial(kernel, orders, core_bit, calls, per_cal...  22.6 us
    ppermute x12, starting transfers between devices, shifted(): lax.ppermute(value, 'col', [(i, (i + by) % size) for i in range(size)])  21.3 us
  transfers between devices with their start and end apart: 50, of which 12 were waited for; matrix products, arithmetic and copies ran while one was open for 13% of the time, Pallas kernels for 23%

profile of v4, /device:TPU:0, one launch (start us, length us, event | category | flops | bytes accessed | tf_op | source)
XLA Modules:
  0.0 358.6 jit_solution(2515634801495124877)
XLA Ops:
  3.1 5.1 %collective-permute-start.2 = (bf16[96,768]{1,0:T(8,128)(2,1)S(1)}, bf16[96,768]{1,0:T(8,128)(2,1)S(1)}, u32[]{:S(2)}, u32[]{:S(2)}) collective-permute-start(bf16[96,768]{1,0:T(8,128)(2,1)S(1)} %copy.70), channel_id=1, source_target_pairs={{0,3},{1,0},{2,1},{3,2},{4,7},{5,4},{6,5},{7,6},{8,11},{9,8},{10,9... | collective-permute-start | bytes 442376 | tf_op jit(solution)/shard_map/ppermute | solution.py:419
  12.5 8.2 %collective-permute-done.1 = bf16[96,768]{1,0:T(8,128)(2,1)S(1)} collective-permute-done((bf16[96,768]{1,0:T(8,128)(2,1)S(1)}, bf16[96,768]{1,0:T(8,128)(2,1)S(1)}, u32[]{:S(2)}, u32[]{:S(2)}) %collective-permute-start.1) | collective-permute-done | bytes 147488 | tf_op jit(solution)/shard_map/ppermute | solution.py:419
  21.6 1.5 collective-permute-start.5
  24.6 1.9 collective-permute-start.3
  26.9 1.6 collective-permute-start.8
  28.5 1.5 collective-permute-start.12
  31.0 19.1 %collective-permute-done.4 = bf16[96,1536]{1,0:T(8,128)(2,1)S(1)} collective-permute-done((bf16[96,1536]{1,0:T(8,128)(2,1)}, bf16[96,1536]{1,0:T(8,128)(2,1)S(1)}, u32[]{:S(2)}, u32[]{:S(2)}) %collective-permute-start.4) | collective-permute-done | bytes 294944 | tf_op jit(solution)/shard_map/ppermute | solution.py:419
  53.2 1.5 collective-permute-start.6
  55.6 1.5 collective-permute-start.9
  58.6 2.7 shard_map.256
  72.2 7.7 %collective-permute-done.13.__7_.rest_5_ = bf16[2,4,96,384]{3,2,1,0:T(8,128)(2,1)S(1)} collective-permute-done((bf16[2,4,96,384]{3,2,1,0:T(8,128)(2,1)}, bf16[2,4,96,384]{3,2,1,0:T(8,128)(2,1)S(1)}, u32[]{:S(2)}, u32[]{:S(2)}) %collective-permute-start.13) | collective-permute-done | bytes 589856 | tf_op jit(solution)/shard_map/ppermute | solution.py:414
  81.9 2.4 pad_maximum_fusion.1.__0_
  84.2 2.4 pad_maximum_fusion.2.__1_
  88.7 1.5 collective-permute-start.16
  90.4 1.5 collective-permute-start.17
  108.9 17.9 %shard_map.257 = (bf16[2,512,768]{2,1,0:T(8,128)(2,1)S(1)}, bf16[2,512,384]{2,1,0:T(8,128)(2,1)S(1)}, f32[2,1,768]{2,1,0:T(1,128)S(1)}, bf16[8,4,96,384]{3,2,1,0:T(8,128)(2,1)S(1)}, bf16[8,4,96,384]{3,2,1,0:T(8,128)(2,1)S(1)}) custom-call(s32[1]{0:T(128)} %bitcast.me_ref, bf16[512,768]{1,0:T(8,128)(2,1)S(1)} %copy-done.109, ...), custom_call_target="tpu_custom_call" | custom-call | flops 25300000768 | bytes 1048576 | tf_op jit(solution)/shard_map/pallas_call | solution.py:267
  133.4 1.7 copy-done.15
  152.1 17.9 %shard_map.259 = (bf16[2,512,768]{2,1,0:T(8,128)(2,1)S(1)}, bf16[2,512,384]{2,1,0:T(8,128)(2,1)S(1)}, f32[2,1,768]{2,1,0:T(1,128)S(1)}, bf16[8,4,96,384]{3,2,1,0:T(8,128)(2,1)S(1)}, bf16[8,4,96,384]{3,2,1,0:T(8,128)(2,1)S(1)}) custom-call(s32[1]{0:T(128)} %bitcast.me_ref, ...), custom_call_target="tpu_custom_call", output_to_operand_aliasing={{3}: (19, {}), {4}: (20, {})} | custom-call | flops 25300000768 | bytes 1048576 | tf_op jit(solution)/shard_map/pallas_call | solution.py:267
  172.7 1.8 copy-done.16
  178.1 1.7 copy-done.17
  190.7 10.2 %shard_map.261 = (bf16[2,512,768]{2,1,0:T(8,128)(2,1)S(1)}, bf16[2,512,768]{2,1,0:T(8,128)(2,1)S(1)}, f32[2,1,768]{2,1,0:T(1,128)S(1)}, bf16[8,2,96,768]{3,2,1,0:T(8,128)(2,1)S(1)}, bf16[8,2,96,768]{3,2,1,0:T(8,128)(2,1)S(1)}) custom-call(s32[1]{0:T(128)} %bitcast.me_ref, bf16[512,768]{1,0:T(8,128)(2,1)S(1)} %copy-done.98, bf16[768,512]{1,0:T(8,128)(2,1)S(1)} %copy-done.101, ...), custom_call_target="tpu_custom_call" | custom-call | flops 13799999488 | bytes 1048576 | tf_op jit(solution)/shard_map/pallas_call | solution.py:267
  206.6 1.5 copy-done.2
  208.6 4.1 %add_convert_fusion.8 = (bf16[2,4,96,384]{3,2,1,0:T(8,128)(2,1)}, bf16[2,4,96,384]{3,2,1,0:T(8,128)(2,1)}, bf16[2,4,96,384]{3,2,1,0:T(8,128)(2,1)S(1)}, bf16[2,4,96,384]{3,2,1,0:T(8,128)(2,1)S(1)}) fusion(bf16[8,4,96,384]{3,2,1,0:T(8,128)(2,1)} %get-tuple-element.89.rest_9_, bf16[8,4,96,384]{3,2,1,0:T(8,128)(2,1)} %copy-done.13), kind=kLoop, calls=%fused_computation.15 | loop fusion | flops 4718592 | bytes 7077888 | tf_op jit(solution)/shard_map/convert_element_type | solution.py:431
  220.8 10.4 %shard_map.263 = (bf16[2,512,768]{2,1,0:T(8,128)(2,1)S(1)}, bf16[2,512,768]{2,1,0:T(8,128)(2,1)S(1)}, f32[2,1,768]{2,1,0:T(1,128)S(1)}, bf16[8,2,96,768]{3,2,1,0:T(8,128)(2,1)S(1)}, bf16[8,2,96,768]{3,2,1,0:T(8,128)(2,1)S(1)}) custom-call(s32[1]{0:T(128)} %bitcast.me_ref, bf16[512,768]{1,0:T(8,128)(2,1)S(1)} %copy-done.99, bf16[768,512]{1,0:T(8,128)(2,1)S(1)} %copy-done.102, ...), custom_call_target="tpu_custom_call" | custom-call | flops 13799999488 | bytes 1048576 | tf_op jit(solution)/shard_map/pallas_call | solution.py:267
  235.7 1.5 copy-done.18
  243.8 1.6 collective-permute-start.26
  246.6 1.6 collective-permute-start.27
  248.2 4.1 %add_convert_fusion.4 = (bf16[2,2,96,768]{3,2,1,0:T(8,128)(2,1)}, bf16[2,2,96,768]{3,2,1,0:T(8,128)(2,1)}, bf16[2,2,96,768]{3,2,1,0:T(8,128)(2,1)S(1)}, bf16[2,2,96,768]{3,2,1,0:T(8,128)(2,1)S(1)}) fusion(bf16[8,2,96,768]{3,2,1,0:T(8,128)(2,1)} %get-tuple-element.106, bf16[8,2,96,768]{3,2,1,0:T(8,128)(2,1)} %copy-done.12), kind=kLoop, calls=%fused_computation.11 | loop fusion | flops 4718592 | bytes 7077888 | tf_op jit(solution)/shard_map/convert_element_type | solution.py:431
  253.5 8.7 %shard_map.265 = (f32[512,768]{1,0:T(8,128)S(1)}, f32[512,768]{1,0:T(8,128)S(1)}) custom-call(s32[1]{0:T(128)} %bitcast.me_ref, bf16[2,4,96,384]{3,2,1,0:T(8,128)(2,1)} %pad_maximum_fusion.4.__2_.rest_0_, bf16[2,4,96,384]{3,2,1,0:T(8,128)(2,1)S(1)} %copy-done.47, bf16[2,4,96,384]{3,2,1,0:T(8,128)(2,1)S(1)} %copy-done.55, ...), custom_call_target="tpu_custom_call" | custom-call | flops 10350000128 | bytes 1048576 | tf_op jit(solution)/shard_map/pallas_call | solution.py:378
  264.5 3.5 collective-permute-done.28.__2_
  268.0 2.0 add_convert_fusion.27
  270.5 1.8 add_convert_fusion.26
  272.3 1.5 collective-permute-start.32
  273.8 1.6 fusion.2
  275.6 1.8 collective-permute-start.41
  277.4 2.8 collective-permute-start.40
  280.3 3.4 add_convert_fusion.1
  284.7 3.1 collective-permute-done.41
  287.8 1.5 collective-permute-start.34
  290.1 14.0 %shard_map.267 = (bf16[512,768]{1,0:T(8,128)(2,1)}, bf16[512,768]{1,0:T(8,128)(2,1)}, f32[8,768]{1,0:T(8,128)S(1)}) custom-call(s32[1]{0:T(128)} %bitcast.me_ref, bf16[2,4,96,768]{3,2,1,0:T(8,128)(2,1)S(1)} %copy-done.5, bf16[2,4,96,768]{3,2,1,0:T(8,128)(2,1)S(1)} %copy-done.39, bf16[2,4,96,768]{3,2,1,0:T(8,128)(2,1)S(1)} %copy-done.26, ...), custom_call_target="tpu_custom_call" | custom-call | flops 14949999616 | bytes 1048576 | tf_op jit(solution)/shard_map/pallas_call | solution.py:378
  310.3 1.6 collective-permute-start.46
  311.8 5.4 %collective-permute-done.36 = f32[72,128]{1,0:T(8,128)S(1)} collective-permute-done((f32[72,128]{1,0:T(8,128)S(1)}, f32[72,128]{1,0:T(8,128)S(1)}, u32[]{:S(2)}, u32[]{:S(2)}) %collective-permute-start.36) | collective-permute-done | bytes 36896 | tf_op jit(solution)/shard_map/ppermute | solution.py:414
  317.3 1.6 collective-permute-start.37
  321.3 2.2 collective-permute-start.38
  324.4 2.5 collective-permute-start.44
  331.1 3.0 collective-permute-start.48
  336.8 11.4 %collective-permute-done.39 = f32[72,128]{1,0:T(8,128)S(1)} collective-permute-done((f32[72,128]{1,0:T(8,128)S(1)}, f32[72,128]{1,0:T(8,128)S(1)}, u32[]{:S(2)}, u32[]{:S(2)}) %collective-permute-start.39) | collective-permute-done | bytes 36896 | tf_op jit(solution)/shard_map/ppermute | solution.py:414
  351.9 4.9 %collective-permute-done.49 = bf16[96,1536]{1,0:T(8,128)(2,1)S(1)} collective-permute-done((bf16[96,1536]{1,0:T(8,128)(2,1)S(1)}, bf16[96,1536]{1,0:T(8,128)(2,1)S(1)}, u32[]{:S(2)}, u32[]{:S(2)}) %collective-permute-start.49) | collective-permute-done | bytes 294944 | tf_op jit(solution)/shard_map/ppermute | solution.py:414
  (472 shorter events, 142.4 us)
Async XLA Ops:
  3.1 9.4 %collective-permute-start.2 = (bf16[96,768]{1,0:T(8,128)(2,1)S(1)}, bf16[96,768]{1,0:T(8,128)(2,1)S(1)}, u32[]{:S(2)}, u32[]{:S(2)}) collective-permute-start(bf16[96,768]{1,0:T(8,128)(2,1)S(1)} %copy.70), channel_id=1, source_target_pairs={{0,3},{1,0},{2,1},{3,2},{4,7},{5,4},{6,5},{7,6},{8,11},{9,8},{10,9... | collective-permute-start | bytes 442376 | tf_op jit(solution)/shard_map/ppermute | solution.py:419
  8.2 12.5 %collective-permute-start.1 = (bf16[96,768]{1,0:T(8,128)(2,1)S(1)}, bf16[96,768]{1,0:T(8,128)(2,1)S(1)}, u32[]{:S(2)}, u32[]{:S(2)}) collective-permute-start(bf16[96,768]{1,0:T(8,128)(2,1)S(1)} %copy.70), channel_id=1, source_target_pairs={{0,2},{1,3},{2,0},{3,1},{4,6},{5,7},{6,4},{7,5},{8,10},{9,11},{10,... | collective-permute-start | bytes 442376 | tf_op jit(solution)/shard_map/ppermute | solution.py:419
  8.2 12.5 %collective-permute-start = (bf16[96,768]{1,0:T(8,128)(2,1)S(1)}, bf16[96,768]{1,0:T(8,128)(2,1)S(1)}, u32[]{:S(2)}, u32[]{:S(2)}) collective-permute-start(bf16[96,768]{1,0:T(8,128)(2,1)S(1)} %copy.70), channel_id=1, source_target_pairs={{0,1},{1,2},{2,3},{3,0},{4,5},{5,6},{6,7},{7,4},{8,9},{9,10},{10,1... | collective-permute-start | bytes 442376 | tf_op jit(solution)/shard_map/ppermute | solution.py:419
  21.6 9.3 %collective-permute-start.5 = (bf16[96,1536]{1,0:T(8,128)(2,1)}, bf16[96,1536]{1,0:T(8,128)(2,1)S(1)}, u32[]{:S(2)}, u32[]{:S(2)}) collective-permute-start(bf16[96,1536]{1,0:T(8,128)(2,1)} %shard_map.254), channel_id=1, source_target_pairs={{0,3},{1,0},{2,1},{3,2},{4,7},{5,4},{6,5},{7,6},{8,11},{9,8},{10,9... | collective-permute-start | bytes 884744 | tf_op jit(solution)/shard_map/ppermute | solution.py:419
  23.1 27.0 %collective-permute-start.4 = (bf16[96,1536]{1,0:T(8,128)(2,1)}, bf16[96,1536]{1,0:T(8,128)(2,1)S(1)}, u32[]{:S(2)}, u32[]{:S(2)}) collective-permute-start(bf16[96,1536]{1,0:T(8,128)(2,1)} %shard_map.254), channel_id=1, source_target_pairs={{0,2},{1,3},{2,0},{3,1},{4,6},{5,7},{6,4},{7,5},{8,10},{9,11},{10,... | collective-permute-start | bytes 884744 | tf_op jit(solution)/shard_map/ppermute | solution.py:419
  24.6 25.5 %collective-permute-start.3 = (bf16[96,1536]{1,0:T(8,128)(2,1)}, bf16[96,1536]{1,0:T(8,128)(2,1)S(1)}, u32[]{:S(2)}, u32[]{:S(2)}) collective-permute-start(bf16[96,1536]{1,0:T(8,128)(2,1)} %shard_map.254), channel_id=1, source_target_pairs={{0,1},{1,2},{2,3},{3,0},{4,5},{5,6},{6,7},{7,4},{8,9},{9,10},{10,1... | collective-permute-start | bytes 884744 | tf_op jit(solution)/shard_map/ppermute | solution.py:419
  26.9 27.8 %collective-permute-start.8 = (bf16[1,4,96,384]{3,2,1,0:T(8,128)(2,1)S(1)}, bf16[1,4,96,384]{3,2,1,0:T(8,128)(2,1)S(1)}, u32[]{:S(2)}, u32[]{:S(2)}) collective-permute-start(bf16[1,4,96,384]{3,2,1,0:T(8,128)(2,1)S(1)} %get-tuple-element.175), channel_id=1, source_target_pairs={{0,8},{4,12},{8,0},{12,4},{1,9},{5,13},{9,1},{13,5},{2,10},{6,14},... | collective-permute-start | bytes 884744 | tf_op jit(solution)/shard_map/ppermute | solution.py:414
  28.5 28.6 %collective-permute-start.12 = (bf16[1,4,96,384]{3,2,1,0:T(8,128)(2,1)S(1)}, bf16[1,4,96,384]{3,2,1,0:T(8,128)(2,1)S(1)}, u32[]{:S(2)}, u32[]{:S(2)}) collective-permute-start(bf16[1,4,96,384]{3,2,1,0:T(8,128)(2,1)S(1)} %get-tuple-element.174), channel_id=1, source_target_pairs={{0,16},{16,0},{1,17},{17,1},{2,18},{18,2},{3,19},{19,3},{4,20},{20... | collective-permute-start | bytes 884744 | tf_op jit(solution)/shard_map/ppermute | solution.py:414
  53.2 18.4 %collective-permute-start.6 = (bf16[1,4,96,768]{3,2,1,0:T(8,128)(2,1)}, bf16[1,4,96,768]{3,2,1,0:T(8,128)(2,1)}, u32[]{:S(2)}, u32[]{:S(2)}) collective-permute-start(bf16[1,4,96,768]{3,2,1,0:T(8,128)(2,1)} %get-tuple-element.166), channel_id=1, source_target_pairs={{0,8},{4,12},{8,0},{12,4},{1,9},{5,13},{9,1},{13,5},{2,10},{6,14},... | collective-permute-start | bytes 1769480 | tf_op jit(solution)/shard_map/ppermute | solution.py:414
  55.6 16.5 %collective-permute-start.9 = (bf16[2,4,96,384]{3,2,1,0:T(8,128)(2,1)}, bf16[2,4,96,384]{3,2,1,0:T(8,128)(2,1)S(1)}, u32[]{:S(2)}, u32[]{:S(2)}) collective-permute-start(bf16[2,4,96,384]{3,2,1,0:T(8,128)(2,1)} %pad_maximum_fusion.4.__2_.rest_0_), channel_id=1, source_target_pairs={{0,16},{16,0},{1,17},{17,1},{2,18},{18,2},{3,19},{19,3},{4,20},{20... | collective-permute-start | bytes 1769480 | tf_op jit(solution)/shard_map/ppermute | solution.py:414
  58.0 21.8 %collective-permute-start.13 = (bf16[2,4,96,384]{3,2,1,0:T(8,128)(2,1)}, bf16[2,4,96,384]{3,2,1,0:T(8,128)(2,1)S(1)}, u32[]{:S(2)}, u32[]{:S(2)}) collective-permute-start(bf16[2,4,96,384]{3,2,1,0:T(8,128)(2,1)} %pad_maximum_fusion.5.__6_.rest_4_), channel_id=1, source_target_pairs={{0,8},{4,12},{8,0},{12,4},{1,9},{5,13},{9,1},{13,5},{2,10},{6,14},... | collective-permute-start | bytes 1769480 | tf_op jit(solution)/shard_map/ppermute | solution.py:414
  68.8 15.5 %collective-permute-start.7 = (bf16[1,4,96,768]{3,2,1,0:T(8,128)(2,1)}, bf16[1,4,96,768]{3,2,1,0:T(8,128)(2,1)}, u32[]{:S(2)}, u32[]{:S(2)}) collective-permute-start(bf16[1,4,96,768]{3,2,1,0:T(8,128)(2,1)} %get-tuple-element.165), channel_id=1, source_target_pairs={{0,16},{16,0},{1,17},{17,1},{2,18},{18,2},{3,19},{19,3},{4,20},{20... | collective-permute-start | bytes 1769480 | tf_op jit(solution)/shard_map/ppermute | solution.py:414
  71.6 15.0 %collective-permute-start.10 = (bf16[2,4,96,384]{3,2,1,0:T(8,128)(2,1)}, bf16[2,4,96,384]{3,2,1,0:T(8,128)(2,1)S(1)}, u32[]{:S(2)}, u32[]{:S(2)}) collective-permute-start(bf16[2,4,96,384]{3,2,1,0:T(8,128)(2,1)} %pad_maximum_fusion.4.__2_.rest_0_), channel_id=1, source_target_pairs={{0,4},{4,0},{8,12},{12,8},{1,5},{5,1},{9,13},{13,9},{2,6},{6,2},{1... | collective-permute-start | bytes 1769480 | tf_op jit(solution)/shard_map/ppermute | solution.py:414
  71.6 15.0 %collective-permute-start.14 = (bf16[2,4,96,384]{3,2,1,0:T(8,128)(2,1)}, bf16[2,4,96,384]{3,2,1,0:T(8,128)(2,1)S(1)}, u32[]{:S(2)}, u32[]{:S(2)}) collective-permute-start(bf16[2,4,96,384]{3,2,1,0:T(8,128)(2,1)} %pad_maximum_fusion.5.__6_.rest_4_), channel_id=1, source_target_pairs={{0,4},{4,0},{8,12},{12,8},{1,5},{5,1},{9,13},{13,9},{2,6},{6,2},{1... | collective-permute-start | bytes 1769480 | tf_op jit(solution)/shard_map/ppermute | solution.py:414
  72.1 14.5 %collective-permute-start.11 = (bf16[2,4,96,384]{3,2,1,0:T(8,128)(2,1)S(1)}, bf16[2,4,96,384]{3,2,1,0:T(8,128)(2,1)S(1)}, u32[]{:S(2)}, u32[]{:S(2)}) collective-permute-start(bf16[2,4,96,384]{3,2,1,0:T(8,128)(2,1)S(1)} %collective-permute-done.9.__3_.rest_1_), channel_id=1, source_target_pairs={{0,4},{4,0},{8,12},{12,8},{1,5},{5,1},{9,13},{13,9},{2,6},{6,2},{1... | collective-permute-start | bytes 1769480 | tf_op jit(solution)/shard_map/ppermute | solution.py:414
  79.9 6.8 %collective-permute-start.15 = (bf16[2,4,96,384]{3,2,1,0:T(8,128)(2,1)S(1)}, bf16[2,4,96,384]{3,2,1,0:T(8,128)(2,1)S(1)}, u32[]{:S(2)}, u32[]{:S(2)}) collective-permute-start(bf16[2,4,96,384]{3,2,1,0:T(8,128)(2,1)S(1)} %collective-permute-done.13.__7_.rest_5_), channel_id=1, source_target_pairs={{0,4},{4,0},{8,12},{12,8},{1,5},{5,1},{9,13},{13,9},{2,6},{6,2},{1... | collective-permute-start | bytes 1769480 | tf_op jit(solution)/shard_map/ppermute | solution.py:414
  88.7 42.2 %collective-permute-start.16 = (bf16[2,4,96,768]{3,2,1,0:T(8,128)(2,1)}, bf16[2,4,96,768]{3,2,1,0:T(8,128)(2,1)S(1)}, u32[]{:S(2)}, u32[]{:S(2)}) collective-permute-start(bf16[2,4,96,768]{3,2,1,0:T(8,128)(2,1)} %get-tuple-element.69.rest_13_.rest_0_), channel_id=1, source_target_pairs={{0,16},{16,0},{1,17},{17,1},{2,18},{18,2},{3,19},{19,3},{4,20},{20... | collective-permute-start | bytes 3538952 | tf_op jit(solution)/shard_map/ppermute | solution.py:414
  90.2 40.7 %collective-permute-start.18 = (bf16[2,4,96,768]{3,2,1,0:T(8,128)(2,1)}, bf16[2,4,96,768]{3,2,1,0:T(8,128)(2,1)S(1)}, u32[]{:S(2)}, u32[]{:S(2)}) collective-permute-start(bf16[2,4,96,768]{3,2,1,0:T(8,128)(2,1)} %get-tuple-element.69.rest_13_.rest_0_), channel_id=1, source_target_pairs={{0,4},{4,0},{8,12},{12,8},{1,5},{5,1},{9,13},{13,9},{2,6},{6,2},{1... | collective-permute-start | bytes 3538952 | tf_op jit(solution)/shard_map/ppermute | solution.py:414
  90.4 40.5 %collective-permute-start.17 = (bf16[2,4,96,768]{3,2,1,0:T(8,128)(2,1)}, bf16[2,4,96,768]{3,2,1,0:T(8,128)(2,1)S(1)}, u32[]{:S(2)}, u32[]{:S(2)}) collective-permute-start(bf16[2,4,96,768]{3,2,1,0:T(8,128)(2,1)} %get-tuple-element.70.rest_4_), channel_id=1, source_target_pairs={{0,8},{4,12},{8,0},{12,4},{1,9},{5,13},{9,1},{13,5},{2,10},{6,14},... | collective-permute-start | bytes 3538952 | tf_op jit(solution)/shard_map/ppermute | solution.py:414
  91.8 40.1 %collective-permute-start.19 = (bf16[2,4,96,768]{3,2,1,0:T(8,128)(2,1)}, bf16[2,4,96,768]{3,2,1,0:T(8,128)(2,1)}, u32[]{:S(2)}, u32[]{:S(2)}) collective-permute-start(bf16[2,4,96,768]{3,2,1,0:T(8,128)(2,1)} %get-tuple-element.70.rest_4_), channel_id=1, source_target_pairs={{0,4},{4,0},{8,12},{12,8},{1,5},{5,1},{9,13},{13,9},{2,6},{6,2},{1... | collective-permute-start | bytes 3538952 | tf_op jit(solution)/shard_map/ppermute | solution.py:414
  132.9 39.8 %collective-permute-start.20 = (bf16[2,4,96,768]{3,2,1,0:T(8,128)(2,1)}, bf16[2,4,96,768]{3,2,1,0:T(8,128)(2,1)S(1)}, u32[]{:S(2)}, u32[]{:S(2)}) collective-permute-start(bf16[2,4,96,768]{3,2,1,0:T(8,128)(2,1)} %get-tuple-element.79.rest_13_.rest_1_), channel_id=1, source_target_pairs={{0,4},{4,0},{8,12},{12,8},{1,5},{5,1},{9,13},{13,9},{2,6},{6,2},{1... | collective-permute-start | bytes 3538952 | tf_op jit(solution)/shard_map/ppermute | solution.py:414
  133.4 39.3 %collective-permute-start.21 = (bf16[2,4,96,768]{3,2,1,0:T(8,128)(2,1)}, bf16[2,4,96,768]{3,2,1,0:T(8,128)(2,1)S(1)}, u32[]{:S(2)}, u32[]{:S(2)}) collective-permute-start(bf16[2,4,96,768]{3,2,1,0:T(8,128)(2,1)} %get-tuple-element.80.rest_5_), channel_id=1, source_target_pairs={{0,4},{4,0},{8,12},{12,8},{1,5},{5,1},{9,13},{13,9},{2,6},{6,2},{1... | collective-permute-start | bytes 3538952 | tf_op jit(solution)/shard_map/ppermute | solution.py:414
  175.6 29.7 %collective-permute-start.22 = (bf16[8,4,96,384]{3,2,1,0:T(8,128)(2,1)}, bf16[8,4,96,384]{3,2,1,0:T(8,128)(2,1)S(1)}, u32[]{:S(2)}, u32[]{:S(2)}) collective-permute-start(bf16[8,4,96,384]{3,2,1,0:T(8,128)(2,1)} %shard_map.260.rest_9_), channel_id=1, source_target_pairs={{0,4},{4,0},{8,12},{12,8},{1,5},{5,1},{9,13},{13,9},{2,6},{6,2},{1... | collective-permute-start | bytes 7077896 | tf_op jit(solution)/shard_map/ppermute | solution.py:414
  208.1 29.1 %collective-permute-start.25 = (bf16[8,2,96,768]{3,2,1,0:T(8,128)(2,1)}, bf16[8,2,96,768]{3,2,1,0:T(8,128)(2,1)S(1)}, u32[]{:S(2)}, u32[]{:S(2)}) collective-permute-start(bf16[8,2,96,768]{3,2,1,0:T(8,128)(2,1)} %get-tuple-element.98), channel_id=1, source_target_pairs={{0,4},{4,0},{8,12},{12,8},{1,5},{5,1},{9,13},{13,9},{2,6},{6,2},{1... | collective-permute-start | bytes 7077896 | tf_op jit(solution)/shard_map/ppermute | solution.py:414
  212.7 23.0 %collective-permute-start.23 = (bf16[2,4,96,384]{3,2,1,0:T(8,128)(2,1)S(1)}, bf16[2,4,96,384]{3,2,1,0:T(8,128)(2,1)S(1)}, u32[]{:S(2)}, u32[]{:S(2)}) collective-permute-start(bf16[2,4,96,384]{3,2,1,0:T(8,128)(2,1)S(1)} %get-tuple-element.162), channel_id=1, source_target_pairs={{0,8},{4,12},{8,0},{12,4},{1,9},{5,13},{9,1},{13,5},{2,10},{6,14},... | collective-permute-start | bytes 1769480 | tf_op jit(solution)/shard_map/ppermute | solution.py:414
  213.2 23.9 %collective-permute-start.24 = (bf16[2,4,96,384]{3,2,1,0:T(8,128)(2,1)S(1)}, bf16[2,4,96,384]{3,2,1,0:T(8,128)(2,1)S(1)}, u32[]{:S(2)}, u32[]{:S(2)}) collective-permute-start(bf16[2,4,96,384]{3,2,1,0:T(8,128)(2,1)S(1)} %get-tuple-element.161), channel_id=1, source_target_pairs={{0,16},{16,0},{1,17},{17,1},{2,18},{18,2},{3,19},{19,3},{4,20},{20... | collective-permute-start | bytes 1769480 | tf_op jit(solution)/shard_map/ppermute | solution.py:414
  239.0 29.0 %collective-permute-start.30 = (bf16[8,2,96,768]{3,2,1,0:T(8,128)(2,1)}, bf16[8,2,96,768]{3,2,1,0:T(8,128)(2,1)}, u32[]{:S(2)}, u32[]{:S(2)}) collective-permute-start(bf16[8,2,96,768]{3,2,1,0:T(8,128)(2,1)} %get-tuple-element.107), channel_id=1, source_target_pairs={{0,4},{4,0},{8,12},{12,8},{1,5},{5,1},{9,13},{13,9},{2,6},{6,2},{1... | collective-permute-start | bytes 7077896 | tf_op jit(solution)/shard_map/ppermute | solution.py:414
  243.8 20.7 %collective-permute-start.26 = (bf16[1,4,96,384]{3,2,1,0:T(8,128)(2,1)S(1)}, bf16[1,4,96,384]{3,2,1,0:T(8,128)(2,1)S(1)}, u32[]{:S(2)}, u32[]{:S(2)}) collective-permute-start(bf16[1,4,96,384]{3,2,1,0:T(8,128)(2,1)S(1)} %add_convert_fusion.29), channel_id=1, source_target_pairs={{0,16},{16,0},{1,17},{17,1},{2,18},{18,2},{3,19},{19,3},{4,20},{20... | collective-permute-start | bytes 884744 | tf_op jit(solution)/shard_map/ppermute | solution.py:414
  246.6 17.9 %collective-permute-start.27 = (bf16[1,4,96,384]{3,2,1,0:T(8,128)(2,1)S(1)}, bf16[1,4,96,384]{3,2,1,0:T(8,128)(2,1)S(1)}, u32[]{:S(2)}, u32[]{:S(2)}) collective-permute-start(bf16[1,4,96,384]{3,2,1,0:T(8,128)(2,1)S(1)} %add_convert_fusion.28), channel_id=1, source_target_pairs={{0,8},{4,12},{8,0},{12,4},{1,9},{5,13},{9,1},{13,5},{2,10},{6,14},... | collective-permute-start | bytes 884744 | tf_op jit(solution)/shard_map/ppermute | solution.py:414
  252.3 15.6 %collective-permute-start.28 = (bf16[2,2,96,768]{3,2,1,0:T(8,128)(2,1)S(1)}, bf16[2,2,96,768]{3,2,1,0:T(8,128)(2,1)}, u32[]{:S(2)}, u32[]{:S(2)}) collective-permute-start(bf16[2,2,96,768]{3,2,1,0:T(8,128)(2,1)S(1)} %get-tuple-element.158), channel_id=1, source_target_pairs={{0,8},{4,12},{8,0},{12,4},{1,9},{5,13},{9,1},{13,5},{2,10},{6,14},... | collective-permute-start | bytes 1769480 | tf_op jit(solution)/shard_map/ppermute | solution.py:414
  252.9 15.1 %collective-permute-start.29 = (bf16[2,2,96,768]{3,2,1,0:T(8,128)(2,1)S(1)}, bf16[2,2,96,768]{3,2,1,0:T(8,128)(2,1)}, u32[]{:S(2)}, u32[]{:S(2)}) collective-permute-start(bf16[2,2,96,768]{3,2,1,0:T(8,128)(2,1)S(1)} %get-tuple-element.157), channel_id=1, source_target_pairs={{0,16},{16,0},{1,17},{17,1},{2,18},{18,2},{3,19},{19,3},{4,20},{20... | collective-permute-start | bytes 1769480 | tf_op jit(solution)/shard_map/ppermute | solution.py:414
  270.0 34.8 %collective-permute-start.31 = (bf16[1,2,96,768]{3,2,1,0:T(8,128)(2,1)}, bf16[1,2,96,768]{3,2,1,0:T(8,128)(2,1)}, u32[]{:S(2)}, u32[]{:S(2)}) collective-permute-start(bf16[1,2,96,768]{3,2,1,0:T(8,128)(2,1)} %add_convert_fusion.27), channel_id=1, source_target_pairs={{0,16},{16,0},{1,17},{17,1},{2,18},{18,2},{3,19},{19,3},{4,20},{20... | collective-permute-start | bytes 884744 | tf_op jit(solution)/shard_map/ppermute | solution.py:414
  272.3 32.5 %collective-permute-start.32 = (bf16[1,2,96,768]{3,2,1,0:T(8,128)(2,1)}, bf16[1,2,96,768]{3,2,1,0:T(8,128)(2,1)}, u32[]{:S(2)}, u32[]{:S(2)}) collective-permute-start(bf16[1,2,96,768]{3,2,1,0:T(8,128)(2,1)} %add_convert_fusion.26), channel_id=1, source_target_pairs={{0,8},{4,12},{8,0},{12,4},{1,9},{5,13},{9,1},{13,5},{2,10},{6,14},... | collective-permute-start | bytes 884744 | tf_op jit(solution)/shard_map/ppermute | solution.py:414
  275.5 8.7 %collective-permute-start.42 = (bf16[96,768]{1,0:T(8,128)(2,1)S(1)}, bf16[96,768]{1,0:T(8,128)(2,1)S(1)}, u32[]{:S(2)}, u32[]{:S(2)}) collective-permute-start(bf16[96,768]{1,0:T(8,128)(2,1)S(1)} %get-tuple-element.172), channel_id=1, source_target_pairs={{0,1},{1,2},{2,3},{3,0},{4,5},{5,6},{6,7},{7,4},{8,9},{9,10},{10,1... | collective-permute-start | bytes 442376 | tf_op jit(solution)/shard_map/ppermute | solution.py:419
  275.6 12.3 %collective-permute-start.41 = (bf16[96,768]{1,0:T(8,128)(2,1)S(1)}, bf16[96,768]{1,0:T(8,128)(2,1)S(1)}, u32[]{:S(2)}, u32[]{:S(2)}) collective-permute-start(bf16[96,768]{1,0:T(8,128)(2,1)S(1)} %get-tuple-element.173), channel_id=1, source_target_pairs={{0,2},{1,3},{2,0},{3,1},{4,6},{5,7},{6,4},{7,5},{8,10},{9,11},{10,... | collective-permute-start | bytes 442376 | tf_op jit(solution)/shard_map/ppermute | solution.py:419
  277.4 12.0 %collective-permute-start.40 = (bf16[96,768]{1,0:T(8,128)(2,1)S(1)}, bf16[96,768]{1,0:T(8,128)(2,1)S(1)}, u32[]{:S(2)}, u32[]{:S(2)}) collective-permute-start(bf16[96,768]{1,0:T(8,128)(2,1)S(1)} %get-tuple-element.171), channel_id=1, source_target_pairs={{0,3},{1,0},{2,1},{3,2},{4,7},{5,4},{6,5},{7,6},{8,11},{9,8},{10,9... | collective-permute-start | bytes 442376 | tf_op jit(solution)/shard_map/ppermute | solution.py:419
  284.2 20.7 %collective-permute-start.33 = (bf16[2,2,96,768]{3,2,1,0:T(8,128)(2,1)}, bf16[2,2,96,768]{3,2,1,0:T(8,128)(2,1)}, u32[]{:S(2)}, u32[]{:S(2)}) collective-permute-start(bf16[2,2,96,768]{3,2,1,0:T(8,128)(2,1)} %get-tuple-element.154), channel_id=1, source_target_pairs={{0,8},{4,12},{8,0},{12,4},{1,9},{5,13},{9,1},{13,5},{2,10},{6,14},... | collective-permute-start | bytes 1769480 | tf_op jit(solution)/shard_map/ppermute | solution.py:414
  287.8 17.1 %collective-permute-start.34 = (bf16[2,2,96,768]{3,2,1,0:T(8,128)(2,1)}, bf16[2,2,96,768]{3,2,1,0:T(8,128)(2,1)}, u32[]{:S(2)}, u32[]{:S(2)}) collective-permute-start(bf16[2,2,96,768]{3,2,1,0:T(8,128)(2,1)} %get-tuple-element.153), channel_id=1, source_target_pairs={{0,16},{16,0},{1,17},{17,1},{2,18},{18,2},{3,19},{19,3},{4,20},{20... | collective-permute-start | bytes 1769480 | tf_op jit(solution)/shard_map/ppermute | solution.py:414
  289.4 15.2 %collective-permute-start.43 = (bf16[96,768]{1,0:T(8,128)(2,1)S(1)}, bf16[96,768]{1,0:T(8,128)(2,1)S(1)}, u32[]{:S(2)}, u32[]{:S(2)}) collective-permute-start(bf16[96,768]{1,0:T(8,128)(2,1)S(1)} %fusion.16), channel_id=1, source_target_pairs={{0,16},{16,0},{1,17},{17,1},{2,18},{18,2},{3,19},{19,3},{4,20},{20... | collective-permute-start | bytes 442376 | tf_op jit(solution)/shard_map/ppermute | solution.py:414
  307.0 21.2 %collective-permute-start.47 = (bf16[1,2,96,768]{3,2,1,0:T(8,128)(2,1)S(1)}, bf16[1,2,96,768]{3,2,1,0:T(8,128)(2,1)S(1)}, u32[]{:S(2)}, u32[]{:S(2)}) collective-permute-start(bf16[1,2,96,768]{3,2,1,0:T(8,128)(2,1)S(1)} %add_convert_fusion.13), channel_id=1, source_target_pairs={{0,8},{4,12},{8,0},{12,4},{1,9},{5,13},{9,1},{13,5},{2,10},{6,14},... | collective-permute-start | bytes 884744 | tf_op jit(solution)/shard_map/ppermute | solution.py:414
  308.2 9.1 %collective-permute-start.36 = (f32[72,128]{1,0:T(8,128)S(1)}, f32[72,128]{1,0:T(8,128)S(1)}, u32[]{:S(2)}, u32[]{:S(2)}) collective-permute-start(f32[72,128]{1,0:T(8,128)S(1)} %fusion.30), channel_id=1, source_target_pairs={{0,8},{4,12},{8,0},{12,4},{1,9},{5,13},{9,1},{13,5},{2,10},{6,14},... | collective-permute-start | bytes 110600 | tf_op jit(solution)/shard_map/ppermute | solution.py:414
  310.3 19.0 %collective-permute-start.46 = (bf16[1,2,96,768]{3,2,1,0:T(8,128)(2,1)S(1)}, bf16[1,2,96,768]{3,2,1,0:T(8,128)(2,1)S(1)}, u32[]{:S(2)}, u32[]{:S(2)}) collective-permute-start(bf16[1,2,96,768]{3,2,1,0:T(8,128)(2,1)S(1)} %add_convert_fusion.16), channel_id=1, source_target_pairs={{0,16},{16,0},{1,17},{17,1},{2,18},{18,2},{3,19},{19,3},{4,20},{20... | collective-permute-start | bytes 884744 | tf_op jit(solution)/shard_map/ppermute | solution.py:414
  321.3 5.6 %collective-permute-start.38 = (f32[72,128]{1,0:T(8,128)S(1)}, f32[72,128]{1,0:T(8,128)S(1)}, u32[]{:S(2)}, u32[]{:S(2)}) collective-permute-start(f32[72,128]{1,0:T(8,128)S(1)} %add.207), channel_id=1, source_target_pairs={{0,1},{1,0},{2,3},{3,2},{4,5},{5,4},{6,7},{7,6},{8,9},{9,8},{10,11... | collective-permute-start | bytes 110600 | tf_op jit(solution)/shard_map/ppermute | solution.py:414
  324.4 24.3 %collective-permute-start.45 = (bf16[96,1536]{1,0:T(8,128)(2,1)}, bf16[96,1536]{1,0:T(8,128)(2,1)S(1)}, u32[]{:S(2)}, u32[]{:S(2)}) collective-permute-start(bf16[96,1536]{1,0:T(8,128)(2,1)} %get-tuple-element.170), channel_id=1, source_target_pairs={{0,1},{1,2},{2,3},{3,0},{4,5},{5,6},{6,7},{7,4},{8,9},{9,10},{10,1... | collective-permute-start | bytes 884744 | tf_op jit(solution)/shard_map/ppermute | solution.py:419
  324.4 24.3 %collective-permute-start.44 = (bf16[96,1536]{1,0:T(8,128)(2,1)}, bf16[96,1536]{1,0:T(8,128)(2,1)S(1)}, u32[]{:S(2)}, u32[]{:S(2)}) collective-permute-start(bf16[96,1536]{1,0:T(8,128)(2,1)} %get-tuple-element.169), channel_id=1, source_target_pairs={{0,2},{1,3},{2,0},{3,1},{4,6},{5,7},{6,4},{7,5},{8,10},{9,11},{10,... | collective-permute-start | bytes 884744 | tf_op jit(solution)/shard_map/ppermute | solution.py:419
  326.9 21.2 %collective-permute-start.39 = (f32[72,128]{1,0:T(8,128)S(1)}, f32[72,128]{1,0:T(8,128)S(1)}, u32[]{:S(2)}, u32[]{:S(2)}) collective-permute-start(f32[72,128]{1,0:T(8,128)S(1)} %add.208), channel_id=1, source_target_pairs={{0,2},{1,3},{2,0},{3,1},{4,6},{5,7},{6,4},{7,5},{8,10},{9,11},{10,... | collective-permute-start | bytes 110600 | tf_op jit(solution)/shard_map/ppermute | solution.py:414
  331.1 17.6 %collective-permute-start.48 = (bf16[96,1536]{1,0:T(8,128)(2,1)}, bf16[96,1536]{1,0:T(8,128)(2,1)}, u32[]{:S(2)}, u32[]{:S(2)}) collective-permute-start(bf16[96,1536]{1,0:T(8,128)(2,1)} %fusion.12), channel_id=1, source_target_pairs={{0,3},{1,0},{2,1},{3,2},{4,7},{5,4},{6,5},{7,6},{8,11},{9,8},{10,9... | collective-permute-start | bytes 884744 | tf_op jit(solution)/shard_map/ppermute | solution.py:419
  349.9 6.9 %collective-permute-start.49 = (bf16[96,1536]{1,0:T(8,128)(2,1)S(1)}, bf16[96,1536]{1,0:T(8,128)(2,1)S(1)}, u32[]{:S(2)}, u32[]{:S(2)}) collective-permute-start(bf16[96,1536]{1,0:T(8,128)(2,1)S(1)} %fusion.1), channel_id=1, source_target_pairs={{0,16},{16,0},{1,17},{17,1},{2,18},{18,2},{3,19},{19,3},{4,20},{20... | collective-permute-start | bytes 884744 | tf_op jit(solution)/shard_map/ppermute | solution.py:414
  (162 other events, 573.1 us)

commit v5 on v4

--- a/solution.py
+++ b/solution.py
@@ -127,7 +127,7 @@
         + [full(length, 2 * HD)] * 3 + [full(length, length)],
         out_shape=[shaped((length, width), BF16), shaped((width, length), BF16)] * 2
         + [shaped((width, length), BF16)] + [table] * 3 + [shaped((length, length), F32)],
-        compiler_params=pltpu.CompilerParams(vmem_limit_bytes=24 * 2**20),
+        compiler_params=pltpu.CompilerParams(vmem_limit_bytes=60 * 2**20),
         cost_estimate=cost(6),
     )(tokens, cot, *gains, seg_row[:, None], seg_row[None, :], freq)
 
@@ -278,7 +278,7 @@
         + [shaped((count, 1, cols), F32)] + [shaped((pieces, g_blocks, rows, g_cols), BF16)] * 2,
         input_output_aliases={fixed - 2: len(mid_cols) + 1, fixed - 1: len(mid_cols) + 2} if into else {},
         scratch_shapes=scratch,
-        compiler_params=pltpu.CompilerParams(vmem_limit_bytes=30 * 2**20),
+        compiler_params=pltpu.CompilerParams(vmem_limit_bytes=60 * 2**20),
         cost_estimate=cost(us * count),
     )(me, norm, norm_t, cot, cot_t, *left, *right, *vectors, *after)
 
@@ -317,21 +317,22 @@
         dna_ref[rows, :] += dot_nt(dqkv_scr[rows, :], w_scr[...])
 
 
-def mlp_tail_kernel(orders, core_bit, calls, per_call, waits, me_ref, *rest):
-    left, right, rest = rest[:4], rest[4:8], rest[8:]
-    dh_refs, act_refs, rest = rest[:calls], rest[calls : 2 * calls], rest[2 * calls :]
-    branch_in, dna_ref, x_ref, cot_ref, ga_ref, gm_ref, bo_ref, bd_ref = rest[:8]
-    block_ref, grad_ref, stats_ref, branch_ref, dnm_ref, wu_scr, wd_scr, dh_scr, act_scr = rest[8 + waits :]
-    length = x_ref.shape[0]
+def mlp_tail_kernel(orders, core_bit, last, waits, me_ref, *rest):
+    left, right, dh_ref, act_ref, rest = rest[:4], rest[4:8], rest[8], rest[9], rest[10:]
+    if last:
+        branch_in, dnm_in, dna_ref, x_ref, cot_ref, ga_ref, gm_ref, bo_ref, bd_ref = rest[:9]
+        block_ref, grad_ref, stats_ref, branch_ref, dnm_ref, wu_scr, wd_scr = rest[9 + waits :]
+    else:
+        branch_in = rest[0]
+        branch_ref, dnm_ref, wu_scr, wd_scr = rest[1 + waits :]
+    length = branch_ref.shape[0]
     step = pl.program_id(0)
 
     @pl.when(step == 0)
     def _():
         branch_ref[...] = branch_in[...]
-        dnm_ref[...] = jnp.zeros_like(dnm_ref)
-
-    pick(dh_refs, per_call, dh_scr)
-    pick(act_refs, per_call, act_scr)
+        dnm_ref[...] = dnm_in[...] if last else jnp.zeros_like(dnm_ref)
+
     assemble(me_ref, left, gathered_order(orders[0], core_bit), wu_scr, 0)
     assemble(me_ref, right, gathered_order(orders[1], core_bit), wd_scr, 0)
     tile = 256
@@ -339,8 +340,11 @@
     @pl.loop(0, length // tile)
     def _(t):
         rows = pl.ds(pl.multiple_of(t * tile, tile), tile)
-        branch_ref[rows, :] += dot_nt(act_scr[rows, :], wd_scr[...])
-        dnm_ref[rows, :] += dot_nt(dh_scr[rows, :], wu_scr[...])
+        branch_ref[rows, :] += dot_nt(act_ref[0, rows, :], wd_scr[...])
+        dnm_ref[rows, :] += dot_nt(dh_ref[0, rows, :], wu_scr[...])
+
+    if not last:
+        return
 
     @pl.when(step == pl.num_programs(0) - 1)
     def _():
@@ -366,7 +370,7 @@
                 stats_ref[at : at + 1, :] += jnp.sum(term, axis=0, keepdims=True)
 
 
-def tail_part(kernel, block_of, per_call, orders, core_bit, after, me, left, right, mids, extra, outs, scratch, us):
+def attention_tail_part(block_of, per_call, orders, core_bit, after, me, left, right, mids, outs, scratch, us):
     steps = left[0].shape[1]
     calls = steps // per_call
 
@@ -376,17 +380,32 @@
 
     kept = [pltpu.VMEM(group[0].shape[1:], BF16) for group in mids]
     return pl.pallas_call(
-        functools.partial(kernel, orders, core_bit, calls, per_call, len(after)),
+        functools.partial(attention_tail_kernel, orders, core_bit, calls, per_call, len(after)),
         grid=(steps,),
         in_specs=[SCALAR] + [weight_spec(w, block_of) for w in left + right]
-        + [mid_spec(array, n) for group in mids for n, array in enumerate(group)]
+        + [mid_spec(array, n) for group in mids for n, array in enumerate(group)] + [ANY] * len(after),
+        out_specs=[full(*o.shape) for o in outs],
+        out_shape=outs,
+        scratch_shapes=scratch + kept,
+        compiler_params=pltpu.CompilerParams(vmem_limit_bytes=60 * 2**20),
+        cost_estimate=cost(us),
+    )(me, *left, *right, *[array for group in mids for array in group], *after)
+
+
+def mlp_tail_part(k0, last, orders, core_bit, after, me, left, right, dh, act, extra, outs, scratch, us):
+    count, length, cols = dh.shape
+    mid_spec = pl.BlockSpec((1, length, cols), lambda s: (s, 0, 0))
+    return pl.pallas_call(
+        functools.partial(mlp_tail_kernel, orders, core_bit, last, len(after)),
+        grid=(count,),
+        in_specs=[SCALAR] + [weight_spec(w, lambda s: k0 + s) for w in left + right] + [mid_spec] * 2
         + [full(*e.shape) for e in extra] + [ANY] * len(after),
         out_specs=[full(*o.shape) for o in outs],
         out_shape=outs,
-        scratch_shapes=scratch + kept,
-        compiler_params=pltpu.CompilerParams(vmem_limit_bytes=40 * 2**20),
+        scratch_shapes=scratch,
+        compiler_params=pltpu.CompilerParams(vmem_limit_bytes=60 * 2**20),
         cost_estimate=cost(us),
-    )(me, *left, *right, *[array for group in mids for array in group], *extra, *after)
+    )(me, *left, *right, dh, act, *extra, *after)
 
 
 def fence_kernel(*_):
@@ -523,19 +542,33 @@
         ],
         axis=1,
     )
-    def gather_col(own):
-        return jnp.stack([own] + [shifted(own, k) for k in range(1, col_size)])
-
-    attn_all = gather_col(attn_own)
     cut = block_cols // 2
-    attn_left = gather_pieces(attn_all[:, :, :cut], orders[0], core_bit)
-    attn_right = gather_pieces(attn_all[:, :, cut:], orders[1], core_bit)
+    attn_all = jnp.stack([attn_own] + [shifted(attn_own, k) for k in range(1, col_size)])
 
     seg_row = lax.dynamic_index_in_dim(segment_ids, row_id * col_size + col_id, axis=0, keepdims=False)
     na, na_t, nm, nm_t, cot_t, keep, ahead, behind, mask = prep_part(
         tokens_in, out_cotangent, [v[None, :] for v in (attn_gain, attn_shift, mlp_gain, mlp_shift)], seg_row,
     )
-    mlp_all = gather_col(fence([mlp_own], [attn_all])[0])
+    mlp_own = fence([mlp_own], [attn_all])[0]
+    attn_held = [attn_all[None, :, :, :cut], attn_all[None, :, :, cut:]]
+    mlp_parts = [shifted(mlp_own, k) for k in range(1, col_size)]
+    for at in range(len(orders[0]) - 1):
+        came = [swap(one, order[at]) for one, order in zip(attn_held, orders)]
+        came = fence(came, [na])
+        attn_held = [jnp.concatenate(pair, axis=0) for pair in zip(attn_held, came)]
+    came = [swap(one, order[-1]) for one, order in zip(attn_held, orders)]
+    over = [swap(one, core_bit) for one in attn_held]
+    came = fence(came + mlp_parts, over)
+    came, mlp_parts = came[:2], came[2:]
+    came_over = [swap(one, core_bit) for one in came]
+    attn_left, attn_right = ([attn_held[i], came[i], over[i], came_over[i]] for i in range(2))
+    mlp_all = jnp.stack([mlp_own] + list(mlp_parts))
+    mlp_held = [mlp_all[None, :, :, :up_cols], mlp_all[None, :, :, up_cols:]]
+    for at in range(len(orders[0]) - 1):
+        came = [swap(one, order[at]) for one, order in zip(mlp_held, orders)]
+        came = fence(came, came_over)
+        mlp_held = [jnp.concatenate(pair, axis=0) for pair in zip(mlp_held, came)]
+
     blocks_here = (col_id - jnp.arange(col_size)) % col_size
     head_bias = jnp.pad(
         qkv_bias.reshape(col_size, local_heads, QKV), ((0, 0), (0, 0), (0, HEAD - QKV))
@@ -549,12 +582,6 @@
 
     def block_of(s):
         return (calls - 1 - s // per_call) * per_call + s % per_call
-
-    def held_until_last(own, order):
-        held = own[None]
-        for bit in order[:-1]:
-            held = jnp.concatenate([held, swap(held, bit)], axis=0)
-        return held
 
     def attention_call(k0, after, into):
         return block_part(
@@ -574,21 +601,19 @@
             up, down, [hidden_bias], [up_cols, up_cols], up_cols, [pltpu.VMEM((width, up_cols), BF16)] * 3, 6,
         )
 
-    held = [held_until_last(mlp_all[:, :, :up_cols], orders[0]), held_until_last(mlp_all[:, :, up_cols:], orders[1])]
-    held = list(fence(held, [w for w in attn_left + attn_right]))
-    came = [swap(one, order[-1]) for one, order in zip(held, orders)]
-    held_over = [swap(one, core_bit) for one in held]
+    came = [swap(one, order[-1]) for one, order in zip(mlp_held, orders)]
+    held_over = [swap(one, core_bit) for one in mlp_held]
 
     attn_calls, into = [], []
     for n, k0 in enumerate(starts):
-        outs = attention_call(k0, [held[0]] if n == 0 else [came[0]], into)
+        outs = attention_call(k0, [mlp_held[0]] if n == 0 else [came[0]], into)
         attn_calls.append(outs[:3])
         into = list(outs[3:])
         if n == 0:
             came = list(fence(came, [outs[2]] + held_over))
             came_over = [swap(one, core_bit) for one in came]
     attn_sum = Reduction(into[0], into[1], orders, core_bit)
-    up, down = ([held[i], came[i], held_over[i], came_over[i]] for i in range(2))
+    up, down = ([mlp_held[i], came[i], held_over[i], came_over[i]] for i in range(2))
 
     token = phase([attn_sum], [], came_over)
     mlp_calls, mlp_sums = [], []
@@ -598,46 +623,53 @@
         mlp_sums.append(Reduction(g_keep, g_send, orders, core_bit))
         token = phase([attn_sum] + mlp_sums, [], [mids[2]])
 
-    branch, d_norm_attn = tail_part(
-        attention_tail_kernel, block_of, per_call, orders, core_bit, token[:1], me, attn_left, attn_right,
-        [[c[0] for c in attn_calls], [c[1] for c in attn_calls]], [], [shaped((length, width), F32)] * 2,
+    branch, d_norm_attn = attention_tail_part(
+        block_of, per_call, orders, core_bit, token[:1], me, attn_left, attn_right,
+        [[c[0] for c in attn_calls], [c[1] for c in attn_calls]], [shaped((length, width), F32)] * 2,
         [pltpu.VMEM((width, block_cols), BF16), pltpu.VMEM((width, cut), BF16)], 9,
     )
     token = phase([attn_sum] + mlp_sums, [], [branch])
-    block_out, in_grad, stats = tail_part(
-        mlp_tail_kernel, block_of, per_call, orders, core_bit, token[:1], me, up, down,
-        [[c[1] for c in mlp_calls], [c[0] for c in mlp_calls]],
-        [
-            branch, d_norm_attn, tokens_in, out_cotangent, attn_gain[None, :], mlp_gain[None, :], out_bias[None, :],
-            down_bias[None, :],
-        ],
-        [shaped((length, width), BF16)] * 2 + [shaped((8, width), F32)],
-        [pltpu.VMEM((length, width), F32)] * 2 + [pltpu.VMEM((width, up_cols), BF16)] * 2, 13,
-    )
-    stats = phase([attn_sum] + mlp_sums, [stats])[0]
-    while any(r.done < len(orders[0]) for r in mlp_sums):
-        for r in mlp_sums:
-            if r.done < len(orders[0]):
-                r.advance()
-
-    def settle(parts):
-        total = None
-        for k, part in parts:
-            term = (part if k == 0 else shifted(part, -k)).astype(F32)
+    for n, k0 in enumerate(starts):
+        last = n == len(starts) - 1
+        extra = [branch]
+        outs = [shaped((length, width), F32)] * 2
+        scratch = [pltpu.VMEM((width, up_cols), BF16)] * 2
+        if n > 0:
+            extra.append(d_norm_mlp)
+        if last:
+            extra += [
+                d_norm_attn, tokens_in, out_cotangent, attn_gain[None, :], mlp_gain[None, :], out_bias[None, :],
+                down_bias[None, :],
+            ]
+            scratch = [pltpu.VMEM((length, width), F32)] * 2 + scratch
+            outs = [shaped((length, width), BF16)] * 2 + [shaped((8, width), F32)]
+        result = mlp_tail_part(
+            k0, last, orders, core_bit, token[:1], me, up, down, mlp_calls[n][1], mlp_calls[n][0], extra, outs, scratch, 9
+        )
+        if last:
+            block_out, in_grad, stats = result
+            stats = phase([attn_sum] + mlp_sums, [stats])[0]
+        else:
+            branch, d_norm_mlp = result
+            token = phase([attn_sum] + mlp_sums, [], [branch])
+
+    attn_total = attn_sum.total()
+    total = None
+    for k0, one in zip(starts, [r.total() for r in mlp_sums]):
+        for i in range(per_call):
+            part = jnp.concatenate([attn_total[k0 + i], one[i]], axis=1)
+            term = (part if k0 + i == 0 else shifted(part, -(k0 + i))).astype(F32)
             total = term if total is None else total + term
-        flip = 2
-        while flip < lax.axis_size("dp"):
-            total = total + flipped(total, "dp", flip)
-            flip *= 2
-        mine = total.astype(BF16)
-        other = swap(mine, 1)
-        first = half == 0
-        return jnp.concatenate([jnp.where(first, mine, other), jnp.where(first, other, mine)], axis=0).astype(F32)
-
-    attn_sum = attn_sum.total()
-    g_heads = settle([(k, attn_sum[k]) for k in range(col_size)]).reshape(rows, local_heads, HEAD)
-    mlp_totals = [r.total() for r in mlp_sums]
-    g_mlp = settle([(k0 + i, one[i]) for k0, one in zip(starts, mlp_totals) for i in range(per_call)])
+    flip = 2
+    while flip < lax.axis_size("dp"):
+        total = total + flipped(total, "dp", flip)
+        flip *= 2
+    mine = total.astype(BF16)
+    other = swap(mine, 1)
+    first = half == 0
+    grads = jnp.concatenate([jnp.where(first, mine, other), jnp.where(first, other, mine)], axis=0).astype(F32)
+    g_heads = grads[:, :block_cols].reshape(rows, local_heads, HEAD)
+    g_mlp = grads[:, block_cols:]
 
     d_bias_up = jnp.take(jnp.concatenate([c[2] for c in mlp_calls[::-1]]), blocks_here, axis=0)
     d_bias_attn = jnp.take(jnp.concatenate([c[2] for c in attn_calls[::-1]]), blocks_here, axis=0)

time: 365 us -> 302 us (0.83); the launches traced: 359 us -> 301 us
  local copies, waits for them, and re-layouts: 114 us -> 33.4 us
  Pallas kernels: 81.9 us -> 106 us
  waiting for transfers between devices: 66.7 us -> 76.8 us
  starting transfers between devices: 53.3 us -> 44.4 us
    unnamed x328 -> x94, local copies, waits for them, and re-layouts: 101 us -> 14.4 us
    ppermute x38 -> x37, waiting for transfers between devices: 33.9 us -> 57.1 us  [flipped(): lax.ppermute(value, axis, [(i, i ^ flip) for i in range(lax.axis_size(axi...]
    ppermute x12 -> x9, waiting for transfers between devices: 32.8 us -> 19.7 us  [shifted(): lax.ppermute(value, 'col', [(i, (i + by) % size) for i in range(size)])]
    pallas_call x4, Pallas kernels: 56.6 us -> 69.2 us  [block_part(): pl.pallas_call(functools.partial(kernel, orders, core_bit, len(after)), g...]
    pallas_call x2 -> x3, Pallas kernels: 22.6 us -> 30.5 us  [the longest x2 19.3 us: mlp_tail_part(): pl.pallas_call(functools.partial(mlp_tail_kernel, orders, core_bit, last,...]
    ppermute x12 -> x9, starting transfers between devices: 21.3 us -> 15.2 us  [shifted(): lax.ppermute(value, 'col', [(i, (i + by) % size) for i in range(size)])]
    ppermute x38 -> x37, starting transfers between devices: 32 us -> 29.3 us  [flipped(): lax.ppermute(value, axis, [(i, i ^ flip) for i in range(lax.axis_size(axi...]
    convert_element_type x13 -> x12, other arithmetic: 25.2 us -> 26.2 us  [add(): return (a.astype(F32) + b.astype(F32)).astype(BF16)]
  transfers between devices with their start and end apart: 50 -> 46, of which waited for: 12 -> 17; matrix products, arithmetic and copies ran while one was open for 13% -> 15% of each run, Pallas kernels for 23% -> 35%
where the time goes in v5:
time: 302 us; the launch traced here: 301 us
  Pallas kernels  106 us (35%)
  waiting for transfers between devices  76.8 us (25%)
  starting transfers between devices  44.4 us (15%)
  other arithmetic  39.6 us (13%)
  local copies, waits for them, and re-layouts  33.4 us (11%)
    pallas_call x4, Pallas kernels, block_part(): pl.pallas_call(functools.partial(kernel, orders, core_bit, len(after)), g...  69.2 us
    ppermute x37, waiting for transfers between devices, flipped(): lax.ppermute(value, axis, [(i, i ^ flip) for i in range(lax.axis_size(axi...  57.1 us
    ppermute x37, starting transfers between devices, flipped(): lax.ppermute(value, axis, [(i, i ^ flip) for i in range(lax.axis_size(axi...  29.3 us
    convert_element_type x12, other arithmetic, add(): return (a.astype(F32) + b.astype(F32)).astype(BF16)  26.2 us
    ppermute x9, waiting for transfers between devices, shifted(): lax.ppermute(value, 'col', [(i, (i + by) % size) for i in range(size)])  19.7 us
    pallas_call x2, Pallas kernels, mlp_tail_part(): pl.pallas_call(functools.partial(mlp_tail_kernel, orders, core_bit, last,...  19.3 us
    ppermute x9, starting transfers between devices, shifted(): lax.ppermute(value, 'col', [(i, (i + by) % size) for i in range(size)])  15.2 us
    unnamed x94, local copies, waits for them, and re-layouts  14.4 us
  transfers between devices with their start and end apart: 46, of which 17 were waited for; matrix products, arithmetic and copies ran while one was open for 15% of the time, Pallas kernels for 35%

profile of v5, /device:TPU:0, one launch (start us, length us, event | category | flops | bytes accessed | tf_op | source)
XLA Modules:
  0.0 301.4 jit_solution(3185309342503907065)
XLA Ops:
  3.1 5.1 %collective-permute-start.2 = (bf16[96,768]{1,0:T(8,128)(2,1)S(1)}, bf16[96,768]{1,0:T(8,128)(2,1)S(1)}, u32[]{:S(2)}, u32[]{:S(2)}) collective-permute-start(bf16[96,768]{1,0:T(8,128)(2,1)S(1)} %copy.79), channel_id=1, source_target_pairs={{0,3},{1,0},{2,1},{3,2},{4,7},{5,4},{6,5},{7,6},{8,11},{9,8},{10,9... | collective-permute-start | bytes 442376 | tf_op jit(solution)/shard_map/ppermute | solution.py:438
  15.0 6.1 %shard_map.255 = (bf16[512,768]{1,0:T(8,128)(2,1)}, bf16[768,512]{1,0:T(8,128)(2,1)}, bf16[512,768]{1,0:T(8,128)(2,1)}, bf16[768,512]{1,0:T(8,128)(2,1)}, bf16[7...) custom-call(bf16[512,768]{1,0:T(8,128)(2,1)} %rest_13_.1, ...), custom_call_target="tpu_custom_call" | custom-call | flops 6899999744 | bytes 1048576 | tf_op jit(solution)/shard_map/pallas_call | solution.py:121
  21.4 1.6 collective-permute-start.3
  22.9 1.5 collective-permute-start.4
  25.2 2.5 collective-permute-start.7
  32.4 1.6 collective-permute-start.5
  34.6 2.6 collective-permute-done.7.__2_
  37.2 9.9 %collective-permute-done.8.__3_ = bf16[96,1536]{1,0:T(8,128)(2,1)S(1)} collective-permute-done((bf16[96,1536]{1,0:T(8,128)(2,1)}, bf16[96,1536]{1,0:T(8,128)(2,1)S(1)}, u32[]{:S(2)}, u32[]{:S(2)}) %collective-permute-start.8) | collective-permute-done | bytes 294944 | tf_op jit(solution)/shard_map/ppermute | solution.py:438
  47.2 1.7 collective-permute-start.9
  48.9 7.2 %collective-permute-done.9.__4_ = bf16[96,1536]{1,0:T(8,128)(2,1)S(1)} collective-permute-done((bf16[96,1536]{1,0:T(8,128)(2,1)S(1)}, bf16[96,1536]{1,0:T(8,128)(2,1)S(1)}, u32[]{:S(2)}, u32[]{:S(2)}) %collective-permute-start.9) | collective-permute-done | bytes 294944 | tf_op jit(solution)/shard_map/ppermute | solution.py:438
  62.0 10.9 %collective-permute-done.12.__0_ = bf16[1,4,96,768]{3,2,1,0:T(8,128)(2,1)S(1)} collective-permute-done((bf16[1,4,96,768]{3,2,1,0:T(8,128)(2,1)S(1)}, bf16[1,4,96,768]{3,2,1,0:T(8,128)(2,1)S(1)}, u32[]{:S(2)}, u32[]{:S(2)}) %collective-permute-start.12) | collective-permute-done | bytes 589856 | tf_op jit(solution)/shard_map/ppermute | solution.py:433
  74.2 2.3 pad_maximum_fusion.1.rest_13_.rest_0_
  78.2 1.5 collective-permute-start.17
  79.9 21.2 %shard_map.259 = (bf16[2,512,768]{2,1,0:T(8,128)(2,1)}, bf16[2,512,384]{2,1,0:T(8,128)(2,1)}, f32[2,1,768]{2,1,0:T(1,128)}, bf16[8,4,96,384]{3,2,1,0:T(8,128)(2,1)}, bf16[8,4,96,384]{3,2,1,0:T(8,128)(2,1)}) custom-call(s32[1]{0:T(128)} %bitcast.me_ref, bf16[512,768]{1,0:T(8,128)(2,1)} %get-tuple-element.80.__2_.na_ref, ...), custom_call_target="tpu_custom_call" | custom-call | flops 25300000768 | bytes 1048576 | tf_op jit(solution)/shard_map/pallas_call | solution.py:267
  101.1 1.6 collective-permute-done.16.__0_
  102.7 4.1 %collective-permute-done.17.__1_ = bf16[2,4,96,768]{3,2,1,0:T(8,128)(2,1)} collective-permute-done((bf16[2,4,96,768]{3,2,1,0:T(8,128)(2,1)}, bf16[2,4,96,768]{3,2,1,0:T(8,128)(2,1)}, u32[]{:S(2)}, u32[]{:S(2)}) %collective-permute-start.17) | collective-permute-done | bytes 1179680 | tf_op jit(solution)/shard_map/ppermute | solution.py:433
  108.9 21.0 %shard_map.261 = (bf16[2,512,768]{2,1,0:T(8,128)(2,1)}, bf16[2,512,384]{2,1,0:T(8,128)(2,1)}, f32[2,1,768]{2,1,0:T(1,128)}, bf16[8,4,96,384]{3,2,1,0:T(8,128)(2,1)}, bf16[8,4,96,384]{3,2,1,0:T(8,128)(2,1)}) custom-call(s32[1]{0:T(128)} %bitcast.me_ref, ...), custom_call_target="tpu_custom_call", output_to_operand_aliasing={{3}: (19, {}), {4}: (20, {})} | custom-call | flops 25300000768 | bytes 1048576 | tf_op jit(solution)/shard_map/pallas_call | solution.py:267
  131.4 13.6 %shard_map.263 = (bf16[2,512,768]{2,1,0:T(8,128)(2,1)}, bf16[2,512,768]{2,1,0:T(8,128)(2,1)}, f32[2,1,768]{2,1,0:T(1,128)}, bf16[8,2,96,768]{3,2,1,0:T(8,128)(2,1)}, bf16[8,2,96,768]{3,2,1,0:T(8,128)(2,1)}) custom-call(s32[1]{0:T(128)} %bitcast.me_ref, bf16[512,768]{1,0:T(8,128)(2,1)} %get-tuple-element.99.nm_ref, ...), custom_call_target="tpu_custom_call" | custom-call | flops 13799999488 | bytes 1048576 | tf_op jit(solution)/shard_map/pallas_call | solution.py:267
  145.0 1.5 copy-done.3
  147.0 4.0 %add_convert_fusion.8 = (bf16[2,4,96,384]{3,2,1,0:T(8,128)(2,1)S(1)}, bf16[2,4,96,384]{3,2,1,0:T(8,128)(2,1)S(1)}, bf16[2,4,96,384]{3,2,1,0:T(8,128)(2,1)}, bf16[2,4,96,384]{3,2,1,0:T(8,128)(2,1)}) fusion(bf16[8,4,96,384]{3,2,1,0:T(8,128)(2,1)} %get-tuple-element.106.rest_9_, bf16[8,4,96,384]{3,2,1,0:T(8,128)(2,1)} %get-tuple-element.115), kind=kLoop, calls=%fused_computation.15 | loop fusion | flops 4718592 | bytes 7077888 | tf_op jit(solution)/shard_map/convert_element_type | solution.py:450
  151.0 1.5 collective-permute-start.23
  152.5 1.5 collective-permute-start.24
  154.0 13.3 %shard_map.265 = (bf16[2,512,768]{2,1,0:T(8,128)(2,1)}, bf16[2,512,768]{2,1,0:T(8,128)(2,1)}, f32[2,1,768]{2,1,0:T(1,128)}, bf16[8,2,96,768]{3,2,1,0:T(8,128)(2,1)}, bf16[8,2,96,768]{3,2,1,0:T(8,128)(2,1)}) custom-call(s32[1]{0:T(128)} %bitcast.me_ref, bf16[512,768]{1,0:T(8,128)(2,1)} %get-tuple-element.99.nm_ref, ...), custom_call_target="tpu_custom_call" | custom-call | flops 13799999488 | bytes 1048576 | tf_op jit(solution)/shard_map/pallas_call | solution.py:267
  167.8 1.4 copy-done.2
  179.7 1.7 add_convert_fusion.30
  181.4 1.5 collective-permute-start.26
  182.9 1.7 add_convert_fusion.29
  185.2 4.1 %add_convert_fusion.4 = (bf16[2,2,96,768]{3,2,1,0:T(8,128)(2,1)}, bf16[2,2,96,768]{3,2,1,0:T(8,128)(2,1)}, bf16[2,2,96,768]{3,2,1,0:T(8,128)(2,1)}, bf16[2,2,96,768]{3,2,1,0:T(8,128)(2,1)}) fusion(bf16[8,2,96,768]{3,2,1,0:T(8,128)(2,1)} %get-tuple-element.123, bf16[8,2,96,768]{3,2,1,0:T(8,128)(2,1)} %get-tuple-element.122), kind=kLoop, calls=%fused_computation.11 | loop fusion | flops 4718592 | bytes 7077888 | tf_op jit(solution)/shard_map/convert_element_type | solution.py:450
  189.3 1.5 collective-permute-start.28
  191.3 11.2 %shard_map.267 = (f32[512,768]{1,0:T(8,128)}, f32[512,768]{1,0:T(8,128)}) custom-call(s32[1]{0:T(128)} %bitcast.me_ref, bf16[2,4,96,384]{3,2,1,0:T(8,128)(2,1)} %copy-done.16, bf16[2,4,96,384]{3,2,1,0:T(8,128)(2,1)} %get-tuple-element.86.rest_1_, bf16[2,4,96,384]{3,2,1,0:T(8,128)(2,1)} %copy-done.41, bf16[2,4,96,384]{3,2,1,0:T(8,128)(2,1)} %copy-done.42, ...), custom_call_target="tpu_custom_call" | custom-call | flops 10350000128 | bytes 1048576 | tf_op jit(solution)/shard_map/pallas_call | solution.py:382
  202.6 3.5 %collective-permute-done.28.__2_ = bf16[2,2,96,768]{3,2,1,0:T(8,128)(2,1)} collective-permute-done((bf16[2,2,96,768]{3,2,1,0:T(8,128)(2,1)}, bf16[2,2,96,768]{3,2,1,0:T(8,128)(2,1)}, u32[]{:S(2)}, u32[]{:S(2)}) %collective-permute-start.28) | collective-permute-done | bytes 589856 | tf_op jit(solution)/shard_map/ppermute | solution.py:433
  207.5 1.8 add_convert_fusion.28
  209.9 1.8 add_convert_fusion.27
  212.3 3.8 %add_convert_fusion = (bf16[2,2,96,768]{3,2,1,0:T(8,128)(2,1)S(1)}, bf16[2,2,96,768]{3,2,1,0:T(8,128)(2,1)S(1)}, bf16[2,2,96,768]{3,2,1,0:T(8,128)(2,1)S(1)}, bf16[2,2,96,768]{3,2,1,0:T(8,128)(2,1)}) fusion(bf16[8,2,96,768]{3,2,1,0:T(8,128)(2,1)} %get-tuple-element.132, bf16[8,2,96,768]{3,2,1,0:T(8,128)(2,1)} %get-tuple-element.131), kind=kLoop, calls=%fused_computation.7 | loop fusion | flops 4718592 | bytes 7077888 | tf_op jit(solution)/shard_map/convert_element_type | solution.py:450
  216.1 1.5 collective-permute-start.33
  217.5 1.5 collective-permute-start.34
  219.0 8.3 %shard_map.269 = (f32[512,768]{1,0:T(8,128)}, f32[512,768]{1,0:T(8,128)}) custom-call(s32[1]{0:T(128)} %bitcast.me_ref, bf16[2,4,96,768]{3,2,1,0:T(8,128)(2,1)} %pad_maximum_fusion.1.rest_13_.rest_0_, bf16[2,4,96,768]{3,2,1,0:T(8,128)(2,1)} %get-tuple-element.97.rest_13_.rest_1_, bf16[2,4,96,768]{3,2,1,0:T(8,128)(2,1)} %copy-done.11, ...), custom_call_target="tpu_custom_call" | custom-call | flops 10350000128 | bytes 1048576 | tf_op jit(solution)/shard_map/pallas_call | solution.py:398
  228.8 3.2 %collective-permute-done.33.__2_ = bf16[2,2,96,768]{3,2,1,0:T(8,128)(2,1)} collective-permute-done((bf16[2,2,96,768]{3,2,1,0:T(8,128)(2,1)}, bf16[2,2,96,768]{3,2,1,0:T(8,128)(2,1)}, u32[]{:S(2)}, u32[]{:S(2)}) %collective-permute-start.33) | collective-permute-done | bytes 589856 | tf_op jit(solution)/shard_map/ppermute | solution.py:433
  233.1 1.6 collective-permute-start.35
  234.7 1.7 add_convert_fusion.25
  240.4 11.0 %shard_map.271 = (bf16[512,768]{1,0:T(8,128)(2,1)}, bf16[512,768]{1,0:T(8,128)(2,1)}, f32[8,768]{1,0:T(8,128)}) custom-call(s32[1]{0:T(128)} %bitcast.me_ref, bf16[2,4,96,768]{3,2,1,0:T(8,128)(2,1)} %pad_maximum_fusion.1.rest_13_.rest_0_, bf16[2,4,96,768]{3,2,1,0:T(8,128)(2,1)} %get-tuple-element.97.rest_13_.rest_1_, bf16[2,4,96,768]{3,2,1,0:T(8,128)(2,1)} %copy-done.11, ...), custom_call_target="tpu_custom_call" | custom-call | flops 10350000128 | bytes 1048576 | tf_op jit(solution)/shard_map/pallas_call | solution.py:398
  253.1 1.4 fusion.4
  255.6 2.7 collective-permute-start.44
  259.2 3.5 %collective-permute-done.39 = f32[72,128]{1,0:T(8,128)S(1)} collective-permute-done((f32[72,128]{1,0:T(8,128)S(1)}, f32[72,128]{1,0:T(8,128)S(1)}, u32[]{:S(2)}, u32[]{:S(2)}) %collective-permute-start.39) | collective-permute-done | bytes 36896 | tf_op jit(solution)/shard_map/ppermute | solution.py:433
  262.7 3.2 %collective-permute-start.40 = (f32[72,128]{1,0:T(8,128)S(1)}, f32[72,128]{1,0:T(8,128)S(1)}, u32[]{:S(2)}, u32[]{:S(2)}) collective-permute-start(f32[72,128]{1,0:T(8,128)S(1)} %add.202), channel_id=1, source_target_pairs={{0,1},{1,0},{2,3},{3,2},{4,5},{5,4},{6,7},{7,6},{8,9},{9,8},{10,11... | collective-permute-start | bytes 110600 | tf_op jit(solution)/shard_map/ppermute | solution.py:433
  265.8 12.9 %collective-permute-done.40 = f32[72,128]{1,0:T(8,128)S(1)} collective-permute-done((f32[72,128]{1,0:T(8,128)S(1)}, f32[72,128]{1,0:T(8,128)S(1)}, u32[]{:S(2)}, u32[]{:S(2)}) %collective-permute-start.40) | collective-permute-done | bytes 36896 | tf_op jit(solution)/shard_map/ppermute | solution.py:433
  278.8 4.8 %collective-permute-done.41 = f32[72,128]{1,0:T(8,128)S(1)} collective-permute-done((f32[72,128]{1,0:T(8,128)S(1)}, f32[72,128]{1,0:T(8,128)S(1)}, u32[]{:S(2)}, u32[]{:S(2)}) %collective-permute-start.41) | collective-permute-done | bytes 36896 | tf_op jit(solution)/shard_map/ppermute | solution.py:433
  287.3 9.5 %collective-permute-done.45 = bf16[96,2304]{1,0:T(8,128)(2,1)S(1)} collective-permute-done((bf16[96,2304]{1,0:T(8,128)(2,1)S(1)}, bf16[96,2304]{1,0:T(8,128)(2,1)S(1)}, u32[]{:S(2)}, u32[]{:S(2)}) %collective-permute-start.45) | collective-permute-done | bytes 442400 | tf_op jit(solution)/shard_map/ppermute | solution.py:433
  (232 shorter events, 61.3 us)
Async XLA Ops:
  3.1 18.0 %collective-permute-start.2 = (bf16[96,768]{1,0:T(8,128)(2,1)S(1)}, bf16[96,768]{1,0:T(8,128)(2,1)S(1)}, u32[]{:S(2)}, u32[]{:S(2)}) collective-permute-start(bf16[96,768]{1,0:T(8,128)(2,1)S(1)} %copy.79), channel_id=1, source_target_pairs={{0,3},{1,0},{2,1},{3,2},{4,7},{5,4},{6,5},{7,6},{8,11},{9,8},{10,9... | collective-permute-start | bytes 442376 | tf_op jit(solution)/shard_map/ppermute | solution.py:438
  8.2 12.9 %collective-permute-start.1 = (bf16[96,768]{1,0:T(8,128)(2,1)S(1)}, bf16[96,768]{1,0:T(8,128)(2,1)S(1)}, u32[]{:S(2)}, u32[]{:S(2)}) collective-permute-start(bf16[96,768]{1,0:T(8,128)(2,1)S(1)} %copy.79), channel_id=1, source_target_pairs={{0,2},{1,3},{2,0},{3,1},{4,6},{5,7},{6,4},{7,5},{8,10},{9,11},{10,... | collective-permute-start | bytes 442376 | tf_op jit(solution)/shard_map/ppermute | solution.py:438
  8.2 12.9 %collective-permute-start = (bf16[96,768]{1,0:T(8,128)(2,1)S(1)}, bf16[96,768]{1,0:T(8,128)(2,1)S(1)}, u32[]{:S(2)}, u32[]{:S(2)}) collective-permute-start(bf16[96,768]{1,0:T(8,128)(2,1)S(1)} %copy.79), channel_id=1, source_target_pairs={{0,1},{1,2},{2,3},{3,0},{4,5},{5,6},{6,7},{7,4},{8,9},{9,10},{10,1... | collective-permute-start | bytes 442376 | tf_op jit(solution)/shard_map/ppermute | solution.py:438
  21.4 8.0 %collective-permute-start.3 = (bf16[1,4,96,384]{3,2,1,0:T(8,128)(2,1)S(1)}, bf16[1,4,96,384]{3,2,1,0:T(8,128)(2,1)S(1)}, u32[]{:S(2)}, u32[]{:S(2)}) collective-permute-start(bf16[1,4,96,384]{3,2,1,0:T(8,128)(2,1)S(1)} %get-tuple-element.201), channel_id=1, source_target_pairs={{0,8},{4,12},{8,0},{12,4},{1,9},{5,13},{9,1},{13,5},{2,10},{6,14},... | collective-permute-start | bytes 884744 | tf_op jit(solution)/shard_map/ppermute | solution.py:433
  22.9 7.6 %collective-permute-start.4 = (bf16[1,4,96,384]{3,2,1,0:T(8,128)(2,1)S(1)}, bf16[1,4,96,384]{3,2,1,0:T(8,128)(2,1)S(1)}, u32[]{:S(2)}, u32[]{:S(2)}) collective-permute-start(bf16[1,4,96,384]{3,2,1,0:T(8,128)(2,1)S(1)} %get-tuple-element.200), channel_id=1, source_target_pairs={{0,16},{16,0},{1,17},{17,1},{2,18},{18,2},{3,19},{19,3},{4,20},{20... | collective-permute-start | bytes 884744 | tf_op jit(solution)/shard_map/ppermute | solution.py:433
  25.2 12.1 %collective-permute-start.7 = (bf16[96,1536]{1,0:T(8,128)(2,1)}, bf16[96,1536]{1,0:T(8,128)(2,1)S(1)}, u32[]{:S(2)}, u32[]{:S(2)}) collective-permute-start(bf16[96,1536]{1,0:T(8,128)(2,1)} %shard_map.254), channel_id=1, source_target_pairs={{0,1},{1,2},{2,3},{3,0},{4,5},{5,6},{6,7},{7,4},{8,9},{9,10},{10,1... | collective-permute-start | bytes 884744 | tf_op jit(solution)/shard_map/ppermute | solution.py:438
  27.6 19.5 %collective-permute-start.8 = (bf16[96,1536]{1,0:T(8,128)(2,1)}, bf16[96,1536]{1,0:T(8,128)(2,1)S(1)}, u32[]{:S(2)}, u32[]{:S(2)}) collective-permute-start(bf16[96,1536]{1,0:T(8,128)(2,1)} %shard_map.254), channel_id=1, source_target_pairs={{0,2},{1,3},{2,0},{3,1},{4,6},{5,7},{6,4},{7,5},{8,10},{9,11},{10,... | collective-permute-start | bytes 884744 | tf_op jit(solution)/shard_map/ppermute | solution.py:438
  32.4 24.7 %copy-start.16 = (bf16[2,4,96,384]{3,2,1,0:T(8,128)(2,1)}, bf16[2,4,96,384]{3,2,1,0:T(8,128)(2,1)S(1)}, u32[]{:S(2)}) copy-start(bf16[2,4,96,384]{3,2,1,0:T(8,128)(2,1)S(1)} %pad_maximum_fusion.4.rest_0_) | copy-start | bytes 1769476
  32.4 23.7 %collective-permute-start.5 = (bf16[2,4,96,384]{3,2,1,0:T(8,128)(2,1)S(1)}, bf16[2,4,96,384]{3,2,1,0:T(8,128)(2,1)}, u32[]{:S(2)}, u32[]{:S(2)}) collective-permute-start(bf16[2,4,96,384]{3,2,1,0:T(8,128)(2,1)S(1)} %pad_maximum_fusion.4.rest_0_), channel_id=1, source_target_pairs={{0,16},{16,0},{1,17},{17,1},{2,18},{18,2},{3,19},{19,3},{4,20},{20... | collective-permute-start | bytes 1769480 | tf_op jit(solution)/shard_map/ppermute | solution.py:433
  34.0 22.2 %collective-permute-start.10 = (bf16[2,4,96,384]{3,2,1,0:T(8,128)(2,1)S(1)}, bf16[2,4,96,384]{3,2,1,0:T(8,128)(2,1)S(1)}, u32[]{:S(2)}, u32[]{:S(2)}) collective-permute-start(bf16[2,4,96,384]{3,2,1,0:T(8,128)(2,1)S(1)} %pad_maximum_fusion.4.rest_0_), channel_id=1, source_target_pairs={{0,4},{4,0},{8,12},{12,8},{1,5},{5,1},{9,13},{13,9},{2,6},{6,2},{1... | collective-permute-start | bytes 1769480 | tf_op jit(solution)/shard_map/ppermute | solution.py:433
  34.0 23.0 %copy-start.17 = (bf16[2,4,96,384]{3,2,1,0:T(8,128)(2,1)}, bf16[2,4,96,384]{3,2,1,0:T(8,128)(2,1)S(1)}, u32[]{:S(2)}) copy-start(bf16[2,4,96,384]{3,2,1,0:T(8,128)(2,1)S(1)} %pad_maximum_fusion.5.rest_4_) | copy-start | bytes 1769476
  34.0 22.1 %collective-permute-start.6 = (bf16[2,4,96,384]{3,2,1,0:T(8,128)(2,1)S(1)}, bf16[2,4,96,384]{3,2,1,0:T(8,128)(2,1)}, u32[]{:S(2)}, u32[]{:S(2)}) collective-permute-start(bf16[2,4,96,384]{3,2,1,0:T(8,128)(2,1)S(1)} %pad_maximum_fusion.5.rest_4_), channel_id=1, source_target_pairs={{0,8},{4,12},{8,0},{12,4},{1,9},{5,13},{9,1},{13,5},{2,10},{6,14},... | collective-permute-start | bytes 1769480 | tf_op jit(solution)/shard_map/ppermute | solution.py:433
  37.2 18.9 %collective-permute-start.11 = (bf16[2,4,96,384]{3,2,1,0:T(8,128)(2,1)S(1)}, bf16[2,4,96,384]{3,2,1,0:T(8,128)(2,1)}, u32[]{:S(2)}, u32[]{:S(2)}) collective-permute-start(bf16[2,4,96,384]{3,2,1,0:T(8,128)(2,1)S(1)} %pad_maximum_fusion.5.rest_4_), channel_id=1, source_target_pairs={{0,4},{4,0},{8,12},{12,8},{1,5},{5,1},{9,13},{13,9},{2,6},{6,2},{1... | collective-permute-start | bytes 1769480 | tf_op jit(solution)/shard_map/ppermute | solution.py:433
  47.2 8.9 %collective-permute-start.9 = (bf16[96,1536]{1,0:T(8,128)(2,1)S(1)}, bf16[96,1536]{1,0:T(8,128)(2,1)S(1)}, u32[]{:S(2)}, u32[]{:S(2)}) collective-permute-start(bf16[96,1536]{1,0:T(8,128)(2,1)S(1)} %copy-done.10), channel_id=1, source_target_pairs={{0,3},{1,0},{2,1},{3,2},{4,7},{5,4},{6,5},{7,6},{8,11},{9,8},{10,9... | collective-permute-start | bytes 884744 | tf_op jit(solution)/shard_map/ppermute | solution.py:438
  58.4 14.5 %collective-permute-start.12 = (bf16[1,4,96,768]{3,2,1,0:T(8,128)(2,1)S(1)}, bf16[1,4,96,768]{3,2,1,0:T(8,128)(2,1)S(1)}, u32[]{:S(2)}, u32[]{:S(2)}) collective-permute-start(bf16[1,4,96,768]{3,2,1,0:T(8,128)(2,1)S(1)} %get-tuple-element.189), channel_id=1, source_target_pairs={{0,8},{4,12},{8,0},{12,4},{1,9},{5,13},{9,1},{13,5},{2,10},{6,14},... | collective-permute-start | bytes 1769480 | tf_op jit(solution)/shard_map/ppermute | solution.py:433
  59.0 14.1 %collective-permute-start.13 = (bf16[1,4,96,768]{3,2,1,0:T(8,128)(2,1)S(1)}, bf16[1,4,96,768]{3,2,1,0:T(8,128)(2,1)S(1)}, u32[]{:S(2)}, u32[]{:S(2)}) collective-permute-start(bf16[1,4,96,768]{3,2,1,0:T(8,128)(2,1)S(1)} %get-tuple-element.188), channel_id=1, source_target_pairs={{0,16},{16,0},{1,17},{17,1},{2,18},{18,2},{3,19},{19,3},{4,20},{20... | collective-permute-start | bytes 1769480 | tf_op jit(solution)/shard_map/ppermute | solution.py:433
  59.5 13.6 %collective-permute-start.14 = (bf16[2,4,96,384]{3,2,1,0:T(8,128)(2,1)}, bf16[2,4,96,384]{3,2,1,0:T(8,128)(2,1)S(1)}, u32[]{:S(2)}, u32[]{:S(2)}) collective-permute-start(bf16[2,4,96,384]{3,2,1,0:T(8,128)(2,1)} %get-tuple-element.86.rest_1_), channel_id=1, source_target_pairs={{0,4},{4,0},{8,12},{12,8},{1,5},{5,1},{9,13},{13,9},{2,6},{6,2},{1... | collective-permute-start | bytes 1769480 | tf_op jit(solution)/shard_map/ppermute | solution.py:433
  59.5 13.6 %collective-permute-start.15 = (bf16[2,4,96,384]{3,2,1,0:T(8,128)(2,1)}, bf16[2,4,96,384]{3,2,1,0:T(8,128)(2,1)}, u32[]{:S(2)}, u32[]{:S(2)}) collective-permute-start(bf16[2,4,96,384]{3,2,1,0:T(8,128)(2,1)} %get-tuple-element.87.rest_5_), channel_id=1, source_target_pairs={{0,4},{4,0},{8,12},{12,8},{1,5},{5,1},{9,13},{13,9},{2,6},{6,2},{1... | collective-permute-start | bytes 1769480 | tf_op jit(solution)/shard_map/ppermute | solution.py:433
  76.4 26.3 %collective-permute-start.16 = (bf16[2,4,96,768]{3,2,1,0:T(8,128)(2,1)}, bf16[2,4,96,768]{3,2,1,0:T(8,128)(2,1)S(1)}, u32[]{:S(2)}, u32[]{:S(2)}) collective-permute-start(bf16[2,4,96,768]{3,2,1,0:T(8,128)(2,1)} %pad_maximum_fusion.1.rest_13_.rest_0_), channel_id=1, source_target_pairs={{0,16},{16,0},{1,17},{17,1},{2,18},{18,2},{3,19},{19,3},{4,20},{20... | collective-permute-start | bytes 3538952 | tf_op jit(solution)/shard_map/ppermute | solution.py:433
  76.9 29.9 %collective-permute-start.18 = (bf16[2,4,96,768]{3,2,1,0:T(8,128)(2,1)}, bf16[2,4,96,768]{3,2,1,0:T(8,128)(2,1)S(1)}, u32[]{:S(2)}, u32[]{:S(2)}) collective-permute-start(bf16[2,4,96,768]{3,2,1,0:T(8,128)(2,1)} %pad_maximum_fusion.1.rest_13_.rest_0_), channel_id=1, source_target_pairs={{0,4},{4,0},{8,12},{12,8},{1,5},{5,1},{9,13},{13,9},{2,6},{6,2},{1... | collective-permute-start | bytes 3538952 | tf_op jit(solution)/shard_map/ppermute | solution.py:433
  78.2 28.7 %collective-permute-start.17 = (bf16[2,4,96,768]{3,2,1,0:T(8,128)(2,1)}, bf16[2,4,96,768]{3,2,1,0:T(8,128)(2,1)}, u32[]{:S(2)}, u32[]{:S(2)}) collective-permute-start(bf16[2,4,96,768]{3,2,1,0:T(8,128)(2,1)} %pad_maximum_fusion.2.rest_4_), channel_id=1, source_target_pairs={{0,8},{4,12},{8,0},{12,4},{1,9},{5,13},{9,1},{13,5},{2,10},{6,14},... | collective-permute-start | bytes 3538952 | tf_op jit(solution)/shard_map/ppermute | solution.py:433
  79.6 27.2 %collective-permute-start.19 = (bf16[2,4,96,768]{3,2,1,0:T(8,128)(2,1)}, bf16[2,4,96,768]{3,2,1,0:T(8,128)(2,1)S(1)}, u32[]{:S(2)}, u32[]{:S(2)}) collective-permute-start(bf16[2,4,96,768]{3,2,1,0:T(8,128)(2,1)} %pad_maximum_fusion.2.rest_4_), channel_id=1, source_target_pairs={{0,4},{4,0},{8,12},{12,8},{1,5},{5,1},{9,13},{13,9},{2,6},{6,2},{1... | collective-permute-start | bytes 3538952 | tf_op jit(solution)/shard_map/ppermute | solution.py:433
  108.4 21.6 %collective-permute-start.20 = (bf16[2,4,96,768]{3,2,1,0:T(8,128)(2,1)}, bf16[2,4,96,768]{3,2,1,0:T(8,128)(2,1)S(1)}, u32[]{:S(2)}, u32[]{:S(2)}) collective-permute-start(bf16[2,4,96,768]{3,2,1,0:T(8,128)(2,1)} %get-tuple-element.97.rest_13_.rest_1_), channel_id=1, source_target_pairs={{0,4},{4,0},{8,12},{12,8},{1,5},{5,1},{9,13},{13,9},{2,6},{6,2},{1... | collective-permute-start | bytes 3538952 | tf_op jit(solution)/shard_map/ppermute | solution.py:433
  108.4 21.6 %collective-permute-start.21 = (bf16[2,4,96,768]{3,2,1,0:T(8,128)(2,1)}, bf16[2,4,96,768]{3,2,1,0:T(8,128)(2,1)S(1)}, u32[]{:S(2)}, u32[]{:S(2)}) collective-permute-start(bf16[2,4,96,768]{3,2,1,0:T(8,128)(2,1)} %get-tuple-element.98.rest_5_), channel_id=1, source_target_pairs={{0,4},{4,0},{8,12},{12,8},{1,5},{5,1},{9,13},{13,9},{2,6},{6,2},{1... | collective-permute-start | bytes 3538952 | tf_op jit(solution)/shard_map/ppermute | solution.py:433
  131.4 13.6 %collective-permute-start.22 = (bf16[8,4,96,384]{3,2,1,0:T(8,128)(2,1)}, bf16[8,4,96,384]{3,2,1,0:T(8,128)(2,1)S(1)}, u32[]{:S(2)}, u32[]{:S(2)}) collective-permute-start(bf16[8,4,96,384]{3,2,1,0:T(8,128)(2,1)} %shard_map.262.rest_9_), channel_id=1, source_target_pairs={{0,4},{4,0},{8,12},{12,8},{1,5},{5,1},{9,13},{13,9},{2,6},{6,2},{1... | collective-permute-start | bytes 7077896 | tf_op jit(solution)/shard_map/ppermute | solution.py:433
  146.5 21.2 %collective-permute-start.25 = (bf16[8,2,96,768]{3,2,1,0:T(8,128)(2,1)}, bf16[8,2,96,768]{3,2,1,0:T(8,128)(2,1)S(1)}, u32[]{:S(2)}, u32[]{:S(2)}) collective-permute-start(bf16[8,2,96,768]{3,2,1,0:T(8,128)(2,1)} %get-tuple-element.116), channel_id=1, source_target_pairs={{0,4},{4,0},{8,12},{12,8},{1,5},{5,1},{9,13},{13,9},{2,6},{6,2},{1... | collective-permute-start | bytes 7077896 | tf_op jit(solution)/shard_map/ppermute | solution.py:433
  151.0 16.3 %collective-permute-start.23 = (bf16[2,4,96,384]{3,2,1,0:T(8,128)(2,1)}, bf16[2,4,96,384]{3,2,1,0:T(8,128)(2,1)}, u32[]{:S(2)}, u32[]{:S(2)}) collective-permute-start(bf16[2,4,96,384]{3,2,1,0:T(8,128)(2,1)} %get-tuple-element.184), channel_id=1, source_target_pairs={{0,8},{4,12},{8,0},{12,4},{1,9},{5,13},{9,1},{13,5},{2,10},{6,14},... | collective-permute-start | bytes 1769480 | tf_op jit(solution)/shard_map/ppermute | solution.py:433
  152.5 15.3 %collective-permute-start.24 = (bf16[2,4,96,384]{3,2,1,0:T(8,128)(2,1)}, bf16[2,4,96,384]{3,2,1,0:T(8,128)(2,1)}, u32[]{:S(2)}, u32[]{:S(2)}) collective-permute-start(bf16[2,4,96,384]{3,2,1,0:T(8,128)(2,1)} %get-tuple-element.183), channel_id=1, source_target_pairs={{0,16},{16,0},{1,17},{17,1},{2,18},{18,2},{3,19},{19,3},{4,20},{20... | collective-permute-start | bytes 1769480 | tf_op jit(solution)/shard_map/ppermute | solution.py:433
  169.2 36.9 %collective-permute-start.30 = (bf16[8,2,96,768]{3,2,1,0:T(8,128)(2,1)}, bf16[8,2,96,768]{3,2,1,0:T(8,128)(2,1)S(1)}, u32[]{:S(2)}, u32[]{:S(2)}) collective-permute-start(bf16[8,2,96,768]{3,2,1,0:T(8,128)(2,1)} %get-tuple-element.124), channel_id=1, source_target_pairs={{0,4},{4,0},{8,12},{12,8},{1,5},{5,1},{9,13},{13,9},{2,6},{6,2},{1... | collective-permute-start | bytes 7077896 | tf_op jit(solution)/shard_map/ppermute | solution.py:433
  181.4 21.1 %collective-permute-start.26 = (bf16[1,4,96,384]{3,2,1,0:T(8,128)(2,1)}, bf16[1,4,96,384]{3,2,1,0:T(8,128)(2,1)S(1)}, u32[]{:S(2)}, u32[]{:S(2)}) collective-permute-start(bf16[1,4,96,384]{3,2,1,0:T(8,128)(2,1)} %add_convert_fusion.30), channel_id=1, source_target_pairs={{0,16},{16,0},{1,17},{17,1},{2,18},{18,2},{3,19},{19,3},{4,20},{20... | collective-permute-start | bytes 884744 | tf_op jit(solution)/shard_map/ppermute | solution.py:433
  184.7 17.9 %collective-permute-start.27 = (bf16[1,4,96,384]{3,2,1,0:T(8,128)(2,1)}, bf16[1,4,96,384]{3,2,1,0:T(8,128)(2,1)}, u32[]{:S(2)}, u32[]{:S(2)}) collective-permute-start(bf16[1,4,96,384]{3,2,1,0:T(8,128)(2,1)} %add_convert_fusion.29), channel_id=1, source_target_pairs={{0,8},{4,12},{8,0},{12,4},{1,9},{5,13},{9,1},{13,5},{2,10},{6,14},... | collective-permute-start | bytes 884744 | tf_op jit(solution)/shard_map/ppermute | solution.py:433
  189.3 16.8 %collective-permute-start.28 = (bf16[2,2,96,768]{3,2,1,0:T(8,128)(2,1)}, bf16[2,2,96,768]{3,2,1,0:T(8,128)(2,1)}, u32[]{:S(2)}, u32[]{:S(2)}) collective-permute-start(bf16[2,2,96,768]{3,2,1,0:T(8,128)(2,1)} %get-tuple-element.180), channel_id=1, source_target_pairs={{0,8},{4,12},{8,0},{12,4},{1,9},{5,13},{9,1},{13,5},{2,10},{6,14},... | collective-permute-start | bytes 1769480 | tf_op jit(solution)/shard_map/ppermute | solution.py:433
  190.8 15.3 %collective-permute-start.29 = (bf16[2,2,96,768]{3,2,1,0:T(8,128)(2,1)}, bf16[2,2,96,768]{3,2,1,0:T(8,128)(2,1)}, u32[]{:S(2)}, u32[]{:S(2)}) collective-permute-start(bf16[2,2,96,768]{3,2,1,0:T(8,128)(2,1)} %get-tuple-element.179), channel_id=1, source_target_pairs={{0,16},{16,0},{1,17},{17,1},{2,18},{18,2},{3,19},{19,3},{4,20},{20... | collective-permute-start | bytes 1769480 | tf_op jit(solution)/shard_map/ppermute | solution.py:433
  209.4 19.4 %collective-permute-start.31 = (bf16[1,2,96,768]{3,2,1,0:T(8,128)(2,1)}, bf16[1,2,96,768]{3,2,1,0:T(8,128)(2,1)}, u32[]{:S(2)}, u32[]{:S(2)}) collective-permute-start(bf16[1,2,96,768]{3,2,1,0:T(8,128)(2,1)} %add_convert_fusion.28), channel_id=1, source_target_pairs={{0,16},{16,0},{1,17},{17,1},{2,18},{18,2},{3,19},{19,3},{4,20},{20... | collective-permute-start | bytes 884744 | tf_op jit(solution)/shard_map/ppermute | solution.py:433
  211.7 17.0 %collective-permute-start.32 = (bf16[1,2,96,768]{3,2,1,0:T(8,128)(2,1)}, bf16[1,2,96,768]{3,2,1,0:T(8,128)(2,1)}, u32[]{:S(2)}, u32[]{:S(2)}) collective-permute-start(bf16[1,2,96,768]{3,2,1,0:T(8,128)(2,1)} %add_convert_fusion.27), channel_id=1, source_target_pairs={{0,8},{4,12},{8,0},{12,4},{1,9},{5,13},{9,1},{13,5},{2,10},{6,14},... | collective-permute-start | bytes 884744 | tf_op jit(solution)/shard_map/ppermute | solution.py:433
  216.1 15.9 %collective-permute-start.33 = (bf16[2,2,96,768]{3,2,1,0:T(8,128)(2,1)}, bf16[2,2,96,768]{3,2,1,0:T(8,128)(2,1)}, u32[]{:S(2)}, u32[]{:S(2)}) collective-permute-start(bf16[2,2,96,768]{3,2,1,0:T(8,128)(2,1)} %get-tuple-element.176), channel_id=1, source_target_pairs={{0,8},{4,12},{8,0},{12,4},{1,9},{5,13},{9,1},{13,5},{2,10},{6,14},... | collective-permute-start | bytes 1769480 | tf_op jit(solution)/shard_map/ppermute | solution.py:433
  217.5 14.4 %collective-permute-start.34 = (bf16[2,2,96,768]{3,2,1,0:T(8,128)(2,1)S(1)}, bf16[2,2,96,768]{3,2,1,0:T(8,128)(2,1)}, u32[]{:S(2)}, u32[]{:S(2)}) collective-permute-start(bf16[2,2,96,768]{3,2,1,0:T(8,128)(2,1)S(1)} %get-tuple-element.175), channel_id=1, source_target_pairs={{0,16},{16,0},{1,17},{17,1},{2,18},{18,2},{3,19},{19,3},{4,20},{20... | collective-permute-start | bytes 1769480 | tf_op jit(solution)/shard_map/ppermute | solution.py:433
  233.1 18.3 %collective-permute-start.35 = (bf16[1,2,96,768]{3,2,1,0:T(8,128)(2,1)S(1)}, bf16[1,2,96,768]{3,2,1,0:T(8,128)(2,1)S(1)}, u32[]{:S(2)}, u32[]{:S(2)}) collective-permute-start(bf16[1,2,96,768]{3,2,1,0:T(8,128)(2,1)S(1)} %add_convert_fusion.26), channel_id=1, source_target_pairs={{0,16},{16,0},{1,17},{17,1},{2,18},{18,2},{3,19},{19,3},{4,20},{20... | collective-permute-start | bytes 884744 | tf_op jit(solution)/shard_map/ppermute | solution.py:433
  236.4 15.0 %collective-permute-start.36 = (bf16[1,2,96,768]{3,2,1,0:T(8,128)(2,1)}, bf16[1,2,96,768]{3,2,1,0:T(8,128)(2,1)S(1)}, u32[]{:S(2)}, u32[]{:S(2)}) collective-permute-start(bf16[1,2,96,768]{3,2,1,0:T(8,128)(2,1)} %add_convert_fusion.25), channel_id=1, source_target_pairs={{0,8},{4,12},{8,0},{12,4},{1,9},{5,13},{9,1},{13,5},{2,10},{6,14},... | collective-permute-start | bytes 884744 | tf_op jit(solution)/shard_map/ppermute | solution.py:433
  239.0 45.2 %collective-permute-start.43 = (bf16[96,2304]{1,0:T(8,128)(2,1)S(1)}, bf16[96,2304]{1,0:T(8,128)(2,1)S(1)}, u32[]{:S(2)}, u32[]{:S(2)}) collective-permute-start(bf16[96,2304]{1,0:T(8,128)(2,1)S(1)} %pad_maximum_fusion.7), channel_id=1, source_target_pairs={{0,1},{1,2},{2,3},{3,0},{4,5},{5,6},{6,7},{7,4},{8,9},{9,10},{10,1... | collective-permute-start | bytes 1327112 | tf_op jit(solution)/shard_map/ppermute | solution.py:438
  239.1 45.1 %collective-permute-start.42 = (bf16[96,2304]{1,0:T(8,128)(2,1)S(1)}, bf16[96,2304]{1,0:T(8,128)(2,1)}, u32[]{:S(2)}, u32[]{:S(2)}) collective-permute-start(bf16[96,2304]{1,0:T(8,128)(2,1)S(1)} %pad_maximum_fusion.6), channel_id=1, source_target_pairs={{0,2},{1,3},{2,0},{3,1},{4,6},{5,7},{6,4},{7,5},{8,10},{9,11},{10,... | collective-permute-start | bytes 1327112 | tf_op jit(solution)/shard_map/ppermute | solution.py:438
  253.0 1.6 collective-permute-start.37
  254.6 4.0 %collective-permute-start.38 = (f32[72,128]{1,0:T(8,128)S(1)}, f32[72,128]{1,0:T(8,128)S(1)}, u32[]{:S(2)}, u32[]{:S(2)}) collective-permute-start(f32[72,128]{1,0:T(8,128)S(1)} %fusion.25), channel_id=1, source_target_pairs={{0,8},{4,12},{8,0},{12,4},{1,9},{5,13},{9,1},{13,5},{2,10},{6,14},... | collective-permute-start | bytes 110600 | tf_op jit(solution)/shard_map/ppermute | solution.py:433
  255.6 28.6 %collective-permute-start.44 = (bf16[96,2304]{1,0:T(8,128)(2,1)S(1)}, bf16[96,2304]{1,0:T(8,128)(2,1)S(1)}, u32[]{:S(2)}, u32[]{:S(2)}) collective-permute-start(bf16[96,2304]{1,0:T(8,128)(2,1)S(1)} %pad_maximum_fusion.8), channel_id=1, source_target_pairs={{0,3},{1,0},{2,1},{3,2},{4,7},{5,4},{6,5},{7,6},{8,11},{9,8},{10,9... | collective-permute-start | bytes 1327112 | tf_op jit(solution)/shard_map/ppermute | solution.py:438
  258.6 4.0 %collective-permute-start.39 = (f32[72,128]{1,0:T(8,128)S(1)}, f32[72,128]{1,0:T(8,128)S(1)}, u32[]{:S(2)}, u32[]{:S(2)}) collective-permute-start(f32[72,128]{1,0:T(8,128)S(1)} %fusion.27), channel_id=1, source_target_pairs={{0,16},{16,0},{1,17},{17,1},{2,18},{18,2},{3,19},{19,3},{4,20},{20... | collective-permute-start | bytes 110600 | tf_op jit(solution)/shard_map/ppermute | solution.py:433
  262.7 16.1 %collective-permute-start.40 = (f32[72,128]{1,0:T(8,128)S(1)}, f32[72,128]{1,0:T(8,128)S(1)}, u32[]{:S(2)}, u32[]{:S(2)}) collective-permute-start(f32[72,128]{1,0:T(8,128)S(1)} %add.202), channel_id=1, source_target_pairs={{0,1},{1,0},{2,3},{3,2},{4,5},{5,4},{6,7},{7,6},{8,9},{9,8},{10,11... | collective-permute-start | bytes 110600 | tf_op jit(solution)/shard_map/ppermute | solution.py:433
  278.8 4.9 %collective-permute-start.41 = (f32[72,128]{1,0:T(8,128)S(1)}, f32[72,128]{1,0:T(8,128)S(1)}, u32[]{:S(2)}, u32[]{:S(2)}) collective-permute-start(f32[72,128]{1,0:T(8,128)S(1)} %add.203), channel_id=1, source_target_pairs={{0,2},{1,3},{2,0},{3,1},{4,6},{5,7},{6,4},{7,5},{8,10},{9,11},{10,... | collective-permute-start | bytes 110600 | tf_op jit(solution)/shard_map/ppermute | solution.py:433
  285.5 11.3 %collective-permute-start.45 = (bf16[96,2304]{1,0:T(8,128)(2,1)S(1)}, bf16[96,2304]{1,0:T(8,128)(2,1)S(1)}, u32[]{:S(2)}, u32[]{:S(2)}) collective-permute-start(bf16[96,2304]{1,0:T(8,128)(2,1)S(1)} %add_convert_fusion.12), channel_id=1, source_target_pairs={{0,16},{16,0},{1,17},{17,1},{2,18},{18,2},{3,19},{19,3},{4,20},{20... | collective-permute-start | bytes 1327112 | tf_op jit(solution)/shard_map/ppermute | solution.py:433
  (41 other events, 227.5 us)
